TPU v7x, 32 devices: a whole 2x2x4 slice. The times are simulated.
32 devices in a mesh: runs: 2 (over y), lon: 4 (over z), tag: 2 (over x), lev: 2 (over core).
Axes of the slice: x: 2, y: 2, z: 4, core: 2. Of those that a mesh axis runs over, the one named last changes fastest.
Arguments:
- tracer: float32 [128, 2, 1152, 768], P(('runs', 'tag'), 'lev', 'lon'), parts along dimension 0, may hold values from -6 to 6
- courant: float32 [2, 4, 1152, 768], P(None, ('runs', 'lev'), ('lon', 'tag')), parts along dimension 1, may hold values from -1 to 1
- thickness: float32 [4, 1152, 768], P(('runs', 'lev'), ('lon', 'tag')), parts along dimension 0, may hold values from 0.5 to 2
- emission: bfloat16 [8, 1152, 768], P(None, 'lon'), may hold values from -6 to 6
- region_map: int32 [128], P(('runs', 'tag')), parts along dimension 0, may hold values from 0 to 7
- filter_mask: int32 [768], replicated, may hold values from 0 to 1, as said below
- cutoff: int32 [768], replicated, may hold values from 16 to 576
Outputs:
- new_tracer: float32 [128, 2, 1152, 768], P(('runs', 'tag'), 'lev', 'lon'), parts along dimension 0
There are 2 independent parts, one for each index of `runs`. A program takes and returns all parts, laid end to end along the dimension named above; an argument that names none is the same for every part. Nothing has to cross between parts.
Inputs may be any that keep to these rules, and one draw needn't show every extreme that they name: `filter_mask`: exactly 128 latitudes carry a 1.
All inputs are finite; a program needn't handle non-finite values.
Results may differ from a plain program's by a relative error of at most 0.0003.
Values sent between devices are 32-bit elements; how exact they have to be, the bound alone decides.
No kernel may reach another device: no remote copies, remote signals or barrier semaphores. Data moves between devices by JAX's collectives and lax.ppermute only.
A program may use at most 448 MiB of HBM per device.

v0:
```python
import functools

import jax
import jax.numpy as jnp
import ml_dtypes
import numpy as np
from jax import lax
from jax.experimental import pallas as pl
from jax.experimental.pallas import tpu as pltpu
from jax.sharding import PartitionSpec as P

FROWS = 128
GROUP = 8
WAVES = 32
LANES = 128
CHUNK = 4
CAPS = (0.6, 0.66, 1.0)
VMEM = 24 * 1024 * 1024


def wave_table(length):
    waves = np.arange(length // 4).reshape(-1, WAVES)
    phase = (np.arange(length)[:, None, None] * waves[None]) % length
    angle = phase * (2.0 * np.pi / length)
    table = np.concatenate([np.cos(angle), np.sin(angle)], axis=-1).reshape(length, -1)
    high = table.astype(ml_dtypes.bfloat16)
    low = (table - high.astype(np.float64)).astype(ml_dtypes.bfloat16)
    return high, low


def halves(value):
    high = value.astype(jnp.bfloat16)
    low = (value - high.astype(jnp.float32)).astype(jnp.bfloat16)
    return high, low


def mxu(left, right, contract=((1,), (0,))):
    return lax.dot_general(left, right, (contract, ((), ())), preferred_element_type=jnp.float32)


def divergence(face, next_face):
    half, next_half = 0.5 * jnp.abs(face), 0.5 * jnp.abs(next_face)
    return (
        face / 12.0,
        -next_face / 12.0 - 7.0 / 12.0 * face - half,
        7.0 / 12.0 * (next_face - face) + half + next_half,
        7.0 / 12.0 * next_face - next_half + face / 12.0,
        -next_face / 12.0,
    )


def stencil_weights(zonal, zonal_next, merid, merid_next, factor):
    east = divergence(zonal, zonal_next)
    north = divergence(merid, merid_next)
    parts = [east[0], east[1], east[3], east[4], north[0], north[1], north[3], north[4], east[2] + north[2]]
    return jnp.stack([part * factor for part in parts])


def forward_kernel(
    cap, offset_ref, region_ref, q_ref, edge_ref, weight_ref, source_ref, stays_ref, pick_ref, sign_ref,
    high_ref, low_ref, moved_ref, out_ref, wide, tendency, spectrum, *, first
):
    length, lats = q_ref.shape[1:]
    columns = high_ref.shape[1]
    step = 16
    padded = -(-length // step) * step
    for s in range(2):
        wide[s, 6:8] = edge_ref[s, 0:2]
        wide[s, 8:24] = q_ref[s, 0:16]
        wide[s, 40:56] = q_ref[s, length - 16 : length]
        wide[s, 56:58] = edge_ref[s, 2:4]
    stays = stays_ref[...]
    regions = [region_ref[first + 2 * pl.program_id(0) + s] for s in range(2)]
    for start in range(0, length, step):
        rows = min(step, length - start)
        here = slice(start, start + rows)
        for s in range(2):
            q = q_ref[s, here]
            total = source_ref[regions[s], here].astype(jnp.float32) + weight_ref[8, here] * q
            for index, shift in enumerate((-2, -1, 1, 2)):
                if start + shift < 0:
                    moved = wide[s, 8 + shift : 8 + shift + rows]
                elif start + rows + shift > length:
                    moved = wide[s, 56 - rows + shift : 56 + shift]
                else:
                    moved = q_ref[s, start + shift : start + shift + rows]
                total += weight_ref[index, here] * moved
                total += weight_ref[4 + index, here] * pltpu.roll(q, (-shift) % lats, 1)
            moved_ref[s, here] = q + stays * total
            high, low = halves(total)
            tendency[2 * s * padded + start : 2 * s * padded + start + rows] = high
            tendency[(2 * s + 1) * padded + start : (2 * s + 1) * padded + start + rows] = low
    selected = mxu(tendency[...], pick_ref[...])
    turned = []
    for s in range(2):
        at = 2 * s * padded
        x = (selected[at : at + length] + selected[at + padded : at + padded + length]) * sign_ref[...]
        turned.append(x.T)
    x_high, x_low = halves(jnp.concatenate(turned, axis=0))
    with_high = mxu(jnp.concatenate([x_high, x_low], axis=0), high_ref[...])
    spectrum[:, :columns] = with_high[: 2 * FROWS] + with_high[2 * FROWS :] + mxu(x_high, low_ref[...])
    left = lax.broadcasted_iota(jnp.int32, (GROUP, LANES), 1) < 2 * WAVES
    for block in range(columns // (2 * WAVES)):
        lanes = slice(LANES * (block // 2), LANES * (block // 2) + LANES)
        for group in range(FROWS // GROUP):
            a = spectrum[GROUP * group : GROUP * (group + 1), lanes]
            b = spectrum[FROWS + GROUP * group : FROWS + GROUP * (group + 1), lanes]
            if block % 2 == 0:
                tile = jnp.where(left, a, pltpu.roll(b, 2 * WAVES, 1))
            else:
                tile = jnp.where(left, pltpu.roll(a, 2 * WAVES, 1), b)
            out_ref[jnp.minimum(offset_ref[block] + group, cap - 1), 0] = tile


def inverse_kernel(
    cap, offset_ref, end_ref, moved_ref, arrived_ref, held_ref, keep_ref, high_ref, both_ref, flip_ref, put_ref, *rest
):
    out_ref, spectrum = rest[-2:]
    columns = high_ref.shape[1]
    left = lax.broadcasted_iota(jnp.int32, (GROUP, LANES), 1) < 2 * WAVES
    end = lax.broadcasted_iota(jnp.int32, (GROUP, LANES), 0) < GROUP * end_ref[0]
    blocks = columns // (2 * WAVES)

    def load(block, group):
        at = jnp.minimum(offset_ref[block] + group, cap - 1)
        return jnp.where(end, arrived_ref[at, 0], held_ref[at, 0])

    for group in range(FROWS // GROUP):
        for pair in range((blocks + 1) // 2):
            even = load(2 * pair, group)
            odd = load(2 * pair + 1, group) if 2 * pair + 1 < blocks else even
            where = slice(GROUP * group, GROUP * (group + 1)), slice(LANES * pair, LANES * (pair + 1))
            keep = keep_ref[where]
            a = jnp.where(left, even, pltpu.roll(odd, 2 * WAVES, 1))
            b = jnp.where(left, pltpu.roll(even, 2 * WAVES, 1), odd)
            spectrum[(0,) + where] = jnp.where(keep != 0.0, a * keep, 0.0)
            spectrum[(1,) + where] = jnp.where(keep != 0.0, b * keep, 0.0)
    length = high_ref.shape[0]
    s_high, s_low = halves(spectrum[...].reshape(2 * FROWS, -1)[:, :columns])
    last = ((1,), (1,))
    with_high = mxu(both_ref[...], s_high, last)
    back = with_high[:length] + with_high[length:] + mxu(high_ref[...], s_low, last)
    for s in range(2):
        pieces = jnp.concatenate(halves(back[:, s * FROWS : (s + 1) * FROWS] * flip_ref[...]), axis=1)
        out_ref[s] = moved_ref[s] + mxu(pieces, put_ref[...])


RESIDENT = pl.BlockSpec(memory_space=pltpu.VMEM)


def forward(base, size, cap, offsets, regions, tracer, edges, weights, source, stays, pick, sign, high, low):
    tags, length, lats = tracer.shape
    pairs = size // 2
    constants = [weights, source, stays, pick, sign, high, low]
    grid_spec = pltpu.PrefetchScalarGridSpec(
        num_scalar_prefetch=2,
        grid=(pairs,),
        in_specs=[
            pl.BlockSpec((2, length, lats), lambda p, *_: (base // 2 + p, 0, 0)),
            pl.BlockSpec((2, 4, lats), lambda p, *_: (base // 2 + p, 0, 0)),
        ]
        + [RESIDENT] * len(constants),
        out_specs=[
            pl.BlockSpec((2, length, lats), lambda p, *_: (p, 0, 0)),
            pl.BlockSpec((cap, 1, GROUP, LANES), lambda p, *_: (0, p, 0, 0)),
        ],
        scratch_shapes=[
            pltpu.VMEM((2, 64, lats), jnp.float32),
            pltpu.VMEM((4 * (-(-length // 16) * 16), lats), jnp.bfloat16),
            pltpu.VMEM((2 * FROWS, -(-high.shape[1] // LANES) * LANES), jnp.float32),
        ],
    )
    flops = size * 2 * length * (2 * lats * FROWS + 3 * high.shape[1] * FROWS)
    return pl.pallas_call(
        functools.partial(forward_kernel, cap, first=base),
        grid_spec=grid_spec,
        out_shape=[
            jax.ShapeDtypeStruct((size, length, lats), jnp.float32),
            jax.ShapeDtypeStruct((cap, pairs, GROUP, LANES), jnp.float32),
        ],
        compiler_params=pltpu.CompilerParams(vmem_limit_bytes=VMEM),
        cost_estimate=pl.CostEstimate(flops=flops, bytes_accessed=5 * size * length * lats * 4, transcendentals=0),
        name="step_and_transform",
    )(offsets, regions, tracer, edges, *constants)


def inverse(base, size, cap, offsets, end, tracer, moved, arrived, held, keep, high, both, flip, put, out):
    tags, length, lats = tracer.shape
    pairs = size // 2
    constants = [keep, high, both, flip, put]
    specs = [
        pl.BlockSpec((2, length, lats), lambda p, *_: (p, 0, 0)),
        pl.BlockSpec((cap, 1, GROUP, LANES), lambda p, *_: (0, p, 0, 0)),
        pl.BlockSpec((cap, 1, GROUP, LANES), lambda p, *_: (0, p, 0, 0)),
    ] + [RESIDENT] * len(constants)
    operands = [offsets, end, moved, arrived, held] + constants
    aliases = {}
    if out is not None:
        specs.append(pl.BlockSpec(memory_space=pl.ANY))
        operands.append(out)
        aliases = {len(operands) - 1: 0}
    grid_spec = pltpu.PrefetchScalarGridSpec(
        num_scalar_prefetch=2,
        grid=(pairs,),
        in_specs=specs,
        out_specs=pl.BlockSpec((2, length, lats), lambda p, *_: (base // 2 + p, 0, 0)),
        scratch_shapes=[pltpu.VMEM((2, FROWS, keep.shape[1]), jnp.float32)],
    )
    flops = size * 2 * length * (2 * lats * FROWS + 3 * high.shape[1] * FROWS)
    return pl.pallas_call(
        functools.partial(inverse_kernel, cap),
        grid_spec=grid_spec,
        out_shape=jax.ShapeDtypeStruct(tracer.shape, jnp.float32),
        input_output_aliases=aliases,
        compiler_params=pltpu.CompilerParams(vmem_limit_bytes=VMEM),
        cost_estimate=pl.CostEstimate(flops=flops, bytes_accessed=2 * size * length * lats * 4, transcendentals=0),
        name="restore",
    )(*operands)


def sum_over_lon(packed, count, place):
    middle = count // 2
    total = packed
    for hop in range(middle - 1):
        inward = [(hop, hop + 1), (count - 1 - hop, count - 2 - hop)]
        total = total + lax.ppermute(total, "lon", inward)
    total = total + lax.ppermute(total, "lon", [(middle - 1, middle), (middle, middle - 1)])
    for hop in range(middle - 2, -1, -1):
        outward = [(hop + 1, hop), (count - 2 - hop, count - 1 - hop)]
        arrived = lax.ppermute(total, "lon", outward)
        total = jnp.where((place == hop) | (place == count - 1 - hop), arrived, total)
    return total


def plain_pipeline(chunks, forward_at, inverse_at, place, count, offsets):
    out = None
    for chunk in range(chunks):
        moved, packed = forward_at(chunk, offsets)
        total = sum_over_lon(packed, count, place)
        out = inverse_at(chunk, moved, total, total, out, offsets)
    return out


def stepped_pipeline(chunks, forward_at, inverse_at, place, count, offsets):
    swap = [(0, 1), (1, 0), (2, 3), (3, 2)]
    cross = [(1, 2), (2, 1)]
    end = (place == 0) | (place == count - 1)
    moved, own = {}, {}
    moved[0], own[0] = forward_at(0, offsets)
    pair_sum = swapped = crossed = sent = out = None
    for t in range(chunks + 3):
        arrived, held = swapped, sent
        total = None if crossed is None else pair_sum + crossed
        here = own.get(t)
        if here is None:
            sent = total
        else:
            sent = here if total is None else jnp.where(end, here, total)
        pair_sum = own[t - 1] + swapped if 1 <= t <= chunks else None
        if t < chunks + 2:
            sending = [x for x in (sent, pair_sum) if x is not None]
            extra = [out] if out is not None else []
            result = lax.optimization_barrier((offsets, *sending, *extra))
            token, result = result[0], list(result[1:])
            if sent is not None:
                sent = result.pop(0)
            if pair_sum is not None:
                pair_sum = result.pop(0)
            if extra:
                out = result.pop(0)
            swapped = None if sent is None else lax.ppermute(sent, "lon", swap)
            crossed = None if pair_sum is None else lax.ppermute(pair_sum, "lon", cross)
        else:
            token = offsets
        if t + 1 < chunks:
            moved[t + 1], own[t + 1] = forward_at(t + 1, token)
        if t >= 3:
            out = inverse_at(t - 3, moved[t - 3], arrived, held, out, token)
    return out


def ring_edges(first, last, count):
    forward_ring = [(i, (i + 1) % count) for i in range(count)]
    backward_ring = [((i + 1) % count, i) for i in range(count)]
    before = lax.ppermute(last, "lon", forward_ring)
    after = lax.ppermute(first, "lon", backward_ring)
    return before, after


def body(tracer, courant, thickness, emission, region_map, filter_mask, cutoff):
    tracer = tracer[:, 0]
    courant, thickness = courant[:, 0], thickness[0]
    tags, length, lats = tracer.shape
    count = lax.axis_size("lon")
    place = lax.axis_index("lon")
    full = length * count
    nyquist = full // 2
    groups = FROWS // GROUP
    backward_ring = [((i + 1) % count, i) for i in range(count)]

    flipped = cutoff > nyquist - 1 - cutoff
    reach = jnp.minimum(cutoff, nyquist - 1 - cutoff)
    masked = filter_mask == 1
    score = jnp.where(masked, reach + 2, 0)
    lat = jnp.arange(lats, dtype=jnp.int32)
    ahead = (score[None, :] > score[:, None]) | ((score[None, :] == score[:, None]) & (lat[None, :] < lat[:, None]))
    rank = jnp.sum(ahead.astype(jnp.int32), axis=1)
    chosen = rank[:, None] == jnp.arange(FROWS, dtype=jnp.int32)[None, :]
    row_reach = jnp.sum(jnp.where(chosen, reach[:, None], 0), axis=0)
    row_flipped = jnp.any(chosen & flipped[:, None], axis=0)
    one_hot = chosen.astype(jnp.bfloat16)
    put = one_hot.T

    blocks = nyquist // 2 // WAVES
    starts = jnp.arange(blocks, dtype=jnp.int32) * WAVES
    needed = jnp.sum((row_reach[None, :] >= starts[:, None]).astype(jnp.int32), axis=1)
    taken = (needed + GROUP - 1) // GROUP
    offsets = jnp.sum(
        jnp.where(jnp.arange(blocks)[None, :] < jnp.arange(blocks)[:, None], taken[None, :], 0), axis=1
    ).astype(jnp.int32)
    used = jnp.sum(taken)

    lane = jnp.arange(-(-blocks * 2 * WAVES // LANES) * LANES, dtype=jnp.int32)
    wave = lane // (2 * WAVES) * WAVES + lane % WAVES
    scaling = jnp.where(wave == 0, 1.0 / full, 2.0 / full).astype(jnp.float32)
    keep = jnp.where(wave[None, :] <= row_reach[:, None], scaling[None, :], 0.0)
    high, low = (
        lax.dynamic_slice_in_dim(jnp.asarray(table), place * length, length, 0) for table in wave_table(full)
    )
    odd = (place * length + jnp.arange(length, dtype=jnp.int32)) % 2 == 1
    sign = jnp.where(odd[:, None] & row_flipped[None, :], -1.0, 1.0).astype(jnp.float32)
    flip = jnp.where(row_flipped[None, :], -sign, sign)
    stays = jnp.where(masked & ~flipped, 0.0, 1.0).astype(jnp.float32)[None, :]

    largest = blocks * groups
    both = jnp.concatenate([high, low])
    put = jnp.concatenate([put, put])
    is_end = ((place == 0) | (place == count - 1)).astype(jnp.int32).reshape(1)
    sizes = [CHUNK // 2] + [CHUNK] * ((tags - CHUNK) // CHUNK) + [CHUNK // 2]
    bases = [sum(sizes[:i]) for i in range(len(sizes))]

    gathered = lax.all_gather(courant, "tag", axis=1, tiled=True)
    thick = lax.all_gather(thickness, "tag", axis=0, tiled=True)
    zonal_end = lax.all_gather(lax.ppermute(courant[0, :1], "lon", backward_ring), "tag")[0]
    edges = jnp.concatenate(ring_edges(tracer[:, :2], tracer[:, length - 2 :], count), axis=1)

    def run(cap):
        zonal, merid = gathered[0], gathered[1] * (lat > 0).astype(jnp.float32)
        zonal_after = jnp.concatenate([zonal[1:], zonal_end])
        merid_after = jnp.pad(merid[:, 1:], ((0, 0), (0, 1)))
        weights = stencil_weights(zonal, zonal_after, merid, merid_after, -1.0 / thick)
        ones = jnp.ones_like(lat, dtype=bool)
        inside = jnp.stack([ones] * 4 + [lat >= 2, lat >= 1, lat <= lats - 2, lat <= lats - 3] + [ones])
        weights = weights * inside.astype(jnp.float32)[:, None, :]

        def forward_at(chunk, offsets):
            return forward(
                bases[chunk], sizes[chunk], cap, offsets, region_map, tracer, edges, weights, emission, stays, one_hot,
                sign, high, low,
            )

        def inverse_at(chunk, moved, arrived, held, out, offsets):
            return inverse(
                bases[chunk], sizes[chunk], cap, offsets, is_end, tracer, moved, arrived, held, keep, high, both, flip,
                put, out,
            )

        pipeline = stepped_pipeline if count == 4 else plain_pipeline
        return pipeline(len(sizes), forward_at, inverse_at, place, count, offsets)

    caps = [int(share * largest) + 1 for share in CAPS]
    if len(caps) == 1:
        out = run(caps[0])
    else:
        index = sum((used >= cap).astype(jnp.int32) for cap in caps[:-1])
        out = lax.switch(index, [functools.partial(run, cap) for cap in caps])
    return out[:, None]


def solution(mesh):
    in_specs = (
        P(("runs", "tag"), "lev", "lon", None),
        P(None, ("runs", "lev"), ("lon", "tag"), None),
        P(("runs", "lev"), ("lon", "tag"), None),
        P(None, "lon", None),
        P(("runs", "tag")),
        P(),
        P(),
    )
    out_specs = P(("runs", "tag"), "lev", "lon", None)
    return jax.shard_map(body, mesh=mesh, in_specs=in_specs, out_specs=out_specs, check_vma=False)
```

profile of v0, /device:TPU:0, one launch (start us, length us, event | category | flops | bytes accessed | tf_op | source)
XLA Modules:
  0.0 281.6 jit_solution(6792031049892996433)
XLA Ops:
  8.0 5.0 %collective-permute-start.60 = (f32[1,768]{1,0:T(1,128)S(1)}, f32[1,768]{1,0:T(1,128)S(1)}, u32[]{:S(2)}, u32[]{:S(2)}) collective-permute-start(f32[1,768]{1,0:T(1,128)S(1)} %slice_bitcast_fusion.12), channel_id=1, source_target_pairs={{4,0},{8,4},{12,8},{0,12},{5,1},{9,5},{13,9},{1,13},{6,2},{10,6},{... | collective-permute-start | bytes 9224 | tf_op jit(solution)/shard_map/ppermute | solution.py:344
  13.1 1.5 fusion.32
  14.7 3.8 %collective-permute-start.62 = (f32[32,2,768]{2,1,0:T(2,128)S(1)}, f32[32,2,768]{2,1,0:T(2,128)}, u32[]{:S(2)}, u32[]{:S(2)}) collective-permute-start(f32[32,2,768]{2,1,0:T(2,128)S(1)} %get-tuple-element.1008), channel_id=1, source_target_pairs={{4,0},{8,4},{12,8},{0,12},{5,1},{9,5},{13,9},{1,13},{6,2},{10,6},{... | collective-permute-start | bytes 589832 | tf_op jit(solution)/shard_map/ppermute | solution.py:286
  20.2 1.2 constant_dynamic-slice_fusion
  21.4 22.5 %all-gather.1 = f32[1,288,768]{2,1,0:T(8,128)S(1)} all-gather(f32[1,144,768]{2,1,0:T(8,128)S(1)} %copy-done.46), channel_id=3, replica_groups=mesh['runs'=2,'lon'=4,'tag'=2,'lev'=2] {'tag'}, dimensions={1}, use_global_device_ids=true | all-gather | bytes 1327104 | tf_op jit(solution)/shard_map/all_gather | solution.py:343
  47.9 4.3 %all-gather.3 = f32[2,1,768]{2,1,0:T(1,128)S(1)} all-gather(f32[1,1,768]{2,1,0:T(1,128)S(1)} %bitcast.276), channel_id=4, replica_groups=mesh['runs'=2,'lon'=4,'tag'=2,'lev'=2] {'tag'}, dimensions={0}, use_global_device_ids=true | all-gather | bytes 9216 | tf_op jit(solution)/shard_map/all_gather | solution.py:344
  52.2 1.1 pad_maximum_fusion.4
  53.4 221.1 %conditional.1 = (f32[32,1,288,768]{3,2,1,0:T(8,128)}) conditional(s32[]{:T(128)} %clamp.3, (s32[9,9]{1,0:T(8,128)S(1)}, s32[9,9]{1,0:T(8,128)S(1)}, s32[9]{0:T(128)S(1)}, (), s32[]{:T(128)}, /*index=5*/s32[]{:T(128)}, s32[]{:T(128)}, s32[]{:T(128)}, f32[2,1,288,768]{3,2,0,1:T(8,128)}, f32[1,288,768]{2,1,0:T(8,128)S(1)}, ...), branch_computations={%region_4.7_spmd, %region_7.10_spmd, %region_10.13_spmd} | conditional | flops 15427075072 | bytes 634621440 | solution.py:376
  53.9 1.4 slice_bitcast_fusion.5
  55.2 1.3 bitcast_dynamic-update-slice_fusion.17
  60.2 1.9 copy-done.18
  62.1 7.0 %step_and_transform.36 = (f32[2,288,768]{2,1,0:T(8,128)S(1)}, f32[96,1,8,128]{3,2,1,0:T(8,128)S(1)}) custom-call(s32[9]{0:T(128)S(1)} %select_reduce_fusion.1.offset_ref, s32[32]{0:T(128)S(1)} %get-tuple-element.945.region_ref, f32[32,288,768]{2,1,0:T(8,128)} %get-tuple-element.744.q_ref, f32[32,4,768]{2,1,0:T(4,128)S(1)} %get-tuple-element.745.edge_ref, ...), custom_call_target="tpu_custom_call" | custom-call | flops 481296384 | bytes 8847360 | tf_op jit(solution)/shard_map/cond/branch_1_fun/step_and_transform/pallas_call | solution.py:174
  69.2 11.1 %step_and_transform.37 = (f32[4,288,768]{2,1,0:T(8,128)S(1)}, f32[96,2,8,128]{3,2,1,0:T(8,128)S(1)}) custom-call(s32[9]{0:T(128)S(1)} %select_reduce_fusion.1.offset_ref, s32[32]{0:T(128)S(1)} %get-tuple-element.945.region_ref, f32[32,288,768]{2,1,0:T(8,128)} %get-tuple-element.744.q_ref, f32[32,4,768]{2,1,0:T(4,128)} %copy-done.35, ...), custom_call_target="tpu_custom_call" | custom-call | flops 962592768 | bytes 17694720 | tf_op jit(solution)/shard_map/cond/branch_1_fun/step_and_transform/pallas_call | solution.py:174
  80.3 1.9 copy-done.8
  83.0 1.4 collective-permute-start.21
  84.4 3.0 %collective-permute-start.22 = (f32[96,2,8,128]{3,2,1,0:T(8,128)S(1)}, f32[96,2,8,128]{3,2,1,0:T(8,128)}, u32[]{:S(2)}, u32[]{:S(2)}) collective-permute-start(f32[96,2,8,128]{3,2,1,0:T(8,128)S(1)} %get-tuple-element.773), channel_id=1, source_target_pairs={{0,4},{4,0},{8,12},{12,8},{1,5},{5,1},{9,13},{13,9},{2,6},{6,2},{1... | collective-permute-start | bytes 2359304 | tf_op jit(solution)/shard_map/cond/branch_1_fun/ppermute | solution.py:271
  87.4 3.3 %copy-done.3 = f32[9,288,768]{2,1,0:T(8,128)S(1)} copy-done((f32[9,288,768]{2,1,0:T(8,128)S(1)}, f32[9,288,768]{2,1,0:T(8,128)}, u32[]{:S(2)}) %copy-start.3) | copy-done | bytes 7962648 | tf_op jit(solution)/shard_map/cond
  90.6 11.1 %step_and_transform.38 = (f32[4,288,768]{2,1,0:T(8,128)S(1)}, f32[96,2,8,128]{3,2,1,0:T(8,128)S(1)}) custom-call(s32[9]{0:T(128)S(1)} %select_reduce_fusion.1.offset_ref, s32[32]{0:T(128)S(1)} %get-tuple-element.945.region_ref, f32[32,288,768]{2,1,0:T(8,128)} %get-tuple-element.744.q_ref, f32[32,4,768]{2,1,0:T(4,128)} %copy-done.35, ...), custom_call_target="tpu_custom_call" | custom-call | flops 962592768 | bytes 17694720 | tf_op jit(solution)/shard_map/cond/branch_1_fun/step_and_transform/pallas_call | solution.py:174
  101.8 1.3 add_bitcast_fusion.1
  103.2 1.3 add.299
  104.5 1.5 collective-permute-start.24
  106.8 10.0 %step_and_transform.39 = (f32[4,288,768]{2,1,0:T(8,128)S(1)}, f32[96,2,8,128]{3,2,1,0:T(8,128)S(1)}) custom-call(s32[9]{0:T(128)S(1)} %select_reduce_fusion.1.offset_ref, s32[32]{0:T(128)S(1)} %get-tuple-element.945.region_ref, f32[32,288,768]{2,1,0:T(8,128)} %get-tuple-element.744.q_ref, f32[32,4,768]{2,1,0:T(4,128)S(1)} %copy-done.36, ...), custom_call_target="tpu_custom_call" | custom-call | flops 962592768 | bytes 17694720 | tf_op jit(solution)/shard_map/cond/branch_1_fun/step_and_transform/pallas_call | solution.py:174
  116.8 4.7 %collective-permute-done.24.arrived_ref = f32[96,2,8,128]{3,2,1,0:T(8,128)S(1)} collective-permute-done((f32[96,2,8,128]{3,2,1,0:T(8,128)S(1)}, f32[96,2,8,128]{3,2,1,0:T(8,128)S(1)}, u32[]{:S(2)}, u32[]{:S(2)}) %collective-permute-start.24) | collective-permute-done | bytes 786464 | tf_op jit(solution)/shard_map/cond/branch_1_fun/ppermute | solution.py:271
  121.8 3.6 %collective-permute-start.26 = (f32[96,2,8,128]{3,2,1,0:T(8,128)S(1)}, f32[96,2,8,128]{3,2,1,0:T(8,128)S(1)}, u32[]{:S(2)}, u32[]{:S(2)}) collective-permute-start(f32[96,2,8,128]{3,2,1,0:T(8,128)S(1)} %add_select_fusion.12.held_ref), channel_id=1, source_target_pairs={{0,4},{4,0},{8,12},{12,8},{1,5},{5,1},{9,13},{13,9},{2,6},{6,2},{1... | collective-permute-start | bytes 2359304 | tf_op jit(solution)/shard_map/cond/branch_1_fun/ppermute | solution.py:271
  126.7 3.2 %restore.36.rest_0_ = f32[32,288,768]{2,1,0:T(8,128)} custom-call(s32[9]{0:T(128)S(1)} %select_reduce_fusion.1.offset_ref, s32[1]{0:T(128)} %bitcast.25.end_ref, f32[2,288,768]{2,1,0:T(8,128)S(1)} %get-tuple-element.782.moved_ref, f32[96,2,8,128]{3,2,1,0:T(8,128)S(1)} %collective-permute-done.24.arrived_ref, ...), custom_call_target="tpu_custom_call" | custom-call | flops 481296384 | bytes 3538944 | tf_op jit(solution)/shard_map/cond/branch_1_fun/restore/pallas_call | solution.py:210
  129.9 10.0 %step_and_transform.40 = (f32[4,288,768]{2,1,0:T(8,128)S(1)}, f32[96,2,8,128]{3,2,1,0:T(8,128)S(1)}) custom-call(s32[9]{0:T(128)S(1)} %select_reduce_fusion.1.offset_ref, s32[32]{0:T(128)S(1)} %get-tuple-element.945.region_ref, f32[32,288,768]{2,1,0:T(8,128)} %get-tuple-element.744.q_ref, f32[32,4,768]{2,1,0:T(4,128)S(1)} %copy-done.36, ...), custom_call_target="tpu_custom_call" | custom-call | flops 962592768 | bytes 17694720 | tf_op jit(solution)/shard_map/cond/branch_1_fun/step_and_transform/pallas_call | solution.py:174
  140.2 3.4 %collective-permute-start.28 = (f32[96,2,8,128]{3,2,1,0:T(8,128)S(1)}, f32[96,2,8,128]{3,2,1,0:T(8,128)S(1)}, u32[]{:S(2)}, u32[]{:S(2)}) collective-permute-start(f32[96,2,8,128]{3,2,1,0:T(8,128)S(1)} %add_select_fusion.11.held_ref), channel_id=1, source_target_pairs={{0,4},{4,0},{8,12},{12,8},{1,5},{5,1},{9,13},{13,9},{2,6},{6,2},{1... | collective-permute-start | bytes 2359304 | tf_op jit(solution)/shard_map/cond/branch_1_fun/ppermute | solution.py:271
  144.3 10.0 %step_and_transform.41 = (f32[4,288,768]{2,1,0:T(8,128)S(1)}, f32[96,2,8,128]{3,2,1,0:T(8,128)S(1)}) custom-call(s32[9]{0:T(128)S(1)} %select_reduce_fusion.1.offset_ref, s32[32]{0:T(128)S(1)} %get-tuple-element.945.region_ref, f32[32,288,768]{2,1,0:T(8,128)} %get-tuple-element.744.q_ref, f32[32,4,768]{2,1,0:T(4,128)S(1)} %copy-done.36, ...), custom_call_target="tpu_custom_call" | custom-call | flops 962592768 | bytes 17694720 | tf_op jit(solution)/shard_map/cond/branch_1_fun/step_and_transform/pallas_call | solution.py:174
  154.3 4.8 %restore.37.rest_0_ = f32[32,288,768]{2,1,0:T(8,128)} custom-call(s32[9]{0:T(128)S(1)} %select_reduce_fusion.1.offset_ref, s32[1]{0:T(128)} %bitcast.25.end_ref, f32[4,288,768]{2,1,0:T(8,128)S(1)} %copy-done.9, f32[96,2,8,128]{3,2,1,0:T(8,128)S(1)} %collective-permute-done.26.arrived_ref, ...), custom_call_target="tpu_custom_call", output_to_operand_aliasing={{}: (10, {})} | custom-call | flops 962592768 | bytes 7077888 | tf_op jit(solution)/shard_map/cond/branch_1_fun/restore/pallas_call | solution.py:210
  159.4 1.8 collective-permute-start.30
  162.1 10.0 %step_and_transform.42 = (f32[4,288,768]{2,1,0:T(8,128)S(1)}, f32[96,2,8,128]{3,2,1,0:T(8,128)S(1)}) custom-call(s32[9]{0:T(128)S(1)} %select_reduce_fusion.1.offset_ref, s32[32]{0:T(128)S(1)} %get-tuple-element.945.region_ref, f32[32,288,768]{2,1,0:T(8,128)} %get-tuple-element.744.q_ref, f32[32,4,768]{2,1,0:T(4,128)S(1)} %copy-done.36, ...), custom_call_target="tpu_custom_call" | custom-call | flops 962592768 | bytes 17694720 | tf_op jit(solution)/shard_map/cond/branch_1_fun/step_and_transform/pallas_call | solution.py:174
  172.1 4.8 %restore.38.rest_0_ = f32[32,288,768]{2,1,0:T(8,128)} custom-call(s32[9]{0:T(128)S(1)} %select_reduce_fusion.1.offset_ref, s32[1]{0:T(128)} %bitcast.25.end_ref, f32[4,288,768]{2,1,0:T(8,128)S(1)} %get-tuple-element.798.moved_ref, f32[96,2,8,128]{3,2,1,0:T(8,128)S(1)} %collective-permute-done.28.arrived_ref, ...), custom_call_target="tpu_custom_call", output_to_operand_aliasing={{}: (10, {})} | custom-call | flops 962592768 | bytes 7077888 | tf_op jit(solution)/shard_map/cond/branch_1_fun/restore/pallas_call | solution.py:210
  177.2 3.0 %collective-permute-start.32 = (f32[96,2,8,128]{3,2,1,0:T(8,128)S(1)}, f32[96,2,8,128]{3,2,1,0:T(8,128)S(1)}, u32[]{:S(2)}, u32[]{:S(2)}) collective-permute-start(f32[96,2,8,128]{3,2,1,0:T(8,128)S(1)} %add_select_fusion.9.held_ref), channel_id=1, source_target_pairs={{0,4},{4,0},{8,12},{12,8},{1,5},{5,1},{9,13},{13,9},{2,6},{6,2},{1... | collective-permute-start | bytes 2359304 | tf_op jit(solution)/shard_map/cond/branch_1_fun/ppermute | solution.py:271
  181.0 10.0 %step_and_transform.43 = (f32[4,288,768]{2,1,0:T(8,128)S(1)}, f32[96,2,8,128]{3,2,1,0:T(8,128)S(1)}) custom-call(s32[9]{0:T(128)S(1)} %select_reduce_fusion.1.offset_ref, s32[32]{0:T(128)S(1)} %get-tuple-element.945.region_ref, f32[32,288,768]{2,1,0:T(8,128)} %get-tuple-element.744.q_ref, f32[32,4,768]{2,1,0:T(4,128)S(1)} %copy-done.36, ...), custom_call_target="tpu_custom_call" | custom-call | flops 962592768 | bytes 17694720 | tf_op jit(solution)/shard_map/cond/branch_1_fun/step_and_transform/pallas_call | solution.py:174
  191.0 4.8 %restore.39.rest_0_ = f32[32,288,768]{2,1,0:T(8,128)} custom-call(s32[9]{0:T(128)S(1)} %select_reduce_fusion.1.offset_ref, s32[1]{0:T(128)} %bitcast.25.end_ref, f32[4,288,768]{2,1,0:T(8,128)S(1)} %get-tuple-element.804.moved_ref, f32[96,2,8,128]{3,2,1,0:T(8,128)S(1)} %collective-permute-done.30.arrived_ref, ...), custom_call_target="tpu_custom_call", output_to_operand_aliasing={{}: (10, {})} | custom-call | flops 962592768 | bytes 7077888 | tf_op jit(solution)/shard_map/cond/branch_1_fun/restore/pallas_call | solution.py:210
  196.1 2.1 collective-permute-start.34
  199.1 5.9 %step_and_transform.44 = (f32[2,288,768]{2,1,0:T(8,128)S(1)}, f32[96,1,8,128]{3,2,1,0:T(8,128)S(1)}) custom-call(s32[9]{0:T(128)S(1)} %select_reduce_fusion.1.offset_ref, s32[32]{0:T(128)S(1)} %get-tuple-element.945.region_ref, f32[32,288,768]{2,1,0:T(8,128)} %get-tuple-element.744.q_ref, f32[32,4,768]{2,1,0:T(4,128)S(1)} %copy-done.36, ...), custom_call_target="tpu_custom_call" | custom-call | flops 481296384 | bytes 8847360 | tf_op jit(solution)/shard_map/cond/branch_1_fun/step_and_transform/pallas_call | solution.py:174
  205.0 4.8 %restore.40.rest_0_ = f32[32,288,768]{2,1,0:T(8,128)} custom-call(s32[9]{0:T(128)S(1)} %select_reduce_fusion.1.offset_ref, s32[1]{0:T(128)} %bitcast.25.end_ref, f32[4,288,768]{2,1,0:T(8,128)S(1)} %get-tuple-element.811.moved_ref, f32[96,2,8,128]{3,2,1,0:T(8,128)S(1)} %collective-permute-done.32.arrived_ref, ...), custom_call_target="tpu_custom_call", output_to_operand_aliasing={{}: (10, {})} | custom-call | flops 962592768 | bytes 7077888 | tf_op jit(solution)/shard_map/cond/branch_1_fun/restore/pallas_call | solution.py:210
  211.5 7.6 %collective-permute-start.36 = (f32[96,2,8,128]{3,2,1,0:T(8,128)S(1)}, f32[96,2,8,128]{3,2,1,0:T(8,128)S(1)}, u32[]{:S(2)}, u32[]{:S(2)}) collective-permute-start(f32[96,2,8,128]{3,2,1,0:T(8,128)S(1)} %add_select_fusion.7.held_ref), channel_id=1, source_target_pairs={{0,4},{4,0},{8,12},{12,8},{1,5},{5,1},{9,13},{13,9},{2,6},{6,2},{1... | collective-permute-start | bytes 2359304 | tf_op jit(solution)/shard_map/cond/branch_1_fun/ppermute | solution.py:271
  219.1 4.8 %restore.41.rest_0_ = f32[32,288,768]{2,1,0:T(8,128)} custom-call(s32[9]{0:T(128)S(1)} %select_reduce_fusion.1.offset_ref, s32[1]{0:T(128)} %bitcast.25.end_ref, f32[4,288,768]{2,1,0:T(8,128)S(1)} %get-tuple-element.816.moved_ref, f32[96,2,8,128]{3,2,1,0:T(8,128)S(1)} %collective-permute-done.34.arrived_ref, ...), custom_call_target="tpu_custom_call", output_to_operand_aliasing={{}: (10, {})} | custom-call | flops 962592768 | bytes 7077888 | tf_op jit(solution)/shard_map/cond/branch_1_fun/restore/pallas_call | solution.py:210
  224.0 6.3 %collective-permute-done.36.arrived_ref = f32[96,2,8,128]{3,2,1,0:T(8,128)S(1)} collective-permute-done((f32[96,2,8,128]{3,2,1,0:T(8,128)S(1)}, f32[96,2,8,128]{3,2,1,0:T(8,128)S(1)}, u32[]{:S(2)}, u32[]{:S(2)}) %collective-permute-start.36) | collective-permute-done | bytes 786464 | tf_op jit(solution)/shard_map/cond/branch_1_fun/ppermute | solution.py:271
  231.1 5.7 %collective-permute-start.39 = (f32[96,2,8,128]{3,2,1,0:T(8,128)S(1)}, f32[96,2,8,128]{3,2,1,0:T(8,128)S(1)}, u32[]{:S(2)}, u32[]{:S(2)}) collective-permute-start(f32[96,2,8,128]{3,2,1,0:T(8,128)S(1)} %add.316.held_ref), channel_id=1, source_target_pairs={{0,4},{4,0},{8,12},{12,8},{1,5},{5,1},{9,13},{13,9},{2,6},{6,2},{1... | collective-permute-start | bytes 2359304 | tf_op jit(solution)/shard_map/cond/branch_1_fun/ppermute | solution.py:271
  236.8 4.8 %restore.42.rest_0_ = f32[32,288,768]{2,1,0:T(8,128)} custom-call(s32[9]{0:T(128)S(1)} %select_reduce_fusion.1.offset_ref, s32[1]{0:T(128)} %bitcast.25.end_ref, f32[4,288,768]{2,1,0:T(8,128)S(1)} %get-tuple-element.820.moved_ref, f32[96,2,8,128]{3,2,1,0:T(8,128)S(1)} %collective-permute-done.36.arrived_ref, ...), custom_call_target="tpu_custom_call", output_to_operand_aliasing={{}: (10, {})} | custom-call | flops 962592768 | bytes 7077888 | tf_op jit(solution)/shard_map/cond/branch_1_fun/restore/pallas_call | solution.py:210
  241.7 6.3 %collective-permute-start.38 = (f32[96,2,8,128]{3,2,1,0:T(8,128)S(1)}, f32[96,2,8,128]{3,2,1,0:T(8,128)S(1)}, u32[]{:S(2)}, u32[]{:S(2)}) collective-permute-start(f32[96,2,8,128]{3,2,1,0:T(8,128)S(1)} %add.318.held_ref), channel_id=1, source_target_pairs={{0,4},{4,0},{8,12},{12,8},{1,5},{5,1},{9,13},{13,9},{2,6},{6,2},{1... | collective-permute-start | bytes 2359304 | tf_op jit(solution)/shard_map/cond/branch_1_fun/ppermute | solution.py:271
  248.0 4.5 %collective-permute-done.39.arrived_ref = f32[96,2,8,128]{3,2,1,0:T(8,128)S(1)} collective-permute-done((f32[96,2,8,128]{3,2,1,0:T(8,128)S(1)}, f32[96,2,8,128]{3,2,1,0:T(8,128)S(1)}, u32[]{:S(2)}, u32[]{:S(2)}) %collective-permute-start.39) | collective-permute-done | bytes 786464 | tf_op jit(solution)/shard_map/cond/branch_1_fun/ppermute | solution.py:271
  252.5 4.8 %restore.43.rest_0_ = f32[32,288,768]{2,1,0:T(8,128)} custom-call(s32[9]{0:T(128)S(1)} %select_reduce_fusion.1.offset_ref, s32[1]{0:T(128)} %bitcast.25.end_ref, f32[4,288,768]{2,1,0:T(8,128)S(1)} %get-tuple-element.824.moved_ref, f32[96,2,8,128]{3,2,1,0:T(8,128)S(1)} %collective-permute-done.39.arrived_ref, ...), custom_call_target="tpu_custom_call", output_to_operand_aliasing={{}: (10, {})} | custom-call | flops 962592768 | bytes 7077888 | tf_op jit(solution)/shard_map/cond/branch_1_fun/restore/pallas_call | solution.py:210
  257.4 6.3 %collective-permute-done.38.arrived_ref = f32[96,2,8,128]{3,2,1,0:T(8,128)S(1)} collective-permute-done((f32[96,2,8,128]{3,2,1,0:T(8,128)S(1)}, f32[96,2,8,128]{3,2,1,0:T(8,128)S(1)}, u32[]{:S(2)}, u32[]{:S(2)}) %collective-permute-start.38) | collective-permute-done | bytes 786464 | tf_op jit(solution)/shard_map/cond/branch_1_fun/ppermute | solution.py:271
  263.6 3.2 %restore.44 = f32[32,288,768]{2,1,0:T(8,128)} custom-call(s32[9]{0:T(128)S(1)} %select_reduce_fusion.1.offset_ref, s32[1]{0:T(128)} %bitcast.25.end_ref, f32[2,288,768]{2,1,0:T(8,128)S(1)} %get-tuple-element.807.moved_ref, f32[96,2,8,128]{3,2,1,0:T(8,128)S(1)} %collective-permute-done.38.arrived_ref, ...), custom_call_target="tpu_custom_call", output_to_operand_aliasing={{}: (10, {})} | custom-call | flops 481296384 | bytes 3538944 | tf_op jit(solution)/shard_map/cond/branch_1_fun/restore/pallas_call | solution.py:210
  (135 shorter events, 19.8 us)
Async XLA Ops:
  6.5 14.9 %copy-start.46 = (f32[1,144,768]{2,1,0:T(8,128)S(1)}, f32[1,144,768]{2,1,0:T(8,128)}, u32[]{:S(2)}) copy-start(f32[1,144,768]{2,1,0:T(8,128)} %param.14) | copy-start | bytes 1327108
  6.5 46.8 %all-gather.6.cloned.1.call-start = ((), (), s32[]{:S(2)}) async-start(), calls=%async_computation | async-start | bytes 2654208 | tf_op jit(solution)/shard_map/all_gather | solution.py:342
  7.3 46.1 %copy-start.47 = (s32[32]{0:T(128)S(1)}, s32[32]{0:T(128)}, u32[]{:S(2)}) copy-start(s32[32]{0:T(128)} %param.16) | copy-start | bytes 388
  7.3 46.1 %copy-start.52 = (s32[768]{0:T(1024)S(1)}, s32[768]{0:T(1024)}, u32[]{:S(2)}) copy-start(s32[768]{0:T(1024)} %param.18) | copy-start | bytes 9220
  8.0 39.8 %collective-permute-start.60 = (f32[1,768]{1,0:T(1,128)S(1)}, f32[1,768]{1,0:T(1,128)S(1)}, u32[]{:S(2)}, u32[]{:S(2)}) collective-permute-start(f32[1,768]{1,0:T(1,128)S(1)} %slice_bitcast_fusion.12), channel_id=1, source_target_pairs={{4,0},{8,4},{12,8},{0,12},{5,1},{9,5},{13,9},{1,13},{6,2},{10,6},{... | collective-permute-start | bytes 9224 | tf_op jit(solution)/shard_map/ppermute | solution.py:344
  14.6 37.6 %collective-permute-start.61 = (f32[32,2,768]{2,1,0:T(2,128)S(1)}, f32[32,2,768]{2,1,0:T(2,128)S(1)}, u32[]{:S(2)}, u32[]{:S(2)}) collective-permute-start(f32[32,2,768]{2,1,0:T(2,128)S(1)} %get-tuple-element.1007), channel_id=1, source_target_pairs={{0,4},{4,8},{8,12},{12,0},{1,5},{5,9},{9,13},{13,1},{2,6},{6,10},{... | collective-permute-start | bytes 589832 | tf_op jit(solution)/shard_map/ppermute | solution.py:285
  14.7 37.6 %collective-permute-start.62 = (f32[32,2,768]{2,1,0:T(2,128)S(1)}, f32[32,2,768]{2,1,0:T(2,128)}, u32[]{:S(2)}, u32[]{:S(2)}) collective-permute-start(f32[32,2,768]{2,1,0:T(2,128)S(1)} %get-tuple-element.1008), channel_id=1, source_target_pairs={{4,0},{8,4},{12,8},{0,12},{5,1},{9,5},{13,9},{1,13},{6,2},{10,6},{... | collective-permute-start | bytes 589832 | tf_op jit(solution)/shard_map/ppermute | solution.py:286
  53.6 3.2 %copy-start.48 = (s32[1,640]{1,0:T(1,128)}, s32[1,640]{1,0:T(1,128)S(1)}, u32[]{:S(2)}) copy-start(s32[1,640]{1,0:T(1,128)S(1)} %get-tuple-element.785) | copy-start | bytes 7684 | tf_op jit(solution)/shard_map/cond
  53.6 6.6 %copy-start.29 = (bf16[288,576]{1,0:T(8,128)(2,1)}, bf16[288,576]{1,0:T(8,128)(2,1)S(1)}, u32[]{:S(2)}) copy-start(bf16[288,576]{1,0:T(8,128)(2,1)S(1)} %get-tuple-element.765.low_ref) | copy-start | bytes 995332 | tf_op jit(solution)/shard_map/cond
  53.6 6.6 %copy-start.35 = (f32[32,4,768]{2,1,0:T(4,128)}, f32[32,4,768]{2,1,0:T(4,128)S(1)}, u32[]{:S(2)}) copy-start(f32[32,4,768]{2,1,0:T(4,128)S(1)} %get-tuple-element.745.edge_ref) | copy-start | bytes 1179652 | tf_op jit(solution)/shard_map/cond
  53.9 2.7 copy-start.43
  59.3 2.8 copy-start.18
  60.1 9.1 %copy-start.2 = (f32[9,288,768]{2,1,0:T(8,128)}, f32[9,288,768]{2,1,0:T(8,128)S(1)}, u32[]{:S(2)}) copy-start(f32[9,288,768]{2,1,0:T(8,128)S(1)} %broadcast_multiply_fusion.1.weight_ref) | copy-start | bytes 23887876 | tf_op jit(solution)/shard_map/cond
  69.1 13.1 %collective-permute-start.20 = (f32[96,1,8,128]{3,2,1,0:T(8,128)S(1)}, f32[96,1,8,128]{3,2,1,0:T(8,128)S(1)}, u32[]{:S(2)}, u32[]{:S(2)}) collective-permute-start(f32[96,1,8,128]{3,2,1,0:T(8,128)S(1)} %get-tuple-element.769), channel_id=1, source_target_pairs={{0,4},{4,0},{8,12},{12,8},{1,5},{5,1},{9,13},{13,9},{2,6},{6,2},{1... | collective-permute-start | bytes 1179656 | tf_op jit(solution)/shard_map/cond/branch_1_fun/ppermute | solution.py:271
  80.3 1.9 copy-start.8
  83.0 18.8 %collective-permute-start.21 = (f32[96,1,8,128]{3,2,1,0:T(8,128)}, f32[96,1,8,128]{3,2,1,0:T(8,128)}, u32[]{:S(2)}, u32[]{:S(2)}) collective-permute-start(f32[96,1,8,128]{3,2,1,0:T(8,128)} %add.297), channel_id=1, source_target_pairs={{4,8},{8,4},{5,9},{9,5},{6,10},{10,6},{7,11},{11,7},{20,24},{24,20... | collective-permute-start | bytes 1179656 | tf_op jit(solution)/shard_map/cond/branch_1_fun/ppermute | solution.py:272
  84.4 18.8 %collective-permute-start.22 = (f32[96,2,8,128]{3,2,1,0:T(8,128)S(1)}, f32[96,2,8,128]{3,2,1,0:T(8,128)}, u32[]{:S(2)}, u32[]{:S(2)}) collective-permute-start(f32[96,2,8,128]{3,2,1,0:T(8,128)S(1)} %get-tuple-element.773), channel_id=1, source_target_pairs={{0,4},{4,0},{8,12},{12,8},{1,5},{5,1},{9,13},{13,9},{2,6},{6,2},{1... | collective-permute-start | bytes 2359304 | tf_op jit(solution)/shard_map/cond/branch_1_fun/ppermute | solution.py:271
  87.4 3.3 %copy-start.3 = (f32[9,288,768]{2,1,0:T(8,128)S(1)}, f32[9,288,768]{2,1,0:T(8,128)}, u32[]{:S(2)}) copy-start(f32[9,288,768]{2,1,0:T(8,128)} %copy-done.2) | copy-start | bytes 23887876 | tf_op jit(solution)/shard_map/cond
  101.7 5.0 %copy-start.19 = (bf16[8,288,768]{2,1,0:T(8,128)(2,1)S(1)}, bf16[8,288,768]{2,1,0:T(8,128)(2,1)}, u32[]{:S(2)}) copy-start(bf16[8,288,768]{2,1,0:T(8,128)(2,1)} %get-tuple-element.948.source_ref) | copy-start | bytes 10616836 | tf_op jit(solution)/shard_map/cond
  101.7 5.0 %copy-start.30 = (bf16[288,576]{1,0:T(8,128)(2,1)S(1)}, bf16[288,576]{1,0:T(8,128)(2,1)}, u32[]{:S(2)}) copy-start(bf16[288,576]{1,0:T(8,128)(2,1)} %copy-done.29) | copy-start | bytes 995332 | tf_op jit(solution)/shard_map/cond
  101.8 5.0 %copy-start.36 = (f32[32,4,768]{2,1,0:T(4,128)S(1)}, f32[32,4,768]{2,1,0:T(4,128)}, u32[]{:S(2)}) copy-start(f32[32,4,768]{2,1,0:T(4,128)} %copy-done.35) | copy-start | bytes 1179652 | tf_op jit(solution)/shard_map/cond
  104.5 17.1 %collective-permute-start.24 = (f32[96,2,8,128]{3,2,1,0:T(8,128)S(1)}, f32[96,2,8,128]{3,2,1,0:T(8,128)S(1)}, u32[]{:S(2)}, u32[]{:S(2)}) collective-permute-start(f32[96,2,8,128]{3,2,1,0:T(8,128)S(1)} %broadcast_select_fusion.1.held_ref), channel_id=1, source_target_pairs={{0,4},{4,0},{8,12},{12,8},{1,5},{5,1},{9,13},{13,9},{2,6},{6,2},{1... | collective-permute-start | bytes 2359304 | tf_op jit(solution)/shard_map/cond/branch_1_fun/ppermute | solution.py:271
  106.0 15.6 %collective-permute-start.23 = (f32[96,2,8,128]{3,2,1,0:T(8,128)S(1)}, f32[96,2,8,128]{3,2,1,0:T(8,128)S(1)}, u32[]{:S(2)}, u32[]{:S(2)}) collective-permute-start(f32[96,2,8,128]{3,2,1,0:T(8,128)S(1)} %add.299), channel_id=1, source_target_pairs={{4,8},{8,4},{5,9},{9,5},{6,10},{10,6},{7,11},{11,7},{20,24},{24,20... | collective-permute-start | bytes 2359304 | tf_op jit(solution)/shard_map/cond/branch_1_fun/ppermute | solution.py:272
  116.8 9.7 %copy-start.49 = (s32[1,640]{1,0:T(1,128)S(1)}, s32[1,640]{1,0:T(1,128)}, u32[]{:S(2)}) copy-start(s32[1,640]{1,0:T(1,128)} %copy-done.48) | copy-start | bytes 7684 | tf_op jit(solution)/shard_map/cond
  116.8 9.9 %copy-start.25 = (bf16[576,576]{1,0:T(8,128)(2,1)S(1)}, bf16[576,576]{1,0:T(8,128)(2,1)}, u32[]{:S(2)}) copy-start(bf16[576,576]{1,0:T(8,128)(2,1)} %get-tuple-element.786.both_ref) | copy-start | bytes 1990660 | tf_op jit(solution)/shard_map/cond
  116.8 9.9 %copy-start.40 = (bf16[256,768]{1,0:T(8,128)(2,1)S(1)}, bf16[256,768]{1,0:T(8,128)(2,1)}, u32[]{:S(2)}) copy-start(bf16[256,768]{1,0:T(8,128)(2,1)} %get-tuple-element.787.put_ref) | copy-start | bytes 1179652 | tf_op jit(solution)/shard_map/cond
  121.7 8.3 %slice-start.2 = ((s8[7962624]{0:T(1024)(128)(4,1)}), s8[4194304]{0:T(1024)(128)(4,1)S(1)}, s32[]{:S(2)}) async-start(s8[7962624]{0:T(1024)(128)(4,1)} %bitcast.239), calls=%async_computation.3 | async-start | bytes 8388608 | tf_op jit(solution)/shard_map/cond
  121.8 18.1 %collective-permute-start.26 = (f32[96,2,8,128]{3,2,1,0:T(8,128)S(1)}, f32[96,2,8,128]{3,2,1,0:T(8,128)S(1)}, u32[]{:S(2)}, u32[]{:S(2)}) collective-permute-start(f32[96,2,8,128]{3,2,1,0:T(8,128)S(1)} %add_select_fusion.12.held_ref), channel_id=1, source_target_pairs={{0,4},{4,0},{8,12},{12,8},{1,5},{5,1},{9,13},{13,9},{2,6},{6,2},{1... | collective-permute-start | bytes 2359304 | tf_op jit(solution)/shard_map/cond/branch_1_fun/ppermute | solution.py:271
  125.4 14.6 %collective-permute-start.25 = (f32[96,2,8,128]{3,2,1,0:T(8,128)S(1)}, f32[96,2,8,128]{3,2,1,0:T(8,128)S(1)}, u32[]{:S(2)}, u32[]{:S(2)}) collective-permute-start(f32[96,2,8,128]{3,2,1,0:T(8,128)S(1)} %add.301), channel_id=1, source_target_pairs={{4,8},{8,4},{5,9},{9,5},{6,10},{10,6},{7,11},{11,7},{20,24},{24,20... | collective-permute-start | bytes 2359304 | tf_op jit(solution)/shard_map/cond/branch_1_fun/ppermute | solution.py:272
  126.7 3.2 %slice-start.3 = ((s8[7962624]{0:T(1024)(128)(4,1)}), s8[3768320]{0:T(1024)(128)(4,1)S(1)}, s32[]{:S(2)}) async-start(s8[7962624]{0:T(1024)(128)(4,1)} %bitcast.239), calls=%async_computation.4 | async-start | bytes 7536640 | tf_op jit(solution)/shard_map/cond
  140.2 14.1 %copy-start.9 = (f32[4,288,768]{2,1,0:T(8,128)S(1)}, f32[4,288,768]{2,1,0:T(8,128)}, u32[]{:S(2)}) copy-start(f32[4,288,768]{2,1,0:T(8,128)} %copy-done.8) | copy-start | bytes 10616836 | tf_op jit(solution)/shard_map/cond
  140.2 18.9 %collective-permute-start.28 = (f32[96,2,8,128]{3,2,1,0:T(8,128)S(1)}, f32[96,2,8,128]{3,2,1,0:T(8,128)S(1)}, u32[]{:S(2)}, u32[]{:S(2)}) collective-permute-start(f32[96,2,8,128]{3,2,1,0:T(8,128)S(1)} %add_select_fusion.11.held_ref), channel_id=1, source_target_pairs={{0,4},{4,0},{8,12},{12,8},{1,5},{5,1},{9,13},{13,9},{2,6},{6,2},{1... | collective-permute-start | bytes 2359304 | tf_op jit(solution)/shard_map/cond/branch_1_fun/ppermute | solution.py:271
  143.6 15.7 %collective-permute-start.27 = (f32[96,2,8,128]{3,2,1,0:T(8,128)S(1)}, f32[96,2,8,128]{3,2,1,0:T(8,128)S(1)}, u32[]{:S(2)}, u32[]{:S(2)}) collective-permute-start(f32[96,2,8,128]{3,2,1,0:T(8,128)S(1)} %add.303), channel_id=1, source_target_pairs={{4,8},{8,4},{5,9},{9,5},{6,10},{10,6},{7,11},{11,7},{20,24},{24,20... | collective-permute-start | bytes 2359304 | tf_op jit(solution)/shard_map/cond/branch_1_fun/ppermute | solution.py:272
  159.4 17.6 %collective-permute-start.30 = (f32[96,2,8,128]{3,2,1,0:T(8,128)S(1)}, f32[96,2,8,128]{3,2,1,0:T(8,128)S(1)}, u32[]{:S(2)}, u32[]{:S(2)}) collective-permute-start(f32[96,2,8,128]{3,2,1,0:T(8,128)S(1)} %add_select_fusion.10.held_ref), channel_id=1, source_target_pairs={{0,4},{4,0},{8,12},{12,8},{1,5},{5,1},{9,13},{13,9},{2,6},{6,2},{1... | collective-permute-start | bytes 2359304 | tf_op jit(solution)/shard_map/cond/branch_1_fun/ppermute | solution.py:271
  161.3 15.8 %collective-permute-start.29 = (f32[96,2,8,128]{3,2,1,0:T(8,128)S(1)}, f32[96,2,8,128]{3,2,1,0:T(8,128)S(1)}, u32[]{:S(2)}, u32[]{:S(2)}) collective-permute-start(f32[96,2,8,128]{3,2,1,0:T(8,128)S(1)} %add.309), channel_id=1, source_target_pairs={{4,8},{8,4},{5,9},{9,5},{6,10},{10,6},{7,11},{11,7},{20,24},{24,20... | collective-permute-start | bytes 2359304 | tf_op jit(solution)/shard_map/cond/branch_1_fun/ppermute | solution.py:272
  177.2 18.6 %collective-permute-start.32 = (f32[96,2,8,128]{3,2,1,0:T(8,128)S(1)}, f32[96,2,8,128]{3,2,1,0:T(8,128)S(1)}, u32[]{:S(2)}, u32[]{:S(2)}) collective-permute-start(f32[96,2,8,128]{3,2,1,0:T(8,128)S(1)} %add_select_fusion.9.held_ref), channel_id=1, source_target_pairs={{0,4},{4,0},{8,12},{12,8},{1,5},{5,1},{9,13},{13,9},{2,6},{6,2},{1... | collective-permute-start | bytes 2359304 | tf_op jit(solution)/shard_map/cond/branch_1_fun/ppermute | solution.py:271
  180.3 15.6 %collective-permute-start.31 = (f32[96,2,8,128]{3,2,1,0:T(8,128)S(1)}, f32[96,2,8,128]{3,2,1,0:T(8,128)S(1)}, u32[]{:S(2)}, u32[]{:S(2)}) collective-permute-start(f32[96,2,8,128]{3,2,1,0:T(8,128)S(1)} %add.311), channel_id=1, source_target_pairs={{4,8},{8,4},{5,9},{9,5},{6,10},{10,6},{7,11},{11,7},{20,24},{24,20... | collective-permute-start | bytes 2359304 | tf_op jit(solution)/shard_map/cond/branch_1_fun/ppermute | solution.py:272
  196.1 14.4 %collective-permute-start.34 = (f32[96,2,8,128]{3,2,1,0:T(8,128)S(1)}, f32[96,2,8,128]{3,2,1,0:T(8,128)S(1)}, u32[]{:S(2)}, u32[]{:S(2)}) collective-permute-start(f32[96,2,8,128]{3,2,1,0:T(8,128)S(1)} %add_select_fusion.8.held_ref), channel_id=1, source_target_pairs={{0,4},{4,0},{8,12},{12,8},{1,5},{5,1},{9,13},{13,9},{2,6},{6,2},{1... | collective-permute-start | bytes 2359304 | tf_op jit(solution)/shard_map/cond/branch_1_fun/ppermute | solution.py:271
  198.1 12.5 %collective-permute-start.33 = (f32[96,2,8,128]{3,2,1,0:T(8,128)S(1)}, f32[96,2,8,128]{3,2,1,0:T(8,128)S(1)}, u32[]{:S(2)}, u32[]{:S(2)}) collective-permute-start(f32[96,2,8,128]{3,2,1,0:T(8,128)S(1)} %add.313), channel_id=1, source_target_pairs={{4,8},{8,4},{5,9},{9,5},{6,10},{10,6},{7,11},{11,7},{20,24},{24,20... | collective-permute-start | bytes 2359304 | tf_op jit(solution)/shard_map/cond/branch_1_fun/ppermute | solution.py:272
  210.8 13.1 %collective-permute-start.35 = (f32[96,2,8,128]{3,2,1,0:T(8,128)S(1)}, f32[96,2,8,128]{3,2,1,0:T(8,128)S(1)}, u32[]{:S(2)}, u32[]{:S(2)}) collective-permute-start(f32[96,2,8,128]{3,2,1,0:T(8,128)S(1)} %add.315), channel_id=1, source_target_pairs={{4,8},{8,4},{5,9},{9,5},{6,10},{10,6},{7,11},{11,7},{20,24},{24,20... | collective-permute-start | bytes 2359304 | tf_op jit(solution)/shard_map/cond/branch_1_fun/ppermute | solution.py:272
  211.5 18.8 %collective-permute-start.36 = (f32[96,2,8,128]{3,2,1,0:T(8,128)S(1)}, f32[96,2,8,128]{3,2,1,0:T(8,128)S(1)}, u32[]{:S(2)}, u32[]{:S(2)}) collective-permute-start(f32[96,2,8,128]{3,2,1,0:T(8,128)S(1)} %add_select_fusion.7.held_ref), channel_id=1, source_target_pairs={{0,4},{4,0},{8,12},{12,8},{1,5},{5,1},{9,13},{13,9},{2,6},{6,2},{1... | collective-permute-start | bytes 2359304 | tf_op jit(solution)/shard_map/cond/branch_1_fun/ppermute | solution.py:271
  230.4 11.2 %collective-permute-start.37 = (f32[96,2,8,128]{3,2,1,0:T(8,128)S(1)}, f32[96,2,8,128]{3,2,1,0:T(8,128)S(1)}, u32[]{:S(2)}, u32[]{:S(2)}) collective-permute-start(f32[96,2,8,128]{3,2,1,0:T(8,128)S(1)} %broadcast_add_fusion.1), channel_id=1, source_target_pairs={{4,8},{8,4},{5,9},{9,5},{6,10},{10,6},{7,11},{11,7},{20,24},{24,20... | collective-permute-start | bytes 2359304 | tf_op jit(solution)/shard_map/cond/branch_1_fun/ppermute | solution.py:272
  231.1 21.4 %collective-permute-start.39 = (f32[96,2,8,128]{3,2,1,0:T(8,128)S(1)}, f32[96,2,8,128]{3,2,1,0:T(8,128)S(1)}, u32[]{:S(2)}, u32[]{:S(2)}) collective-permute-start(f32[96,2,8,128]{3,2,1,0:T(8,128)S(1)} %add.316.held_ref), channel_id=1, source_target_pairs={{0,4},{4,0},{8,12},{12,8},{1,5},{5,1},{9,13},{13,9},{2,6},{6,2},{1... | collective-permute-start | bytes 2359304 | tf_op jit(solution)/shard_map/cond/branch_1_fun/ppermute | solution.py:271
  241.7 21.9 %collective-permute-start.38 = (f32[96,2,8,128]{3,2,1,0:T(8,128)S(1)}, f32[96,2,8,128]{3,2,1,0:T(8,128)S(1)}, u32[]{:S(2)}, u32[]{:S(2)}) collective-permute-start(f32[96,2,8,128]{3,2,1,0:T(8,128)S(1)} %add.318.held_ref), channel_id=1, source_target_pairs={{0,4},{4,0},{8,12},{12,8},{1,5},{5,1},{9,13},{13,9},{2,6},{6,2},{1... | collective-permute-start | bytes 2359304 | tf_op jit(solution)/shard_map/cond/branch_1_fun/ppermute | solution.py:271
Sparse Core Ops, SparseCore 0:
  8.9 41.6 all-gather.5
where the time goes:
time: 280 us; the launch traced here: 282 us
  Pallas kernels  125 us (45%)
  starting transfers between devices  54.7 us (20%)
  blocking collectives  26.8 us (10%)
  waiting for transfers between devices  23.3 us (8%)
  other arithmetic  15.5 us (6%)
  between operations  15.1 us (5%)
  local copies, waits for them, and re-layouts  12.3 us (4%)
  loops' own time  8.56 us (3%)
    pallas_call x9, Pallas kernels, forward(): pl.pallas_call(functools.partial(forward_kernel, cap, first=base), grid_s...  85.1 us
    pallas_call x9, Pallas kernels, inverse(): pl.pallas_call(functools.partial(inverse_kernel, cap), grid_spec=grid_spe...  40.1 us
    ppermute x11, starting transfers between devices, stepped_pipeline(): swapped = None if sent is None else lax.ppermute(sent, 'lon', swap)  38 us
    ppermute x11, waiting for transfers between devices, stepped_pipeline(): swapped = None if sent is None else lax.ppermute(sent, 'lon', swap)  22.5 us
    all_gather x1, blocking collectives, body(): thick = lax.all_gather(thickness, 'tag', axis=0, tiled=True)  22.5 us
    another operation x1, loops' own time, body(): out = lax.switch(index, [functools.partial(run, cap) for cap in caps])  8.56 us
    ppermute x9, starting transfers between devices, stepped_pipeline(): crossed = None if pair_sum is None else lax.ppermute(pair_sum, 'lon', cross)  7.82 us
    cond x34, local copies, waits for them, and re-layouts  7.05 us
  transfers between devices with their start and end apart: 24, of which 5 were waited for; matrix products, arithmetic and copies ran while one was open for 4% of the time, Pallas kernels for 41%

commit v1 on v0

--- a/solution.py
+++ b/solution.py
@@ -14,8 +14,8 @@
 WAVES = 32
 LANES = 128
 CHUNK = 4
-CAPS = (0.6, 0.66, 1.0)
-VMEM = 24 * 1024 * 1024
+CAPS = (0.605, 0.66, 1.0)
+VMEM = 18 * 1024 * 1024
 
 
 def wave_table(length):
@@ -49,17 +49,45 @@
     )
 
 
-def stencil_weights(zonal, zonal_next, merid, merid_next, factor):
-    east = divergence(zonal, zonal_next)
-    north = divergence(merid, merid_next)
-    parts = [east[0], east[1], east[3], east[4], north[0], north[1], north[3], north[4], east[2] + north[2]]
-    return jnp.stack([part * factor for part in parts])
+def weight_kernel(fields_ref, thick_ref, end_ref, out_ref, wide):
+    length, lats = thick_ref.shape
+    wide[0:length] = fields_ref[0]
+    wide[length : length + 1] = end_ref[...]
+    lat = lax.broadcasted_iota(jnp.int32, (8, lats), 1)
+    for start in range(0, length, 8):
+        here = slice(start, start + 8)
+        merid = jnp.where(lat > 0, fields_ref[1, here], 0.0)
+        north = jnp.where(lat < lats - 1, pltpu.roll(merid, lats - 1, 1), 0.0)
+        factor = -1.0 / thick_ref[here]
+        along = divergence(wide[here], wide[start + 1 : start + 9])
+        across = divergence(merid, north)
+        for index, part in enumerate((along[0], along[1], along[3], along[4])):
+            out_ref[index, here] = part * factor
+        inside = (lat >= 2, lat >= 1, lat <= lats - 2, lat <= lats - 3)
+        for index, part in enumerate((across[0], across[1], across[3], across[4])):
+            out_ref[4 + index, here] = jnp.where(inside[index], part * factor, 0.0)
+        out_ref[8, here] = (along[2] + across[2]) * factor
+
+
+def stencil_weights(fields, thick, zonal_end):
+    length, lats = thick.shape
+    return pl.pallas_call(
+        weight_kernel,
+        in_specs=[RESIDENT] * 3,
+        out_specs=RESIDENT,
+        out_shape=jax.ShapeDtypeStruct((9, length, lats), jnp.float32),
+        scratch_shapes=[pltpu.VMEM((length + 8, lats), jnp.float32)],
+        compiler_params=pltpu.CompilerParams(vmem_limit_bytes=VMEM),
+        cost_estimate=pl.CostEstimate(flops=60 * length * lats, bytes_accessed=12 * length * lats * 4, transcendentals=0),
+        name="stencil_weights",
+    )(fields, thick, zonal_end)
 
 
 def forward_kernel(
     cap, offset_ref, region_ref, q_ref, edge_ref, weight_ref, source_ref, stays_ref, pick_ref, sign_ref,
-    high_ref, low_ref, moved_ref, out_ref, wide, tendency, spectrum, *, first
+    high_ref, low_ref, *rest, first
 ):
+    moved_ref, out_ref, wide, tendency, spectrum = rest[-5:]
     length, lats = q_ref.shape[1:]
     columns = high_ref.shape[1]
     step = 16
@@ -148,20 +176,26 @@
 RESIDENT = pl.BlockSpec(memory_space=pltpu.VMEM)
 
 
-def forward(base, size, cap, offsets, regions, tracer, edges, weights, source, stays, pick, sign, high, low):
+def forward(base, size, cap, offsets, regions, tracer, edges, weights, source, stays, pick, sign, high, low, out):
     tags, length, lats = tracer.shape
     pairs = size // 2
     constants = [weights, source, stays, pick, sign, high, low]
+    specs = [
+        pl.BlockSpec((2, length, lats), lambda p, *_: (base // 2 + p, 0, 0)),
+        pl.BlockSpec((2, 4, lats), lambda p, *_: (base // 2 + p, 0, 0)),
+    ] + [RESIDENT] * len(constants)
+    operands = [offsets, regions, tracer, edges] + constants
+    aliases = {}
+    if out is not None:
+        specs.append(pl.BlockSpec(memory_space=pl.ANY))
+        operands.append(out)
+        aliases = {len(operands) - 1: 0}
     grid_spec = pltpu.PrefetchScalarGridSpec(
         num_scalar_prefetch=2,
         grid=(pairs,),
-        in_specs=[
+        in_specs=specs,
+        out_specs=[
             pl.BlockSpec((2, length, lats), lambda p, *_: (base // 2 + p, 0, 0)),
-            pl.BlockSpec((2, 4, lats), lambda p, *_: (base // 2 + p, 0, 0)),
-        ]
-        + [RESIDENT] * len(constants),
-        out_specs=[
-            pl.BlockSpec((2, length, lats), lambda p, *_: (p, 0, 0)),
             pl.BlockSpec((cap, 1, GROUP, LANES), lambda p, *_: (0, p, 0, 0)),
         ],
         scratch_shapes=[
@@ -175,30 +209,26 @@
         functools.partial(forward_kernel, cap, first=base),
         grid_spec=grid_spec,
         out_shape=[
-            jax.ShapeDtypeStruct((size, length, lats), jnp.float32),
+            jax.ShapeDtypeStruct(tracer.shape, jnp.float32),
             jax.ShapeDtypeStruct((cap, pairs, GROUP, LANES), jnp.float32),
         ],
+        input_output_aliases=aliases,
         compiler_params=pltpu.CompilerParams(vmem_limit_bytes=VMEM),
         cost_estimate=pl.CostEstimate(flops=flops, bytes_accessed=5 * size * length * lats * 4, transcendentals=0),
         name="step_and_transform",
-    )(offsets, regions, tracer, edges, *constants)
-
-
-def inverse(base, size, cap, offsets, end, tracer, moved, arrived, held, keep, high, both, flip, put, out):
-    tags, length, lats = tracer.shape
+    )(*operands)
+
+
+def inverse(base, size, cap, offsets, end, out, arrived, held, keep, high, both, flip, put):
+    tags, length, lats = out.shape
     pairs = size // 2
     constants = [keep, high, both, flip, put]
     specs = [
-        pl.BlockSpec((2, length, lats), lambda p, *_: (p, 0, 0)),
+        pl.BlockSpec((2, length, lats), lambda p, *_: (base // 2 + p, 0, 0)),
         pl.BlockSpec((cap, 1, GROUP, LANES), lambda p, *_: (0, p, 0, 0)),
         pl.BlockSpec((cap, 1, GROUP, LANES), lambda p, *_: (0, p, 0, 0)),
     ] + [RESIDENT] * len(constants)
-    operands = [offsets, end, moved, arrived, held] + constants
-    aliases = {}
-    if out is not None:
-        specs.append(pl.BlockSpec(memory_space=pl.ANY))
-        operands.append(out)
-        aliases = {len(operands) - 1: 0}
+    operands = [offsets, end, out, arrived, held] + constants
     grid_spec = pltpu.PrefetchScalarGridSpec(
         num_scalar_prefetch=2,
         grid=(pairs,),
@@ -210,8 +240,8 @@
     return pl.pallas_call(
         functools.partial(inverse_kernel, cap),
         grid_spec=grid_spec,
-        out_shape=jax.ShapeDtypeStruct(tracer.shape, jnp.float32),
-        input_output_aliases=aliases,
+        out_shape=jax.ShapeDtypeStruct(out.shape, jnp.float32),
+        input_output_aliases={2: 0},
         compiler_params=pltpu.CompilerParams(vmem_limit_bytes=VMEM),
         cost_estimate=pl.CostEstimate(flops=flops, bytes_accessed=2 * size * length * lats * 4, transcendentals=0),
         name="restore",
@@ -235,9 +265,9 @@
 def plain_pipeline(chunks, forward_at, inverse_at, place, count, offsets):
     out = None
     for chunk in range(chunks):
-        moved, packed = forward_at(chunk, offsets)
+        out, packed = forward_at(chunk, out, offsets)
         total = sum_over_lon(packed, count, place)
-        out = inverse_at(chunk, moved, total, total, out, offsets)
+        out = inverse_at(chunk, out, total, total, offsets)
     return out
 
 
@@ -245,11 +275,13 @@
     swap = [(0, 1), (1, 0), (2, 3), (3, 2)]
     cross = [(1, 2), (2, 1)]
     end = (place == 0) | (place == count - 1)
-    moved, own = {}, {}
-    moved[0], own[0] = forward_at(0, offsets)
-    pair_sum = swapped = crossed = sent = out = None
+    own, back = {}, {}
+    out, own[0] = forward_at(0, None, offsets)
+    pair_sum = swapped = crossed = sent = None
+    done = 0
     for t in range(chunks + 3):
-        arrived, held = swapped, sent
+        if t >= 3:
+            back[t - 3] = swapped, sent
         total = None if crossed is None else pair_sum + crossed
         here = own.get(t)
         if here is None:
@@ -257,25 +289,23 @@
         else:
             sent = here if total is None else jnp.where(end, here, total)
         pair_sum = own[t - 1] + swapped if 1 <= t <= chunks else None
+        token = offsets
         if t < chunks + 2:
             sending = [x for x in (sent, pair_sum) if x is not None]
-            extra = [out] if out is not None else []
-            result = lax.optimization_barrier((offsets, *sending, *extra))
-            token, result = result[0], list(result[1:])
+            token, out, *sending = lax.optimization_barrier((offsets, out, *sending))
+            if pair_sum is not None:
+                pair_sum = sending.pop()
             if sent is not None:
-                sent = result.pop(0)
-            if pair_sum is not None:
-                pair_sum = result.pop(0)
-            if extra:
-                out = result.pop(0)
+                sent = sending.pop()
             swapped = None if sent is None else lax.ppermute(sent, "lon", swap)
             crossed = None if pair_sum is None else lax.ppermute(pair_sum, "lon", cross)
-        else:
-            token = offsets
         if t + 1 < chunks:
-            moved[t + 1], own[t + 1] = forward_at(t + 1, token)
-        if t >= 3:
-            out = inverse_at(t - 3, moved[t - 3], arrived, held, out, token)
+            out, own[t + 1] = forward_at(t + 1, out, token)
+        quota = chunks if t == chunks + 2 else -(-(chunks - 1 - done) // (chunks + 2 - t)) if t >= chunks - 1 else 0
+        while quota and done in back:
+            out = inverse_at(done, out, *back[done], token)
+            done += 1
+            quota -= 1
     return out
 
 
@@ -336,33 +366,40 @@
     both = jnp.concatenate([high, low])
     put = jnp.concatenate([put, put])
     is_end = ((place == 0) | (place == count - 1)).astype(jnp.int32).reshape(1)
-    sizes = [CHUNK // 2] + [CHUNK] * ((tags - CHUNK) // CHUNK) + [CHUNK // 2]
+    sizes = [CHUNK] * (tags // CHUNK)
     bases = [sum(sizes[:i]) for i in range(len(sizes))]
 
-    gathered = lax.all_gather(courant, "tag", axis=1, tiled=True)
-    thick = lax.all_gather(thickness, "tag", axis=0, tiled=True)
-    zonal_end = lax.all_gather(lax.ppermute(courant[0, :1], "lon", backward_ring), "tag")[0]
+    tag_count, tag = lax.axis_size("tag"), lax.axis_index("tag")
+    if tag_count == 2:
+        cross = [(0, 1), (1, 0)]
+        other, other_thick = lax.ppermute(courant, "tag", cross), lax.ppermute(thickness, "tag", cross)
+        ahead_zonal = courant[0, :1]
+        same = lax.ppermute(ahead_zonal, "lon", backward_ring)
+        skew = lax.ppermute(ahead_zonal, ("lon", "tag"), [((i + 1) % count * 2, i * 2 + 1) for i in range(count)])
+        zonal_end = jnp.where(tag == 0, same, skew)
+
+        def in_order(mine, theirs, axis):
+            return jnp.concatenate([jnp.where(tag == 0, mine, theirs), jnp.where(tag == 0, theirs, mine)], axis=axis)
+
+        gathered, thick = in_order(courant, other, 1), in_order(thickness, other_thick, 0)
+    else:
+        gathered = lax.all_gather(courant, "tag", axis=1, tiled=True)
+        thick = lax.all_gather(thickness, "tag", axis=0, tiled=True)
+        zonal_end = lax.all_gather(lax.ppermute(courant[0, :1], "lon", backward_ring), "tag")[0]
     edges = jnp.concatenate(ring_edges(tracer[:, :2], tracer[:, length - 2 :], count), axis=1)
 
     def run(cap):
-        zonal, merid = gathered[0], gathered[1] * (lat > 0).astype(jnp.float32)
-        zonal_after = jnp.concatenate([zonal[1:], zonal_end])
-        merid_after = jnp.pad(merid[:, 1:], ((0, 0), (0, 1)))
-        weights = stencil_weights(zonal, zonal_after, merid, merid_after, -1.0 / thick)
-        ones = jnp.ones_like(lat, dtype=bool)
-        inside = jnp.stack([ones] * 4 + [lat >= 2, lat >= 1, lat <= lats - 2, lat <= lats - 3] + [ones])
-        weights = weights * inside.astype(jnp.float32)[:, None, :]
-
-        def forward_at(chunk, offsets):
+        weights, keep_, both_, flip_, put_, edges_ = lax.optimization_barrier((stencil_weights(gathered, thick, zonal_end), keep, both, flip, put, edges))
+
+        def forward_at(chunk, out, offsets):
             return forward(
-                bases[chunk], sizes[chunk], cap, offsets, region_map, tracer, edges, weights, emission, stays, one_hot,
-                sign, high, low,
+                bases[chunk], sizes[chunk], cap, offsets, region_map, tracer, edges_, weights, emission, stays, one_hot,
+                sign, high, low, out,
             )
 
-        def inverse_at(chunk, moved, arrived, held, out, offsets):
+        def inverse_at(chunk, out, arrived, held, offsets):
             return inverse(
-                bases[chunk], sizes[chunk], cap, offsets, is_end, tracer, moved, arrived, held, keep, high, both, flip,
-                put, out,
+                bases[chunk], sizes[chunk], cap, offsets, is_end, out, arrived, held, keep_, high, both_, flip_, put_
             )
 
         pipeline = stepped_pipeline if count == 4 else plain_pipeline

time: 280 us -> 251 us (0.90); the launches traced: 282 us -> 247 us
  blocking collectives: 26.8 us -> 0 us
  Pallas kernels: 125 us -> 142 us
  between operations: 15.1 us -> 2.6 us
  starting transfers between devices: 54.7 us -> 49.6 us
  waiting for transfers between devices: 23.3 us -> 19.4 us
    all_gather x2 -> x0, blocking collectives: 26.8 us -> none  [the longest x1 22.5 us: body(): thick = lax.all_gather(thickness, 'tag', axis=0, tiled=True)]
    ppermute x11 -> x10, waiting for transfers between devices: 22.5 us -> 8.81 us  [stepped_pipeline(): swapped = None if sent is None else lax.ppermute(sent, 'lon', swap)]
    ppermute x1 -> x4, waiting for transfers between devices: 0.01 us -> 10.6 us  [the longest x1 10.6 us: body(): lax.ppermute(thickness, 'tag', cross)]
    pallas_call x9 -> x8, Pallas kernels: 40.1 us -> 48.9 us  [inverse(): pl.pallas_call(functools.partial(inverse_kernel, cap), grid_spec=grid_spe...]
    ppermute x11 -> x10, starting transfers between devices: 38 us -> 29.5 us  [stepped_pipeline(): swapped = None if sent is None else lax.ppermute(sent, 'lon', swap)]
    pallas_call x9 -> x8, Pallas kernels: 85.1 us -> 90.8 us  [forward(): pl.pallas_call(functools.partial(forward_kernel, cap, first=base), grid_s...]
    ppermute x1 -> x4, starting transfers between devices: 5.05 us -> 8.47 us  [the longest x1 5.46 us: body(): lax.ppermute(ahead_zonal, ('lon', 'tag'), [((i + 1) % count * 2, i * 2 +...]
    unnamed x6 -> x10, local copies, waits for them, and re-layouts: 0.01 us -> 2.89 us
  transfers between devices with their start and end apart: 24 -> 24, of which waited for: 5 -> 7; matrix products, arithmetic and copies ran while one was open for 4% -> 5% of each run, Pallas kernels for 41% -> 49%
where the time goes in v1:
time: 251 us; the launch traced here: 247 us
  Pallas kernels  142 us (57%)
  starting transfers between devices  49.6 us (20%)
  waiting for transfers between devices  19.4 us (8%)
  other arithmetic  12.9 us (5%)
  local copies, waits for them, and re-layouts  12.5 us (5%)
  loops' own time  8.06 us (3%)
  between operations  2.6 us (1%)
    pallas_call x8, Pallas kernels, forward(): pl.pallas_call(functools.partial(forward_kernel, cap, first=base), grid_s...  90.8 us
    pallas_call x8, Pallas kernels, inverse(): pl.pallas_call(functools.partial(inverse_kernel, cap), grid_spec=grid_spe...  48.9 us
    ppermute x10, starting transfers between devices, stepped_pipeline(): swapped = None if sent is None else lax.ppermute(sent, 'lon', swap)  29.5 us
    ppermute x1, waiting for transfers between devices, body(): lax.ppermute(thickness, 'tag', cross)  10.6 us
    ppermute x10, waiting for transfers between devices, stepped_pipeline(): swapped = None if sent is None else lax.ppermute(sent, 'lon', swap)  8.81 us
    another operation x1, loops' own time, body(): out = lax.switch(index, [functools.partial(run, cap) for cap in caps])  8.06 us
    ppermute x8, starting transfers between devices, stepped_pipeline(): crossed = None if pair_sum is None else lax.ppermute(pair_sum, 'lon', cross)  7.78 us
    cond x30, local copies, waits for them, and re-layouts  6.15 us
  transfers between devices with their start and end apart: 24, of which 7 were waited for; matrix products, arithmetic and copies ran while one was open for 5% of the time, Pallas kernels for 49%

profile of v1, /device:TPU:0, one launch (start us, length us, event | category | flops | bytes accessed | tf_op | source)
XLA Modules:
  0.0 247.3 jit_solution(9522391368660843977)
XLA Ops:
  0.0 2.9 %collective-permute-start.56 = (f32[2,144,768]{2,1,0:T(8,128)}, f32[2,144,768]{2,1,0:T(8,128)}, u32[]{:S(2)}, u32[]{:S(2)}) collective-permute-start(f32[2,144,768]{2,1,0:T(8,128)} %bitcast.70), channel_id=1, source_target_pairs={{0,2},{2,0},{1,3},{3,1},{4,6},{6,4},{5,7},{7,5},{8,10},{10,8},{9,1... | collective-permute-start | bytes 2654216 | tf_op jit(solution)/shard_map/ppermute | solution.py:375
  3.7 5.5 %collective-permute-start.55 = (f32[1,768]{1,0:T(1,128)S(1)}, f32[1,768]{1,0:T(1,128)S(1)}, u32[]{:S(2)}, u32[]{:S(2)}) collective-permute-start(f32[1,768]{1,0:T(1,128)S(1)} %slice_bitcast_fusion), channel_id=1, source_target_pairs={{4,2},{8,6},{12,10},{0,14},{5,3},{9,7},{13,11},{1,15},{20,18},{24,... | collective-permute-start | bytes 9224 | tf_op jit(solution)/shard_map/ppermute | solution.py:378
  9.2 1.5 fusion.26
  10.8 3.8 %collective-permute-start.59 = (f32[32,2,768]{2,1,0:T(2,128)S(1)}, f32[32,2,768]{2,1,0:T(2,128)S(1)}, u32[]{:S(2)}, u32[]{:S(2)}) collective-permute-start(f32[32,2,768]{2,1,0:T(2,128)S(1)} %get-tuple-element.981), channel_id=1, source_target_pairs={{4,0},{8,4},{12,8},{0,12},{5,1},{9,5},{13,9},{1,13},{6,2},{10,6},{... | collective-permute-start | bytes 589832 | tf_op jit(solution)/shard_map/ppermute | solution.py:316
  17.0 1.2 constant_dynamic-slice_fusion
  18.2 0.9 pad_maximum_fusion.2
  21.7 10.6 %collective-permute-done.57 = f32[144,768]{1,0:T(8,128)S(1)} collective-permute-done((f32[144,768]{1,0:T(8,128)}, f32[144,768]{1,0:T(8,128)S(1)}, u32[]{:S(2)}, u32[]{:S(2)}) %collective-permute-start.57) | collective-permute-done | bytes 442400 | tf_op jit(solution)/shard_map/ppermute | solution.py:375
  32.4 1.1 copy-done.27
  33.5 1.3 broadcast_select_fusion.4
  35.1 1.8 copy-done.10
  36.8 209.4 %conditional.1 = (f32[32,1,288,768]{3,2,1,0:T(8,128)}) conditional(s32[]{:T(128)} %clamp.3, (s32[9,9]{1,0:T(8,128)S(1)}, s32[9,9]{1,0:T(8,128)S(1)}, s32[9]{0:T(128)S(1)}, (), s32[]{:T(128)}, /*index=5*/s32[]{:T(128)}, s32[]{:T(128)}, pred[]{:T(512)}, f32[1,768]{1,0:T(1,128)S(1)}, f32[1,768]{1,0:T(1,128)S(1)}, ...), branch_computations={%region_4.7_spmd, %region_7.10_spmd, %region_10.13_spmd} | conditional | flops 15421826048 | bytes 699659392 | solution.py:413
  37.9 2.6 %stencil_weights.3.weight_ref = f32[9,288,768]{2,1,0:T(8,128)S(1)} custom-call(f32[2,288,768]{2,1,0:T(8,128)S(1)} %get-tuple-element.646.fields_ref, f32[288,768]{1,0:T(8,128)S(1)} %get-tuple-element.647.thick_ref, f32[1,768]{1,0:T(1,128)S(1)} %broadcast_select_fusion.end_ref), custom_call_target="tpu_custom_call" | custom-call | flops 13271040 | bytes 10616832 | tf_op jit(solution)/shard_map/cond/branch_0_fun/stencil_weights/pallas_call | solution.py:74
  40.7 11.3 %step_and_transform.24 = (f32[32,288,768]{2,1,0:T(8,128)S(1)}, f32[88,2,8,128]{3,2,1,0:T(8,128)S(1)}) custom-call(s32[9]{0:T(128)S(1)} %select_reduce_fusion.offset_ref, s32[32]{0:T(128)S(1)} %get-tuple-element.941.region_ref, f32[32,288,768]{2,1,0:T(8,128)} %get-tuple-element.645.q_ref, f32[32,4,768]{2,1,0:T(4,128)S(1)} %get-tuple-element.664.edge_ref, ...), custom_call_target="tpu_custom_call" | custom-call | flops 962592768 | bytes 17694720 | tf_op jit(solution)/shard_map/cond/branch_0_fun/step_and_transform/pallas_call | solution.py:208
  52.0 1.9 collective-permute-start
  53.9 10.0 %step_and_transform.25 = (f32[32,288,768]{2,1,0:T(8,128)S(1)}, f32[88,2,8,128]{3,2,1,0:T(8,128)S(1)}) custom-call(s32[9]{0:T(128)S(1)} %select_reduce_fusion.offset_ref, s32[32]{0:T(128)S(1)} %get-tuple-element.941.region_ref, f32[32,288,768]{2,1,0:T(8,128)} %get-tuple-element.645.q_ref, ...), custom_call_target="tpu_custom_call", output_to_operand_aliasing={{0}: (11, {})} | custom-call | flops 962592768 | bytes 17694720 | tf_op jit(solution)/shard_map/cond/branch_0_fun/step_and_transform/pallas_call | solution.py:208
  63.9 5.5 %collective-permute-done = f32[88,2,8,128]{3,2,1,0:T(8,128)S(1)} collective-permute-done((f32[88,2,8,128]{3,2,1,0:T(8,128)S(1)}, f32[88,2,8,128]{3,2,1,0:T(8,128)S(1)}, u32[]{:S(2)}, u32[]{:S(2)}) %collective-permute-start) | collective-permute-done | bytes 720928 | tf_op jit(solution)/shard_map/cond/branch_0_fun/ppermute | solution.py:300
  69.4 1.8 add.199
  71.2 2.8 %copy-done.7 = f32[32,288,768]{2,1,0:T(8,128)} copy-done((f32[32,288,768]{2,1,0:T(8,128)}, f32[32,288,768]{2,1,0:T(8,128)S(1)}, u32[]{:S(2)}) %copy-start.7) | copy-done | bytes 28311576 | tf_op jit(solution)/shard_map/cond
  74.2 1.7 collective-permute-start.1
  76.0 3.3 %copy-done.1 = f32[9,288,768]{2,1,0:T(8,128)S(1)} copy-done((f32[9,288,768]{2,1,0:T(8,128)S(1)}, f32[9,288,768]{2,1,0:T(8,128)}, u32[]{:S(2)}) %copy-start.1) | copy-done | bytes 7962648 | tf_op jit(solution)/shard_map/cond
  79.2 12.2 %step_and_transform.26 = (f32[32,288,768]{2,1,0:T(8,128)}, f32[88,2,8,128]{3,2,1,0:T(8,128)S(1)}) custom-call(s32[9]{0:T(128)S(1)} %select_reduce_fusion.offset_ref, s32[32]{0:T(128)S(1)} %get-tuple-element.941.region_ref, f32[32,288,768]{2,1,0:T(8,128)} %get-tuple-element.645.q_ref, ...), custom_call_target="tpu_custom_call", output_to_operand_aliasing={{0}: (11, {})} | custom-call | flops 962592768 | bytes 17694720 | tf_op jit(solution)/shard_map/cond/branch_0_fun/step_and_transform/pallas_call | solution.py:208
  91.4 1.4 add.201
  92.8 1.6 add_select_fusion.5.held_ref
  94.5 3.8 %collective-permute-start.4 = (f32[88,2,8,128]{3,2,1,0:T(8,128)S(1)}, f32[88,2,8,128]{3,2,1,0:T(8,128)S(1)}, u32[]{:S(2)}, u32[]{:S(2)}) collective-permute-start(f32[88,2,8,128]{3,2,1,0:T(8,128)S(1)} %add_select_fusion.5.held_ref), channel_id=1, source_target_pairs={{0,4},{4,0},{8,12},{12,8},{1,5},{5,1},{9,13},{13,9},{2,6},{6,2},{1... | collective-permute-start | bytes 2162696 | tf_op jit(solution)/shard_map/cond/branch_0_fun/ppermute | solution.py:300
  99.1 11.9 %step_and_transform.27 = (f32[32,288,768]{2,1,0:T(8,128)}, f32[88,2,8,128]{3,2,1,0:T(8,128)S(1)}) custom-call(s32[9]{0:T(128)S(1)} %select_reduce_fusion.offset_ref, s32[32]{0:T(128)S(1)} %get-tuple-element.941.region_ref, f32[32,288,768]{2,1,0:T(8,128)} %get-tuple-element.645.q_ref, ...), custom_call_target="tpu_custom_call", output_to_operand_aliasing={{0}: (11, {})} | custom-call | flops 962592768 | bytes 17694720 | tf_op jit(solution)/shard_map/cond/branch_0_fun/step_and_transform/pallas_call | solution.py:208
  111.0 1.7 collective-permute-done.4.arrived_ref
  113.0 4.0 %collective-permute-start.6 = (f32[88,2,8,128]{3,2,1,0:T(8,128)S(1)}, f32[88,2,8,128]{3,2,1,0:T(8,128)S(1)}, u32[]{:S(2)}, u32[]{:S(2)}) collective-permute-start(f32[88,2,8,128]{3,2,1,0:T(8,128)S(1)} %add_select_fusion.4.held_ref), channel_id=1, source_target_pairs={{0,4},{4,0},{8,12},{12,8},{1,5},{5,1},{9,13},{13,9},{2,6},{6,2},{1... | collective-permute-start | bytes 2162696 | tf_op jit(solution)/shard_map/cond/branch_0_fun/ppermute | solution.py:300
  117.0 0.9 collective-permute-start.5
  118.0 11.6 %step_and_transform.28 = (f32[32,288,768]{2,1,0:T(8,128)}, f32[88,2,8,128]{3,2,1,0:T(8,128)S(1)}) custom-call(s32[9]{0:T(128)S(1)} %select_reduce_fusion.offset_ref, s32[32]{0:T(128)S(1)} %get-tuple-element.941.region_ref, f32[32,288,768]{2,1,0:T(8,128)S(1)} %bitcast.65, ...), custom_call_target="tpu_custom_call", output_to_operand_aliasing={{0}: (11, {})} | custom-call | flops 962592768 | bytes 17694720 | tf_op jit(solution)/shard_map/cond/branch_0_fun/step_and_transform/pallas_call | solution.py:208
  129.6 0.9 collective-permute-done.6.arrived_ref
  130.7 3.6 %collective-permute-start.8 = (f32[88,2,8,128]{3,2,1,0:T(8,128)S(1)}, f32[88,2,8,128]{3,2,1,0:T(8,128)S(1)}, u32[]{:S(2)}, u32[]{:S(2)}) collective-permute-start(f32[88,2,8,128]{3,2,1,0:T(8,128)S(1)} %add_select_fusion.3.held_ref), channel_id=1, source_target_pairs={{0,4},{4,0},{8,12},{12,8},{1,5},{5,1},{9,13},{13,9},{2,6},{6,2},{1... | collective-permute-start | bytes 2162696 | tf_op jit(solution)/shard_map/cond/branch_0_fun/ppermute | solution.py:300
  135.0 11.6 %step_and_transform.29 = (f32[32,288,768]{2,1,0:T(8,128)}, f32[88,2,8,128]{3,2,1,0:T(8,128)S(1)}) custom-call(s32[9]{0:T(128)S(1)} %select_reduce_fusion.offset_ref, s32[32]{0:T(128)S(1)} %get-tuple-element.941.region_ref, f32[32,288,768]{2,1,0:T(8,128)S(1)} %bitcast.65, ...), custom_call_target="tpu_custom_call", output_to_operand_aliasing={{0}: (11, {})} | custom-call | flops 962592768 | bytes 17694720 | tf_op jit(solution)/shard_map/cond/branch_0_fun/step_and_transform/pallas_call | solution.py:208
  147.2 3.6 %collective-permute-start.10 = (f32[88,2,8,128]{3,2,1,0:T(8,128)S(1)}, f32[88,2,8,128]{3,2,1,0:T(8,128)S(1)}, u32[]{:S(2)}, u32[]{:S(2)}) collective-permute-start(f32[88,2,8,128]{3,2,1,0:T(8,128)S(1)} %add_select_fusion.2.held_ref), channel_id=1, source_target_pairs={{0,4},{4,0},{8,12},{12,8},{1,5},{5,1},{9,13},{13,9},{2,6},{6,2},{1... | collective-permute-start | bytes 2162696 | tf_op jit(solution)/shard_map/cond/branch_0_fun/ppermute | solution.py:300
  150.8 0.9 collective-permute-start.9
  151.7 11.1 %step_and_transform.30 = (f32[32,288,768]{2,1,0:T(8,128)}, f32[88,2,8,128]{3,2,1,0:T(8,128)S(1)}) custom-call(s32[9]{0:T(128)S(1)} %select_reduce_fusion.offset_ref, s32[32]{0:T(128)S(1)} %get-tuple-element.941.region_ref, f32[32,288,768]{2,1,0:T(8,128)} %get-tuple-element.645.q_ref, ...), custom_call_target="tpu_custom_call", output_to_operand_aliasing={{0}: (11, {})} | custom-call | flops 962592768 | bytes 17694720 | tf_op jit(solution)/shard_map/cond/branch_0_fun/step_and_transform/pallas_call | solution.py:208
  163.5 3.6 %collective-permute-start.12 = (f32[88,2,8,128]{3,2,1,0:T(8,128)S(1)}, f32[88,2,8,128]{3,2,1,0:T(8,128)S(1)}, u32[]{:S(2)}, u32[]{:S(2)}) collective-permute-start(f32[88,2,8,128]{3,2,1,0:T(8,128)S(1)} %add_select_fusion.1.held_ref), channel_id=1, source_target_pairs={{0,4},{4,0},{8,12},{12,8},{1,5},{5,1},{9,13},{13,9},{2,6},{6,2},{1... | collective-permute-start | bytes 2162696 | tf_op jit(solution)/shard_map/cond/branch_0_fun/ppermute | solution.py:300
  167.8 11.1 %step_and_transform.31 = (f32[32,288,768]{2,1,0:T(8,128)}, f32[88,2,8,128]{3,2,1,0:T(8,128)S(1)}) custom-call(s32[9]{0:T(128)S(1)} %select_reduce_fusion.offset_ref, s32[32]{0:T(128)S(1)} %get-tuple-element.941.region_ref, f32[32,288,768]{2,1,0:T(8,128)} %get-tuple-element.645.q_ref, ...), custom_call_target="tpu_custom_call", output_to_operand_aliasing={{0}: (11, {})} | custom-call | flops 962592768 | bytes 17694720 | tf_op jit(solution)/shard_map/cond/branch_0_fun/step_and_transform/pallas_call | solution.py:208
  179.1 1.3 collective-permute-start.13
  180.4 6.6 %collective-permute-start.14 = (f32[88,2,8,128]{3,2,1,0:T(8,128)S(1)}, f32[88,2,8,128]{3,2,1,0:T(8,128)S(1)}, u32[]{:S(2)}, u32[]{:S(2)}) collective-permute-start(f32[88,2,8,128]{3,2,1,0:T(8,128)S(1)} %add_select_fusion.held_ref), channel_id=1, source_target_pairs={{0,4},{4,0},{8,12},{12,8},{1,5},{5,1},{9,13},{13,9},{2,6},{6,2},{1... | collective-permute-start | bytes 2162696 | tf_op jit(solution)/shard_map/cond/branch_0_fun/ppermute | solution.py:300
  187.0 6.1 %restore.24.moved_ref = f32[32,288,768]{2,1,0:T(8,128)} custom-call(s32[9]{0:T(128)S(1)} %select_reduce_fusion.offset_ref, s32[1]{0:T(128)} %bitcast.2.end_ref, f32[32,288,768]{2,1,0:T(8,128)} %get-tuple-element.716.moved_ref, f32[88,2,8,128]{3,2,1,0:T(8,128)S(1)} %collective-permute-done.4.arrived_ref, ...), custom_call_target="tpu_custom_call", output_to_operand_aliasing={{}: (2, {})} | custom-call | flops 962592768 | bytes 7077888 | tf_op jit(solution)/shard_map/cond/branch_0_fun/restore/pallas_call | solution.py:240
  193.1 6.1 %restore.25.moved_ref = f32[32,288,768]{2,1,0:T(8,128)} custom-call(s32[9]{0:T(128)S(1)} %select_reduce_fusion.offset_ref, s32[1]{0:T(128)} %bitcast.2.end_ref, f32[32,288,768]{2,1,0:T(8,128)} %restore.24.moved_ref, f32[88,2,8,128]{3,2,1,0:T(8,128)S(1)} %collective-permute-done.6.arrived_ref, ...), custom_call_target="tpu_custom_call", output_to_operand_aliasing={{}: (2, {})} | custom-call | flops 962592768 | bytes 7077888 | tf_op jit(solution)/shard_map/cond/branch_0_fun/restore/pallas_call | solution.py:240
  199.3 6.1 %restore.26.moved_ref = f32[32,288,768]{2,1,0:T(8,128)} custom-call(s32[9]{0:T(128)S(1)} %select_reduce_fusion.offset_ref, s32[1]{0:T(128)} %bitcast.2.end_ref, f32[32,288,768]{2,1,0:T(8,128)} %restore.25.moved_ref, f32[88,2,8,128]{3,2,1,0:T(8,128)S(1)} %collective-permute-done.8.arrived_ref, ...), custom_call_target="tpu_custom_call", output_to_operand_aliasing={{}: (2, {})} | custom-call | flops 962592768 | bytes 7077888 | tf_op jit(solution)/shard_map/cond/branch_0_fun/restore/pallas_call | solution.py:240
  206.3 2.1 collective-permute-start.16
  208.4 6.1 %restore.27.moved_ref = f32[32,288,768]{2,1,0:T(8,128)} custom-call(s32[9]{0:T(128)S(1)} %select_reduce_fusion.offset_ref, s32[1]{0:T(128)} %bitcast.2.end_ref, f32[32,288,768]{2,1,0:T(8,128)} %restore.26.moved_ref, f32[88,2,8,128]{3,2,1,0:T(8,128)S(1)} %collective-permute-done.10.arrived_ref, ...), custom_call_target="tpu_custom_call", output_to_operand_aliasing={{}: (2, {})} | custom-call | flops 962592768 | bytes 7077888 | tf_op jit(solution)/shard_map/cond/branch_0_fun/restore/pallas_call | solution.py:240
  214.5 6.1 %restore.28.moved_ref = f32[32,288,768]{2,1,0:T(8,128)} custom-call(s32[9]{0:T(128)S(1)} %select_reduce_fusion.offset_ref, s32[1]{0:T(128)} %bitcast.2.end_ref, f32[32,288,768]{2,1,0:T(8,128)} %restore.27.moved_ref, f32[88,2,8,128]{3,2,1,0:T(8,128)S(1)} %collective-permute-done.12.arrived_ref, ...), custom_call_target="tpu_custom_call", output_to_operand_aliasing={{}: (2, {})} | custom-call | flops 962592768 | bytes 7077888 | tf_op jit(solution)/shard_map/cond/branch_0_fun/restore/pallas_call | solution.py:240
  220.8 6.1 %restore.29.moved_ref = f32[32,288,768]{2,1,0:T(8,128)} custom-call(s32[9]{0:T(128)S(1)} %select_reduce_fusion.offset_ref, s32[1]{0:T(128)} %bitcast.2.end_ref, f32[32,288,768]{2,1,0:T(8,128)} %restore.28.moved_ref, f32[88,2,8,128]{3,2,1,0:T(8,128)S(1)} %collective-permute-done.14.arrived_ref, ...), custom_call_target="tpu_custom_call", output_to_operand_aliasing={{}: (2, {})} | custom-call | flops 962592768 | bytes 7077888 | tf_op jit(solution)/shard_map/cond/branch_0_fun/restore/pallas_call | solution.py:240
  226.9 6.1 %restore.30.moved_ref = f32[32,288,768]{2,1,0:T(8,128)} custom-call(s32[9]{0:T(128)S(1)} %select_reduce_fusion.offset_ref, s32[1]{0:T(128)} %bitcast.2.end_ref, f32[32,288,768]{2,1,0:T(8,128)} %restore.29.moved_ref, f32[88,2,8,128]{3,2,1,0:T(8,128)S(1)} %collective-permute-done.16.arrived_ref, ...), custom_call_target="tpu_custom_call", output_to_operand_aliasing={{}: (2, {})} | custom-call | flops 962592768 | bytes 7077888 | tf_op jit(solution)/shard_map/cond/branch_0_fun/restore/pallas_call | solution.py:240
  233.1 6.1 %restore.31 = f32[32,288,768]{2,1,0:T(8,128)} custom-call(s32[9]{0:T(128)S(1)} %select_reduce_fusion.offset_ref, s32[1]{0:T(128)} %bitcast.2.end_ref, f32[32,288,768]{2,1,0:T(8,128)} %restore.30.moved_ref, f32[88,2,8,128]{3,2,1,0:T(8,128)S(1)} %collective-permute-done.17.arrived_ref, ...), custom_call_target="tpu_custom_call", output_to_operand_aliasing={{}: (2, {})} | custom-call | flops 962592768 | bytes 7077888 | tf_op jit(solution)/shard_map/cond/branch_0_fun/restore/pallas_call | solution.py:240
  (108 shorter events, 10.8 us)
Async XLA Ops:
  0.0 32.4 %collective-permute-start.56 = (f32[2,144,768]{2,1,0:T(8,128)}, f32[2,144,768]{2,1,0:T(8,128)}, u32[]{:S(2)}, u32[]{:S(2)}) collective-permute-start(f32[2,144,768]{2,1,0:T(8,128)} %bitcast.70), channel_id=1, source_target_pairs={{0,2},{2,0},{1,3},{3,1},{4,6},{6,4},{5,7},{7,5},{8,10},{10,8},{9,1... | collective-permute-start | bytes 2654216 | tf_op jit(solution)/shard_map/ppermute | solution.py:375
  3.7 31.3 %collective-permute-start.55 = (f32[1,768]{1,0:T(1,128)S(1)}, f32[1,768]{1,0:T(1,128)S(1)}, u32[]{:S(2)}, u32[]{:S(2)}) collective-permute-start(f32[1,768]{1,0:T(1,128)S(1)} %slice_bitcast_fusion), channel_id=1, source_target_pairs={{4,2},{8,6},{12,10},{0,14},{5,3},{9,7},{13,11},{1,15},{20,18},{24,... | collective-permute-start | bytes 9224 | tf_op jit(solution)/shard_map/ppermute | solution.py:378
  10.7 10.7 %collective-permute-start.58 = (f32[32,2,768]{2,1,0:T(2,128)S(1)}, f32[32,2,768]{2,1,0:T(2,128)S(1)}, u32[]{:S(2)}, u32[]{:S(2)}) collective-permute-start(f32[32,2,768]{2,1,0:T(2,128)S(1)} %get-tuple-element.980), channel_id=1, source_target_pairs={{0,4},{4,8},{8,12},{12,0},{1,5},{5,9},{9,13},{13,1},{2,6},{6,10},{... | collective-permute-start | bytes 589832 | tf_op jit(solution)/shard_map/ppermute | solution.py:315
  10.8 10.7 %collective-permute-start.59 = (f32[32,2,768]{2,1,0:T(2,128)S(1)}, f32[32,2,768]{2,1,0:T(2,128)S(1)}, u32[]{:S(2)}, u32[]{:S(2)}) collective-permute-start(f32[32,2,768]{2,1,0:T(2,128)S(1)} %get-tuple-element.981), channel_id=1, source_target_pairs={{4,0},{8,4},{12,8},{0,12},{5,1},{9,5},{13,9},{1,13},{6,2},{10,6},{... | collective-permute-start | bytes 589832 | tf_op jit(solution)/shard_map/ppermute | solution.py:316
  14.6 17.7 %collective-permute-start.57 = (f32[144,768]{1,0:T(8,128)}, f32[144,768]{1,0:T(8,128)S(1)}, u32[]{:S(2)}, u32[]{:S(2)}) collective-permute-start(f32[144,768]{1,0:T(8,128)} %bitcast.72), channel_id=1, source_target_pairs={{0,2},{2,0},{1,3},{3,1},{4,6},{6,4},{5,7},{7,5},{8,10},{10,8},{9,1... | collective-permute-start | bytes 1327112 | tf_op jit(solution)/shard_map/ppermute | solution.py:375
  18.2 14.1 %copy-start.28 = (f32[1,144,768]{2,1,0:T(8,128)S(1)}, f32[1,144,768]{2,1,0:T(8,128)}, u32[]{:S(2)}) copy-start(f32[1,144,768]{2,1,0:T(8,128)} %param.14) | copy-start | bytes 1327108
  21.4 13.6 %collective-permute-start.54 = (f32[1,768]{1,0:T(1,128)S(1)}, f32[1,768]{1,0:T(1,128)S(1)}, u32[]{:S(2)}, u32[]{:S(2)}) collective-permute-start(f32[1,768]{1,0:T(1,128)S(1)} %slice_bitcast_fusion), channel_id=1, source_target_pairs={{4,0},{8,4},{12,8},{0,12},{5,1},{9,5},{13,9},{1,13},{6,2},{10,6},{... | collective-permute-start | bytes 9224 | tf_op jit(solution)/shard_map/ppermute | solution.py:377
  32.3 1.2 copy-start.27
  34.8 2.0 copy-start.10
  34.8 2.0 copy-start.29
  34.9 2.0 copy-start.30
  37.4 16.5 %copy-start.11 = (bf16[8,288,768]{2,1,0:T(8,128)(2,1)}, bf16[8,288,768]{2,1,0:T(8,128)(2,1)S(1)}, u32[]{:S(2)}) copy-start(bf16[8,288,768]{2,1,0:T(8,128)(2,1)S(1)} %get-tuple-element.944.source_ref) | copy-start | bytes 10616836 | tf_op jit(solution)/shard_map/cond
  40.5 13.4 %copy-start = (f32[9,288,768]{2,1,0:T(8,128)}, f32[9,288,768]{2,1,0:T(8,128)S(1)}, u32[]{:S(2)}) copy-start(f32[9,288,768]{2,1,0:T(8,128)S(1)} %stencil_weights.3.weight_ref) | copy-start | bytes 23887876 | tf_op jit(solution)/shard_map/cond
  52.0 17.4 %collective-permute-start = (f32[88,2,8,128]{3,2,1,0:T(8,128)S(1)}, f32[88,2,8,128]{3,2,1,0:T(8,128)S(1)}, u32[]{:S(2)}, u32[]{:S(2)}) collective-permute-start(f32[88,2,8,128]{3,2,1,0:T(8,128)S(1)} %get-tuple-element.677), channel_id=1, source_target_pairs={{0,4},{4,0},{8,12},{12,8},{1,5},{5,1},{9,13},{13,9},{2,6},{6,2},{1... | collective-permute-start | bytes 2162696 | tf_op jit(solution)/shard_map/cond/branch_0_fun/ppermute | solution.py:300
  63.9 10.2 %copy-start.7 = (f32[32,288,768]{2,1,0:T(8,128)}, f32[32,288,768]{2,1,0:T(8,128)S(1)}, u32[]{:S(2)}) copy-start(f32[32,288,768]{2,1,0:T(8,128)S(1)} %get-tuple-element.679.rest_0_) | copy-start | bytes 84934656 | tf_op jit(solution)/shard_map/cond
  74.0 17.3 %collective-permute-start.2 = (f32[88,2,8,128]{3,2,1,0:T(8,128)S(1)}, f32[88,2,8,128]{3,2,1,0:T(8,128)}, u32[]{:S(2)}, u32[]{:S(2)}) collective-permute-start(f32[88,2,8,128]{3,2,1,0:T(8,128)S(1)} %get-tuple-element.684), channel_id=1, source_target_pairs={{0,4},{4,0},{8,12},{12,8},{1,5},{5,1},{9,13},{13,9},{2,6},{6,2},{1... | collective-permute-start | bytes 2162696 | tf_op jit(solution)/shard_map/cond/branch_0_fun/ppermute | solution.py:300
  74.2 18.5 %collective-permute-start.1 = (f32[88,2,8,128]{3,2,1,0:T(8,128)}, f32[88,2,8,128]{3,2,1,0:T(8,128)}, u32[]{:S(2)}, u32[]{:S(2)}) collective-permute-start(f32[88,2,8,128]{3,2,1,0:T(8,128)} %add.199), channel_id=1, source_target_pairs={{4,8},{8,4},{5,9},{9,5},{6,10},{10,6},{7,11},{11,7},{20,24},{24,20... | collective-permute-start | bytes 2162696 | tf_op jit(solution)/shard_map/cond/branch_0_fun/ppermute | solution.py:301
  76.0 3.3 %copy-start.1 = (f32[9,288,768]{2,1,0:T(8,128)S(1)}, f32[9,288,768]{2,1,0:T(8,128)}, u32[]{:S(2)}) copy-start(f32[9,288,768]{2,1,0:T(8,128)} %copy-done) | copy-start | bytes 23887876 | tf_op jit(solution)/shard_map/cond
  91.4 7.7 %copy-start.12 = (bf16[8,288,768]{2,1,0:T(8,128)(2,1)S(1)}, bf16[8,288,768]{2,1,0:T(8,128)(2,1)}, u32[]{:S(2)}) copy-start(bf16[8,288,768]{2,1,0:T(8,128)(2,1)} %copy-done.11) | copy-start | bytes 10616836 | tf_op jit(solution)/shard_map/cond
  92.8 25.1 %slice-start = ((s8[28311552]{0:T(1024)(128)(4,1)}), s8[4194304]{0:T(1024)(128)(4,1)S(1)}, s32[]{:S(2)}) async-start(s8[28311552]{0:T(1024)(128)(4,1)} %bitcast.64), calls=%async_computation | async-start | bytes 8388608 | tf_op jit(solution)/shard_map/cond
  94.4 23.5 %slice-start.1 = ((s8[28311552]{0:T(1024)(128)(4,1)}), s8[4194304]{0:T(1024)(128)(4,1)S(1)}, s32[]{:S(2)}) async-start(s8[28311552]{0:T(1024)(128)(4,1)} %bitcast.64), calls=%async_computation.1 | async-start | bytes 8388608 | tf_op jit(solution)/shard_map/cond
  94.4 23.5 %slice-start.2 = ((s8[28311552]{0:T(1024)(128)(4,1)}), s8[4194304]{0:T(1024)(128)(4,1)S(1)}, s32[]{:S(2)}) async-start(s8[28311552]{0:T(1024)(128)(4,1)} %bitcast.64), calls=%async_computation.2 | async-start | bytes 8388608 | tf_op jit(solution)/shard_map/cond
  94.4 23.5 %slice-start.3 = ((s8[28311552]{0:T(1024)(128)(4,1)}), s8[4194304]{0:T(1024)(128)(4,1)S(1)}, s32[]{:S(2)}) async-start(s8[28311552]{0:T(1024)(128)(4,1)} %bitcast.64), calls=%async_computation.3 | async-start | bytes 8388608 | tf_op jit(solution)/shard_map/cond
  94.4 23.5 %slice-start.4 = ((s8[28311552]{0:T(1024)(128)(4,1)}), s8[4194304]{0:T(1024)(128)(4,1)S(1)}, s32[]{:S(2)}) async-start(s8[28311552]{0:T(1024)(128)(4,1)} %bitcast.64), calls=%async_computation.4 | async-start | bytes 8388608 | tf_op jit(solution)/shard_map/cond
  94.4 23.5 %slice-start.5 = ((s8[28311552]{0:T(1024)(128)(4,1)}), s8[4194304]{0:T(1024)(128)(4,1)S(1)}, s32[]{:S(2)}) async-start(s8[28311552]{0:T(1024)(128)(4,1)} %bitcast.64), calls=%async_computation.5 | async-start | bytes 8388608 | tf_op jit(solution)/shard_map/cond
  94.4 23.5 %slice-start.6 = ((s8[28311552]{0:T(1024)(128)(4,1)}), s8[3145728]{0:T(1024)(128)(4,1)S(1)}, s32[]{:S(2)}) async-start(s8[28311552]{0:T(1024)(128)(4,1)} %bitcast.64), calls=%async_computation.6 | async-start | bytes 6291456 | tf_op jit(solution)/shard_map/cond
  94.5 18.3 %collective-permute-start.4 = (f32[88,2,8,128]{3,2,1,0:T(8,128)S(1)}, f32[88,2,8,128]{3,2,1,0:T(8,128)S(1)}, u32[]{:S(2)}, u32[]{:S(2)}) collective-permute-start(f32[88,2,8,128]{3,2,1,0:T(8,128)S(1)} %add_select_fusion.5.held_ref), channel_id=1, source_target_pairs={{0,4},{4,0},{8,12},{12,8},{1,5},{5,1},{9,13},{13,9},{2,6},{6,2},{1... | collective-permute-start | bytes 2162696 | tf_op jit(solution)/shard_map/cond/branch_0_fun/ppermute | solution.py:300
  98.3 14.5 %collective-permute-start.3 = (f32[88,2,8,128]{3,2,1,0:T(8,128)S(1)}, f32[88,2,8,128]{3,2,1,0:T(8,128)S(1)}, u32[]{:S(2)}, u32[]{:S(2)}) collective-permute-start(f32[88,2,8,128]{3,2,1,0:T(8,128)S(1)} %add.201), channel_id=1, source_target_pairs={{4,8},{8,4},{5,9},{9,5},{6,10},{10,6},{7,11},{11,7},{20,24},{24,20... | collective-permute-start | bytes 2162696 | tf_op jit(solution)/shard_map/cond/branch_0_fun/ppermute | solution.py:301
  113.0 17.5 %collective-permute-start.6 = (f32[88,2,8,128]{3,2,1,0:T(8,128)S(1)}, f32[88,2,8,128]{3,2,1,0:T(8,128)S(1)}, u32[]{:S(2)}, u32[]{:S(2)}) collective-permute-start(f32[88,2,8,128]{3,2,1,0:T(8,128)S(1)} %add_select_fusion.4.held_ref), channel_id=1, source_target_pairs={{0,4},{4,0},{8,12},{12,8},{1,5},{5,1},{9,13},{13,9},{2,6},{6,2},{1... | collective-permute-start | bytes 2162696 | tf_op jit(solution)/shard_map/cond/branch_0_fun/ppermute | solution.py:300
  117.0 13.6 %collective-permute-start.5 = (f32[88,2,8,128]{3,2,1,0:T(8,128)S(1)}, f32[88,2,8,128]{3,2,1,0:T(8,128)S(1)}, u32[]{:S(2)}, u32[]{:S(2)}) collective-permute-start(f32[88,2,8,128]{3,2,1,0:T(8,128)S(1)} %add.203), channel_id=1, source_target_pairs={{4,8},{8,4},{5,9},{9,5},{6,10},{10,6},{7,11},{11,7},{20,24},{24,20... | collective-permute-start | bytes 2162696 | tf_op jit(solution)/shard_map/cond/branch_0_fun/ppermute | solution.py:301
  130.7 16.2 %collective-permute-start.8 = (f32[88,2,8,128]{3,2,1,0:T(8,128)S(1)}, f32[88,2,8,128]{3,2,1,0:T(8,128)S(1)}, u32[]{:S(2)}, u32[]{:S(2)}) collective-permute-start(f32[88,2,8,128]{3,2,1,0:T(8,128)S(1)} %add_select_fusion.3.held_ref), channel_id=1, source_target_pairs={{0,4},{4,0},{8,12},{12,8},{1,5},{5,1},{9,13},{13,9},{2,6},{6,2},{1... | collective-permute-start | bytes 2162696 | tf_op jit(solution)/shard_map/cond/branch_0_fun/ppermute | solution.py:300
  134.3 12.7 %collective-permute-start.7 = (f32[88,2,8,128]{3,2,1,0:T(8,128)S(1)}, f32[88,2,8,128]{3,2,1,0:T(8,128)S(1)}, u32[]{:S(2)}, u32[]{:S(2)}) collective-permute-start(f32[88,2,8,128]{3,2,1,0:T(8,128)S(1)} %add.205), channel_id=1, source_target_pairs={{4,8},{8,4},{5,9},{9,5},{6,10},{10,6},{7,11},{11,7},{20,24},{24,20... | collective-permute-start | bytes 2162696 | tf_op jit(solution)/shard_map/cond/branch_0_fun/ppermute | solution.py:301
  146.9 4.8 %copy-start.13 = (bf16[8,288,768]{2,1,0:T(8,128)(2,1)S(1)}, bf16[8,288,768]{2,1,0:T(8,128)(2,1)}, u32[]{:S(2)}) copy-start(bf16[8,288,768]{2,1,0:T(8,128)(2,1)} %copy-done.11) | copy-start | bytes 10616836 | tf_op jit(solution)/shard_map/cond
  147.2 16.0 %collective-permute-start.10 = (f32[88,2,8,128]{3,2,1,0:T(8,128)S(1)}, f32[88,2,8,128]{3,2,1,0:T(8,128)S(1)}, u32[]{:S(2)}, u32[]{:S(2)}) collective-permute-start(f32[88,2,8,128]{3,2,1,0:T(8,128)S(1)} %add_select_fusion.2.held_ref), channel_id=1, source_target_pairs={{0,4},{4,0},{8,12},{12,8},{1,5},{5,1},{9,13},{13,9},{2,6},{6,2},{1... | collective-permute-start | bytes 2162696 | tf_op jit(solution)/shard_map/cond/branch_0_fun/ppermute | solution.py:300
  150.8 12.5 %collective-permute-start.9 = (f32[88,2,8,128]{3,2,1,0:T(8,128)S(1)}, f32[88,2,8,128]{3,2,1,0:T(8,128)S(1)}, u32[]{:S(2)}, u32[]{:S(2)}) collective-permute-start(f32[88,2,8,128]{3,2,1,0:T(8,128)S(1)} %add.207), channel_id=1, source_target_pairs={{4,8},{8,4},{5,9},{9,5},{6,10},{10,6},{7,11},{11,7},{20,24},{24,20... | collective-permute-start | bytes 2162696 | tf_op jit(solution)/shard_map/cond/branch_0_fun/ppermute | solution.py:301
  163.5 15.4 %collective-permute-start.12 = (f32[88,2,8,128]{3,2,1,0:T(8,128)S(1)}, f32[88,2,8,128]{3,2,1,0:T(8,128)S(1)}, u32[]{:S(2)}, u32[]{:S(2)}) collective-permute-start(f32[88,2,8,128]{3,2,1,0:T(8,128)S(1)} %add_select_fusion.1.held_ref), channel_id=1, source_target_pairs={{0,4},{4,0},{8,12},{12,8},{1,5},{5,1},{9,13},{13,9},{2,6},{6,2},{1... | collective-permute-start | bytes 2162696 | tf_op jit(solution)/shard_map/cond/branch_0_fun/ppermute | solution.py:300
  167.1 11.9 %collective-permute-start.11 = (f32[88,2,8,128]{3,2,1,0:T(8,128)S(1)}, f32[88,2,8,128]{3,2,1,0:T(8,128)S(1)}, u32[]{:S(2)}, u32[]{:S(2)}) collective-permute-start(f32[88,2,8,128]{3,2,1,0:T(8,128)S(1)} %add.209), channel_id=1, source_target_pairs={{4,8},{8,4},{5,9},{9,5},{6,10},{10,6},{7,11},{11,7},{20,24},{24,20... | collective-permute-start | bytes 2162696 | tf_op jit(solution)/shard_map/cond/branch_0_fun/ppermute | solution.py:301
  179.0 8.1 %copy-start.21 = (bf16[576,576]{1,0:T(8,128)(2,1)S(1)}, bf16[576,576]{1,0:T(8,128)(2,1)}, u32[]{:S(2)}) copy-start(bf16[576,576]{1,0:T(8,128)(2,1)} %get-tuple-element.718.both_ref) | copy-start | bytes 1990660 | tf_op jit(solution)/shard_map/cond
  179.0 8.0 %copy-start.24 = (bf16[256,768]{1,0:T(8,128)(2,1)S(1)}, bf16[256,768]{1,0:T(8,128)(2,1)}, u32[]{:S(2)}) copy-start(bf16[256,768]{1,0:T(8,128)(2,1)} %get-tuple-element.720.put_ref) | copy-start | bytes 1179652 | tf_op jit(solution)/shard_map/cond
  179.1 26.2 %collective-permute-start.13 = (f32[88,2,8,128]{3,2,1,0:T(8,128)S(1)}, f32[88,2,8,128]{3,2,1,0:T(8,128)S(1)}, u32[]{:S(2)}, u32[]{:S(2)}) collective-permute-start(f32[88,2,8,128]{3,2,1,0:T(8,128)S(1)} %add.211), channel_id=1, source_target_pairs={{4,8},{8,4},{5,9},{9,5},{6,10},{10,6},{7,11},{11,7},{20,24},{24,20... | collective-permute-start | bytes 2162696 | tf_op jit(solution)/shard_map/cond/branch_0_fun/ppermute | solution.py:301
  180.4 25.0 %collective-permute-start.14 = (f32[88,2,8,128]{3,2,1,0:T(8,128)S(1)}, f32[88,2,8,128]{3,2,1,0:T(8,128)S(1)}, u32[]{:S(2)}, u32[]{:S(2)}) collective-permute-start(f32[88,2,8,128]{3,2,1,0:T(8,128)S(1)} %add_select_fusion.held_ref), channel_id=1, source_target_pairs={{0,4},{4,0},{8,12},{12,8},{1,5},{5,1},{9,13},{13,9},{2,6},{6,2},{1... | collective-permute-start | bytes 2162696 | tf_op jit(solution)/shard_map/cond/branch_0_fun/ppermute | solution.py:300
  205.6 15.1 %collective-permute-start.15 = (f32[88,2,8,128]{3,2,1,0:T(8,128)S(1)}, f32[88,2,8,128]{3,2,1,0:T(8,128)S(1)}, u32[]{:S(2)}, u32[]{:S(2)}) collective-permute-start(f32[88,2,8,128]{3,2,1,0:T(8,128)S(1)} %add.213), channel_id=1, source_target_pairs={{4,8},{8,4},{5,9},{9,5},{6,10},{10,6},{7,11},{11,7},{20,24},{24,20... | collective-permute-start | bytes 2162696 | tf_op jit(solution)/shard_map/cond/branch_0_fun/ppermute | solution.py:301
  206.3 20.6 %collective-permute-start.16 = (f32[88,2,8,128]{3,2,1,0:T(8,128)S(1)}, f32[88,2,8,128]{3,2,1,0:T(8,128)S(1)}, u32[]{:S(2)}, u32[]{:S(2)}) collective-permute-start(f32[88,2,8,128]{3,2,1,0:T(8,128)S(1)} %add.212.held_ref), channel_id=1, source_target_pairs={{0,4},{4,0},{8,12},{12,8},{1,5},{5,1},{9,13},{13,9},{2,6},{6,2},{1... | collective-permute-start | bytes 2162696 | tf_op jit(solution)/shard_map/cond/branch_0_fun/ppermute | solution.py:300
  220.7 12.4 %collective-permute-start.17 = (f32[88,2,8,128]{3,2,1,0:T(8,128)S(1)}, f32[88,2,8,128]{3,2,1,0:T(8,128)S(1)}, u32[]{:S(2)}, u32[]{:S(2)}) collective-permute-start(f32[88,2,8,128]{3,2,1,0:T(8,128)S(1)} %add.214.held_ref), channel_id=1, source_target_pairs={{0,4},{4,0},{8,12},{12,8},{1,5},{5,1},{9,13},{13,9},{2,6},{6,2},{1... | collective-permute-start | bytes 2162696 | tf_op jit(solution)/shard_map/cond/branch_0_fun/ppermute | solution.py:300

commit v2 on v1

--- a/solution.py
+++ b/solution.py
@@ -140,29 +140,37 @@
             out_ref[jnp.minimum(offset_ref[block] + group, cap - 1), 0] = tile
 
 
-def inverse_kernel(
-    cap, offset_ref, end_ref, moved_ref, arrived_ref, held_ref, keep_ref, high_ref, both_ref, flip_ref, put_ref, *rest
-):
-    out_ref, spectrum = rest[-2:]
+def inverse_kernel(cap, pairs, many, offset_ref, end_ref, moved_ref, *rest):
+    packed_refs = rest[: 2 * many]
+    keep_ref, high_ref, both_ref, flip_ref, put_ref, out_ref, spectrum = rest[2 * many :]
     columns = high_ref.shape[1]
     left = lax.broadcasted_iota(jnp.int32, (GROUP, LANES), 1) < 2 * WAVES
     end = lax.broadcasted_iota(jnp.int32, (GROUP, LANES), 0) < GROUP * end_ref[0]
     blocks = columns // (2 * WAVES)
 
-    def load(block, group):
-        at = jnp.minimum(offset_ref[block] + group, cap - 1)
-        return jnp.where(end, arrived_ref[at, 0], held_ref[at, 0])
-
-    for group in range(FROWS // GROUP):
-        for pair in range((blocks + 1) // 2):
-            even = load(2 * pair, group)
-            odd = load(2 * pair + 1, group) if 2 * pair + 1 < blocks else even
-            where = slice(GROUP * group, GROUP * (group + 1)), slice(LANES * pair, LANES * (pair + 1))
-            keep = keep_ref[where]
-            a = jnp.where(left, even, pltpu.roll(odd, 2 * WAVES, 1))
-            b = jnp.where(left, pltpu.roll(even, 2 * WAVES, 1), odd)
-            spectrum[(0,) + where] = jnp.where(keep != 0.0, a * keep, 0.0)
-            spectrum[(1,) + where] = jnp.where(keep != 0.0, b * keep, 0.0)
+    def unpack(arrived_ref, held_ref):
+        def load(block, group):
+            at = jnp.minimum(offset_ref[block] + group, cap - 1)
+            return jnp.where(end, arrived_ref[at, 0], held_ref[at, 0])
+
+        for group in range(FROWS // GROUP):
+            for pair in range((blocks + 1) // 2):
+                even = load(2 * pair, group)
+                odd = load(2 * pair + 1, group) if 2 * pair + 1 < blocks else even
+                where = slice(GROUP * group, GROUP * (group + 1)), slice(LANES * pair, LANES * (pair + 1))
+                keep = keep_ref[where]
+                a = jnp.where(left, even, pltpu.roll(odd, 2 * WAVES, 1))
+                b = jnp.where(left, pltpu.roll(even, 2 * WAVES, 1), odd)
+                spectrum[(0,) + where] = jnp.where(keep != 0.0, a * keep, 0.0)
+                spectrum[(1,) + where] = jnp.where(keep != 0.0, b * keep, 0.0)
+
+    if many == 1:
+        unpack(*packed_refs)
+    else:
+        for index in range(many):
+            pl.when(pl.program_id(0) // pairs == index)(
+                functools.partial(unpack, packed_refs[2 * index], packed_refs[2 * index + 1])
+            )
     length = high_ref.shape[0]
     s_high, s_low = halves(spectrum[...].reshape(2 * FROWS, -1)[:, :columns])
     last = ((1,), (1,))
@@ -219,33 +227,33 @@
     )(*operands)
 
 
-def inverse(base, size, cap, offsets, end, out, arrived, held, keep, high, both, flip, put):
+def inverse(base, size, cap, offsets, end, out, packed, keep, high, both, flip, put):
     tags, length, lats = out.shape
-    pairs = size // 2
+    pairs, many = size // 2, len(packed)
     constants = [keep, high, both, flip, put]
-    specs = [
-        pl.BlockSpec((2, length, lats), lambda p, *_: (base // 2 + p, 0, 0)),
-        pl.BlockSpec((cap, 1, GROUP, LANES), lambda p, *_: (0, p, 0, 0)),
-        pl.BlockSpec((cap, 1, GROUP, LANES), lambda p, *_: (0, p, 0, 0)),
-    ] + [RESIDENT] * len(constants)
-    operands = [offsets, end, out, arrived, held] + constants
+    specs = [pl.BlockSpec((2, length, lats), lambda p, *_: (base // 2 + p, 0, 0))]
+    for index in range(many):
+        at = lambda p, *_, start=index * pairs: (0, jnp.clip(p - start, 0, pairs - 1), 0, 0)
+        specs += [pl.BlockSpec((cap, 1, GROUP, LANES), at)] * 2
     grid_spec = pltpu.PrefetchScalarGridSpec(
         num_scalar_prefetch=2,
-        grid=(pairs,),
-        in_specs=specs,
+        grid=(many * pairs,),
+        in_specs=specs + [RESIDENT] * len(constants),
         out_specs=pl.BlockSpec((2, length, lats), lambda p, *_: (base // 2 + p, 0, 0)),
         scratch_shapes=[pltpu.VMEM((2, FROWS, keep.shape[1]), jnp.float32)],
     )
-    flops = size * 2 * length * (2 * lats * FROWS + 3 * high.shape[1] * FROWS)
+    flops = many * size * 2 * length * (2 * lats * FROWS + 3 * high.shape[1] * FROWS)
     return pl.pallas_call(
-        functools.partial(inverse_kernel, cap),
+        functools.partial(inverse_kernel, cap, pairs, many),
         grid_spec=grid_spec,
         out_shape=jax.ShapeDtypeStruct(out.shape, jnp.float32),
         input_output_aliases={2: 0},
         compiler_params=pltpu.CompilerParams(vmem_limit_bytes=VMEM),
-        cost_estimate=pl.CostEstimate(flops=flops, bytes_accessed=2 * size * length * lats * 4, transcendentals=0),
+        cost_estimate=pl.CostEstimate(
+            flops=flops, bytes_accessed=2 * many * size * length * lats * 4, transcendentals=0
+        ),
         name="restore",
-    )(*operands)
+    )(offsets, end, out, *[array for pair in packed for array in pair], *constants)
 
 
 def sum_over_lon(packed, count, place):
@@ -267,7 +275,7 @@
     for chunk in range(chunks):
         out, packed = forward_at(chunk, out, offsets)
         total = sum_over_lon(packed, count, place)
-        out = inverse_at(chunk, out, total, total, offsets)
+        out = inverse_at(chunk, out, [(total, total)], offsets)
     return out
 
 
@@ -302,10 +310,10 @@
         if t + 1 < chunks:
             out, own[t + 1] = forward_at(t + 1, out, token)
         quota = chunks if t == chunks + 2 else -(-(chunks - 1 - done) // (chunks + 2 - t)) if t >= chunks - 1 else 0
-        while quota and done in back:
-            out = inverse_at(done, out, *back[done], token)
-            done += 1
-            quota -= 1
+        ready = [back[i] for i in range(done, min(done + quota, chunks)) if i in back]
+        if ready:
+            out = inverse_at(done, out, ready, token)
+            done += len(ready)
     return out
 
 
@@ -397,10 +405,8 @@
                 sign, high, low, out,
             )
 
-        def inverse_at(chunk, out, arrived, held, offsets):
-            return inverse(
-                bases[chunk], sizes[chunk], cap, offsets, is_end, out, arrived, held, keep_, high, both_, flip_, put_
-            )
+        def inverse_at(chunk, out, packed, offsets):
+            return inverse(bases[chunk], CHUNK, cap, offsets, is_end, out, packed, keep_, high, both_, flip_, put_)
 
         pipeline = stepped_pipeline if count == 4 else plain_pipeline
         return pipeline(len(sizes), forward_at, inverse_at, place, count, offsets)

time: 251 us -> 250 us (level)
  starting transfers between devices: 49.6 us -> 47 us
    pallas_call x8, Pallas kernels: 90.8 us -> 98.8 us  [forward(): pl.pallas_call(functools.partial(forward_kernel, cap, first=base), grid_s...]
    pallas_call x8 -> x4, Pallas kernels: 48.9 us -> 41.4 us  [inverse(): pl.pallas_call(functools.partial(inverse_kernel, cap, pairs, many), grid_...]
    ppermute x10, starting transfers between devices: 29.5 us -> 26.9 us  [stepped_pipeline(): swapped = None if sent is None else lax.ppermute(sent, 'lon', swap)]
  transfers between devices with their start and end apart: 24 -> 24, of which waited for: 7 -> 5; matrix products, arithmetic and copies ran while one was open for 5% -> 5% of each run, Pallas kernels for 49% -> 49%
where the time goes in v2:
time: 250 us; the launch traced here: 247 us
  Pallas kernels  143 us (57%)
  starting transfers between devices  47 us (19%)
  waiting for transfers between devices  19.6 us (8%)
  local copies, waits for them, and re-layouts  13.6 us (5%)
  other arithmetic  12.9 us (5%)
  loops' own time  7.85 us (3%)
  between operations  2.89 us (1%)
    pallas_call x8, Pallas kernels, forward(): pl.pallas_call(functools.partial(forward_kernel, cap, first=base), grid_s...  98.8 us
    pallas_call x4, Pallas kernels, inverse(): pl.pallas_call(functools.partial(inverse_kernel, cap, pairs, many), grid_...  41.4 us
    ppermute x10, starting transfers between devices, stepped_pipeline(): swapped = None if sent is None else lax.ppermute(sent, 'lon', swap)  26.9 us
    ppermute x1, waiting for transfers between devices, body(): lax.ppermute(thickness, 'tag', cross)  10.6 us
    ppermute x10, waiting for transfers between devices, stepped_pipeline(): swapped = None if sent is None else lax.ppermute(sent, 'lon', swap)  8.94 us
    another operation x1, loops' own time, body(): out = lax.switch(index, [functools.partial(run, cap) for cap in caps])  7.85 us
    ppermute x8, starting transfers between devices, stepped_pipeline(): crossed = None if pair_sum is None else lax.ppermute(pair_sum, 'lon', cross)  7.78 us
    cond x30, local copies, waits for them, and re-layouts  7.22 us
  transfers between devices with their start and end apart: 24, of which 5 were waited for; matrix products, arithmetic and copies ran while one was open for 5% of the time, Pallas kernels for 49%

profile of v2, /device:TPU:0, one launch (start us, length us, event | category | flops | bytes accessed | tf_op | source)
XLA Modules:
  0.0 246.6 jit_solution(8694363571643557755)
XLA Ops:
  0.0 2.9 %collective-permute-start.56 = (f32[2,144,768]{2,1,0:T(8,128)}, f32[2,144,768]{2,1,0:T(8,128)}, u32[]{:S(2)}, u32[]{:S(2)}) collective-permute-start(f32[2,144,768]{2,1,0:T(8,128)} %bitcast.70), channel_id=1, source_target_pairs={{0,2},{2,0},{1,3},{3,1},{4,6},{6,4},{5,7},{7,5},{8,10},{10,8},{9,1... | collective-permute-start | bytes 2654216 | tf_op jit(solution)/shard_map/ppermute | solution.py:383
  3.7 5.5 %collective-permute-start.55 = (f32[1,768]{1,0:T(1,128)S(1)}, f32[1,768]{1,0:T(1,128)S(1)}, u32[]{:S(2)}, u32[]{:S(2)}) collective-permute-start(f32[1,768]{1,0:T(1,128)S(1)} %slice_bitcast_fusion), channel_id=1, source_target_pairs={{4,2},{8,6},{12,10},{0,14},{5,3},{9,7},{13,11},{1,15},{20,18},{24,... | collective-permute-start | bytes 9224 | tf_op jit(solution)/shard_map/ppermute | solution.py:386
  9.2 1.5 fusion.26
  10.8 3.8 %collective-permute-start.59 = (f32[32,2,768]{2,1,0:T(2,128)S(1)}, f32[32,2,768]{2,1,0:T(2,128)S(1)}, u32[]{:S(2)}, u32[]{:S(2)}) collective-permute-start(f32[32,2,768]{2,1,0:T(2,128)S(1)} %get-tuple-element.981), channel_id=1, source_target_pairs={{4,0},{8,4},{12,8},{0,12},{5,1},{9,5},{13,9},{1,13},{6,2},{10,6},{... | collective-permute-start | bytes 589832 | tf_op jit(solution)/shard_map/ppermute | solution.py:324
  17.0 1.2 constant_dynamic-slice_fusion
  18.2 0.9 pad_maximum_fusion.2
  20.4 0.8 add_convert_fusion
  21.7 10.6 %collective-permute-done.57 = f32[144,768]{1,0:T(8,128)S(1)} collective-permute-done((f32[144,768]{1,0:T(8,128)}, f32[144,768]{1,0:T(8,128)S(1)}, u32[]{:S(2)}, u32[]{:S(2)}) %collective-permute-start.57) | collective-permute-done | bytes 442400 | tf_op jit(solution)/shard_map/ppermute | solution.py:383
  32.4 1.1 copy-done.27
  33.5 1.3 broadcast_select_fusion.4
  35.0 1.8 copy-done.10
  36.8 208.3 %conditional.1 = (f32[32,1,288,768]{3,2,1,0:T(8,128)}) conditional(s32[]{:T(128)} %clamp.3, (s32[9,9]{1,0:T(8,128)S(1)}, s32[9,9]{1,0:T(8,128)S(1)}, s32[9]{0:T(128)S(1)}, (), s32[]{:T(128)}, /*index=5*/s32[]{:T(128)}, s32[]{:T(128)}, pred[]{:T(512)}, f32[1,768]{1,0:T(1,128)S(1)}, f32[1,768]{1,0:T(1,128)S(1)}, ...), branch_computations={%region_4.7_spmd, %region_7.10_spmd, %region_10.13_spmd} | conditional | flops 15421826048 | bytes 699659392 | solution.py:419
  37.6 2.6 %stencil_weights.3.weight_ref = f32[9,288,768]{2,1,0:T(8,128)S(1)} custom-call(f32[2,288,768]{2,1,0:T(8,128)S(1)} %get-tuple-element.646.fields_ref, f32[288,768]{1,0:T(8,128)S(1)} %get-tuple-element.647.thick_ref, f32[1,768]{1,0:T(1,128)S(1)} %broadcast_select_fusion.end_ref), custom_call_target="tpu_custom_call" | custom-call | flops 13271040 | bytes 10616832 | tf_op jit(solution)/shard_map/cond/branch_0_fun/stencil_weights/pallas_call | solution.py:74
  40.3 12.4 %step_and_transform.24 = (f32[32,288,768]{2,1,0:T(8,128)S(1)}, f32[88,2,8,128]{3,2,1,0:T(8,128)S(1)}) custom-call(s32[9]{0:T(128)S(1)} %select_reduce_fusion.offset_ref, s32[32]{0:T(128)S(1)} %get-tuple-element.941.region_ref, f32[32,288,768]{2,1,0:T(8,128)} %get-tuple-element.645.q_ref, f32[32,4,768]{2,1,0:T(4,128)S(1)} %get-tuple-element.664.edge_ref, ...), custom_call_target="tpu_custom_call" | custom-call | flops 962592768 | bytes 17694720 | tf_op jit(solution)/shard_map/cond/branch_0_fun/step_and_transform/pallas_call | solution.py:216
  52.7 1.9 collective-permute-start
  54.6 11.0 %step_and_transform.25 = (f32[32,288,768]{2,1,0:T(8,128)S(1)}, f32[88,2,8,128]{3,2,1,0:T(8,128)S(1)}) custom-call(s32[9]{0:T(128)S(1)} %select_reduce_fusion.offset_ref, s32[32]{0:T(128)S(1)} %get-tuple-element.941.region_ref, f32[32,288,768]{2,1,0:T(8,128)} %get-tuple-element.645.q_ref, ...), custom_call_target="tpu_custom_call", output_to_operand_aliasing={{0}: (11, {})} | custom-call | flops 962592768 | bytes 17694720 | tf_op jit(solution)/shard_map/cond/branch_0_fun/step_and_transform/pallas_call | solution.py:216
  65.6 4.4 %collective-permute-done = f32[88,2,8,128]{3,2,1,0:T(8,128)S(1)} collective-permute-done((f32[88,2,8,128]{3,2,1,0:T(8,128)S(1)}, f32[88,2,8,128]{3,2,1,0:T(8,128)S(1)}, u32[]{:S(2)}, u32[]{:S(2)}) %collective-permute-start) | collective-permute-done | bytes 720928 | tf_op jit(solution)/shard_map/cond/branch_0_fun/ppermute | solution.py:308
  70.1 1.8 add.199
  71.9 3.9 %copy-done.7 = f32[32,288,768]{2,1,0:T(8,128)} copy-done((f32[32,288,768]{2,1,0:T(8,128)}, f32[32,288,768]{2,1,0:T(8,128)S(1)}, u32[]{:S(2)}) %copy-start.7) | copy-done | bytes 28311576 | tf_op jit(solution)/shard_map/cond
  76.0 1.8 collective-permute-start.1
  77.8 3.3 %copy-done.1 = f32[9,288,768]{2,1,0:T(8,128)S(1)} copy-done((f32[9,288,768]{2,1,0:T(8,128)S(1)}, f32[9,288,768]{2,1,0:T(8,128)}, u32[]{:S(2)}) %copy-start.1) | copy-done | bytes 7962648 | tf_op jit(solution)/shard_map/cond
  81.1 13.3 %step_and_transform.26 = (f32[32,288,768]{2,1,0:T(8,128)}, f32[88,2,8,128]{3,2,1,0:T(8,128)S(1)}) custom-call(s32[9]{0:T(128)S(1)} %select_reduce_fusion.offset_ref, s32[32]{0:T(128)S(1)} %get-tuple-element.941.region_ref, f32[32,288,768]{2,1,0:T(8,128)} %get-tuple-element.645.q_ref, ...), custom_call_target="tpu_custom_call", output_to_operand_aliasing={{0}: (11, {})} | custom-call | flops 962592768 | bytes 17694720 | tf_op jit(solution)/shard_map/cond/branch_0_fun/step_and_transform/pallas_call | solution.py:216
  94.3 1.4 add.201
  95.7 1.7 add_select_fusion.5.rest_1_
  97.5 3.8 %collective-permute-start.4 = (f32[88,2,8,128]{3,2,1,0:T(8,128)S(1)}, f32[88,2,8,128]{3,2,1,0:T(8,128)S(1)}, u32[]{:S(2)}, u32[]{:S(2)}) collective-permute-start(f32[88,2,8,128]{3,2,1,0:T(8,128)S(1)} %add_select_fusion.5.rest_1_), channel_id=1, source_target_pairs={{0,4},{4,0},{8,12},{12,8},{1,5},{5,1},{9,13},{13,9},{2,6},{6,2},{1... | collective-permute-start | bytes 2162696 | tf_op jit(solution)/shard_map/cond/branch_0_fun/ppermute | solution.py:308
  101.3 0.8 collective-permute-start.3
  102.1 13.0 %step_and_transform.27 = (f32[32,288,768]{2,1,0:T(8,128)}, f32[88,2,8,128]{3,2,1,0:T(8,128)S(1)}) custom-call(s32[9]{0:T(128)S(1)} %select_reduce_fusion.offset_ref, s32[32]{0:T(128)S(1)} %get-tuple-element.941.region_ref, f32[32,288,768]{2,1,0:T(8,128)} %get-tuple-element.645.q_ref, ...), custom_call_target="tpu_custom_call", output_to_operand_aliasing={{0}: (11, {})} | custom-call | flops 962592768 | bytes 17694720 | tf_op jit(solution)/shard_map/cond/branch_0_fun/step_and_transform/pallas_call | solution.py:216
  116.0 4.0 %collective-permute-start.6 = (f32[88,2,8,128]{3,2,1,0:T(8,128)S(1)}, f32[88,2,8,128]{3,2,1,0:T(8,128)S(1)}, u32[]{:S(2)}, u32[]{:S(2)}) collective-permute-start(f32[88,2,8,128]{3,2,1,0:T(8,128)S(1)} %add_select_fusion.4.rest_3_), channel_id=1, source_target_pairs={{0,4},{4,0},{8,12},{12,8},{1,5},{5,1},{9,13},{13,9},{2,6},{6,2},{1... | collective-permute-start | bytes 2162696 | tf_op jit(solution)/shard_map/cond/branch_0_fun/ppermute | solution.py:308
  120.0 1.2 collective-permute-start.5
  121.2 12.3 %step_and_transform.28 = (f32[32,288,768]{2,1,0:T(8,128)}, f32[88,2,8,128]{3,2,1,0:T(8,128)S(1)}) custom-call(s32[9]{0:T(128)S(1)} %select_reduce_fusion.offset_ref, s32[32]{0:T(128)S(1)} %get-tuple-element.941.region_ref, f32[32,288,768]{2,1,0:T(8,128)S(1)} %bitcast.65, ...), custom_call_target="tpu_custom_call", output_to_operand_aliasing={{0}: (11, {})} | custom-call | flops 962592768 | bytes 17694720 | tf_op jit(solution)/shard_map/cond/branch_0_fun/step_and_transform/pallas_call | solution.py:216
  133.8 3.5 %collective-permute-start.8 = (f32[88,2,8,128]{3,2,1,0:T(8,128)S(1)}, f32[88,2,8,128]{3,2,1,0:T(8,128)S(1)}, u32[]{:S(2)}, u32[]{:S(2)}) collective-permute-start(f32[88,2,8,128]{3,2,1,0:T(8,128)S(1)} %add_select_fusion.3.rest_5_), channel_id=1, source_target_pairs={{0,4},{4,0},{8,12},{12,8},{1,5},{5,1},{9,13},{13,9},{2,6},{6,2},{1... | collective-permute-start | bytes 2162696 | tf_op jit(solution)/shard_map/cond/branch_0_fun/ppermute | solution.py:308
  138.0 12.3 %step_and_transform.29 = (f32[32,288,768]{2,1,0:T(8,128)}, f32[88,2,8,128]{3,2,1,0:T(8,128)S(1)}) custom-call(s32[9]{0:T(128)S(1)} %select_reduce_fusion.offset_ref, s32[32]{0:T(128)S(1)} %get-tuple-element.941.region_ref, f32[32,288,768]{2,1,0:T(8,128)S(1)} %bitcast.65, ...), custom_call_target="tpu_custom_call", output_to_operand_aliasing={{0}: (11, {})} | custom-call | flops 962592768 | bytes 17694720 | tf_op jit(solution)/shard_map/cond/branch_0_fun/step_and_transform/pallas_call | solution.py:216
  150.6 3.1 %collective-permute-start.10 = (f32[88,2,8,128]{3,2,1,0:T(8,128)S(1)}, f32[88,2,8,128]{3,2,1,0:T(8,128)S(1)}, u32[]{:S(2)}, u32[]{:S(2)}) collective-permute-start(f32[88,2,8,128]{3,2,1,0:T(8,128)S(1)} %add_select_fusion.2.rest_1_), channel_id=1, source_target_pairs={{0,4},{4,0},{8,12},{12,8},{1,5},{5,1},{9,13},{13,9},{2,6},{6,2},{1... | collective-permute-start | bytes 2162696 | tf_op jit(solution)/shard_map/cond/branch_0_fun/ppermute | solution.py:308
  153.8 0.9 collective-permute-start.9
  154.7 12.2 %step_and_transform.30 = (f32[32,288,768]{2,1,0:T(8,128)}, f32[88,2,8,128]{3,2,1,0:T(8,128)S(1)}) custom-call(s32[9]{0:T(128)S(1)} %select_reduce_fusion.offset_ref, s32[32]{0:T(128)S(1)} %get-tuple-element.941.region_ref, f32[32,288,768]{2,1,0:T(8,128)} %get-tuple-element.645.q_ref, ...), custom_call_target="tpu_custom_call", output_to_operand_aliasing={{0}: (11, {})} | custom-call | flops 962592768 | bytes 17694720 | tf_op jit(solution)/shard_map/cond/branch_0_fun/step_and_transform/pallas_call | solution.py:216
  167.1 2.5 %collective-permute-start.12 = (f32[88,2,8,128]{3,2,1,0:T(8,128)S(1)}, f32[88,2,8,128]{3,2,1,0:T(8,128)S(1)}, u32[]{:S(2)}, u32[]{:S(2)}) collective-permute-start(f32[88,2,8,128]{3,2,1,0:T(8,128)S(1)} %add_select_fusion.1.rest_3_), channel_id=1, source_target_pairs={{0,4},{4,0},{8,12},{12,8},{1,5},{5,1},{9,13},{13,9},{2,6},{6,2},{1... | collective-permute-start | bytes 2162696 | tf_op jit(solution)/shard_map/cond/branch_0_fun/ppermute | solution.py:308
  170.3 12.2 %step_and_transform.31 = (f32[32,288,768]{2,1,0:T(8,128)}, f32[88,2,8,128]{3,2,1,0:T(8,128)S(1)}) custom-call(s32[9]{0:T(128)S(1)} %select_reduce_fusion.offset_ref, s32[32]{0:T(128)S(1)} %get-tuple-element.941.region_ref, f32[32,288,768]{2,1,0:T(8,128)} %get-tuple-element.645.q_ref, ...), custom_call_target="tpu_custom_call", output_to_operand_aliasing={{0}: (11, {})} | custom-call | flops 962592768 | bytes 17694720 | tf_op jit(solution)/shard_map/cond/branch_0_fun/step_and_transform/pallas_call | solution.py:216
  182.8 0.8 collective-permute-start.13
  183.6 4.7 %collective-permute-start.14 = (f32[88,2,8,128]{3,2,1,0:T(8,128)S(1)}, f32[88,2,8,128]{3,2,1,0:T(8,128)S(1)}, u32[]{:S(2)}, u32[]{:S(2)}) collective-permute-start(f32[88,2,8,128]{3,2,1,0:T(8,128)S(1)} %add_select_fusion.rest_1_), channel_id=1, source_target_pairs={{0,4},{4,0},{8,12},{12,8},{1,5},{5,1},{9,13},{13,9},{2,6},{6,2},{1... | collective-permute-start | bytes 2162696 | tf_op jit(solution)/shard_map/cond/branch_0_fun/ppermute | solution.py:308
  188.3 14.4 %restore.12.moved_ref = f32[32,288,768]{2,1,0:T(8,128)} custom-call(s32[9]{0:T(128)S(1)} %select_reduce_fusion.offset_ref, s32[1]{0:T(128)} %bitcast.2.end_ref, f32[32,288,768]{2,1,0:T(8,128)} %get-tuple-element.716.moved_ref, f32[88,2,8,128]{3,2,1,0:T(8,128)S(1)} %collective-permute-done.4.rest_0_, ...), custom_call_target="tpu_custom_call", output_to_operand_aliasing={{}: (2, {})} | custom-call | flops 2887778304 | bytes 21233664 | tf_op jit(solution)/shard_map/cond/branch_0_fun/restore/pallas_call | solution.py:246
  202.9 0.9 collective-permute-start.15
  203.8 2.3 collective-permute-start.16
  206.1 10.5 %restore.13.moved_ref = f32[32,288,768]{2,1,0:T(8,128)} custom-call(s32[9]{0:T(128)S(1)} %select_reduce_fusion.offset_ref, s32[1]{0:T(128)} %bitcast.2.end_ref, f32[32,288,768]{2,1,0:T(8,128)} %restore.12.moved_ref, f32[88,2,8,128]{3,2,1,0:T(8,128)S(1)} %collective-permute-done.10.rest_0_, ...), custom_call_target="tpu_custom_call", output_to_operand_aliasing={{}: (2, {})} | custom-call | flops 1925185536 | bytes 14155776 | tf_op jit(solution)/shard_map/cond/branch_0_fun/restore/pallas_call | solution.py:246
  216.7 0.8 collective-permute-start.17
  217.5 2.7 %collective-permute-done.16.rest_2_ = f32[88,2,8,128]{3,2,1,0:T(8,128)S(1)} collective-permute-done((f32[88,2,8,128]{3,2,1,0:T(8,128)S(1)}, f32[88,2,8,128]{3,2,1,0:T(8,128)S(1)}, u32[]{:S(2)}, u32[]{:S(2)}) %collective-permute-start.16) | collective-permute-done | bytes 720928 | tf_op jit(solution)/shard_map/cond/branch_0_fun/ppermute | solution.py:308
  220.2 10.5 %restore.14.moved_ref = f32[32,288,768]{2,1,0:T(8,128)} custom-call(s32[9]{0:T(128)S(1)} %select_reduce_fusion.offset_ref, s32[1]{0:T(128)} %bitcast.2.end_ref, f32[32,288,768]{2,1,0:T(8,128)} %restore.13.moved_ref, f32[88,2,8,128]{3,2,1,0:T(8,128)S(1)} %collective-permute-done.14.rest_0_, ...), custom_call_target="tpu_custom_call", output_to_operand_aliasing={{}: (2, {})} | custom-call | flops 1925185536 | bytes 14155776 | tf_op jit(solution)/shard_map/cond/branch_0_fun/restore/pallas_call | solution.py:246
  230.7 1.2 collective-permute-done.17.rest_0_
  231.9 6.1 %restore.15 = f32[32,288,768]{2,1,0:T(8,128)} custom-call(s32[9]{0:T(128)S(1)} %select_reduce_fusion.offset_ref, s32[1]{0:T(128)} %bitcast.2.end_ref, f32[32,288,768]{2,1,0:T(8,128)} %restore.14.moved_ref, f32[88,2,8,128]{3,2,1,0:T(8,128)S(1)} %collective-permute-done.17.rest_0_, ...), custom_call_target="tpu_custom_call", output_to_operand_aliasing={{}: (2, {})} | custom-call | flops 962592768 | bytes 7077888 | tf_op jit(solution)/shard_map/cond/branch_0_fun/restore/pallas_call | solution.py:246
  (104 shorter events, 8.3 us)
Async XLA Ops:
  0.0 32.4 %collective-permute-start.56 = (f32[2,144,768]{2,1,0:T(8,128)}, f32[2,144,768]{2,1,0:T(8,128)}, u32[]{:S(2)}, u32[]{:S(2)}) collective-permute-start(f32[2,144,768]{2,1,0:T(8,128)} %bitcast.70), channel_id=1, source_target_pairs={{0,2},{2,0},{1,3},{3,1},{4,6},{6,4},{5,7},{7,5},{8,10},{10,8},{9,1... | collective-permute-start | bytes 2654216 | tf_op jit(solution)/shard_map/ppermute | solution.py:383
  3.7 31.3 %collective-permute-start.55 = (f32[1,768]{1,0:T(1,128)S(1)}, f32[1,768]{1,0:T(1,128)S(1)}, u32[]{:S(2)}, u32[]{:S(2)}) collective-permute-start(f32[1,768]{1,0:T(1,128)S(1)} %slice_bitcast_fusion), channel_id=1, source_target_pairs={{4,2},{8,6},{12,10},{0,14},{5,3},{9,7},{13,11},{1,15},{20,18},{24,... | collective-permute-start | bytes 9224 | tf_op jit(solution)/shard_map/ppermute | solution.py:386
  10.7 10.7 %collective-permute-start.58 = (f32[32,2,768]{2,1,0:T(2,128)S(1)}, f32[32,2,768]{2,1,0:T(2,128)S(1)}, u32[]{:S(2)}, u32[]{:S(2)}) collective-permute-start(f32[32,2,768]{2,1,0:T(2,128)S(1)} %get-tuple-element.980), channel_id=1, source_target_pairs={{0,4},{4,8},{8,12},{12,0},{1,5},{5,9},{9,13},{13,1},{2,6},{6,10},{... | collective-permute-start | bytes 589832 | tf_op jit(solution)/shard_map/ppermute | solution.py:323
  10.8 10.7 %collective-permute-start.59 = (f32[32,2,768]{2,1,0:T(2,128)S(1)}, f32[32,2,768]{2,1,0:T(2,128)S(1)}, u32[]{:S(2)}, u32[]{:S(2)}) collective-permute-start(f32[32,2,768]{2,1,0:T(2,128)S(1)} %get-tuple-element.981), channel_id=1, source_target_pairs={{4,0},{8,4},{12,8},{0,12},{5,1},{9,5},{13,9},{1,13},{6,2},{10,6},{... | collective-permute-start | bytes 589832 | tf_op jit(solution)/shard_map/ppermute | solution.py:324
  14.6 17.7 %collective-permute-start.57 = (f32[144,768]{1,0:T(8,128)}, f32[144,768]{1,0:T(8,128)S(1)}, u32[]{:S(2)}, u32[]{:S(2)}) collective-permute-start(f32[144,768]{1,0:T(8,128)} %bitcast.72), channel_id=1, source_target_pairs={{0,2},{2,0},{1,3},{3,1},{4,6},{6,4},{5,7},{7,5},{8,10},{10,8},{9,1... | collective-permute-start | bytes 1327112 | tf_op jit(solution)/shard_map/ppermute | solution.py:383
  18.2 14.1 %copy-start.28 = (f32[1,144,768]{2,1,0:T(8,128)S(1)}, f32[1,144,768]{2,1,0:T(8,128)}, u32[]{:S(2)}) copy-start(f32[1,144,768]{2,1,0:T(8,128)} %param.14) | copy-start | bytes 1327108
  21.4 13.6 %collective-permute-start.54 = (f32[1,768]{1,0:T(1,128)S(1)}, f32[1,768]{1,0:T(1,128)S(1)}, u32[]{:S(2)}, u32[]{:S(2)}) collective-permute-start(f32[1,768]{1,0:T(1,128)S(1)} %slice_bitcast_fusion), channel_id=1, source_target_pairs={{4,0},{8,4},{12,8},{0,12},{5,1},{9,5},{13,9},{1,13},{6,2},{10,6},{... | collective-permute-start | bytes 9224 | tf_op jit(solution)/shard_map/ppermute | solution.py:385
  32.3 1.2 copy-start.27
  34.8 2.0 copy-start.10
  34.8 2.0 copy-start.29
  34.8 2.0 copy-start.30
  37.0 17.6 %copy-start.11 = (bf16[8,288,768]{2,1,0:T(8,128)(2,1)}, bf16[8,288,768]{2,1,0:T(8,128)(2,1)S(1)}, u32[]{:S(2)}) copy-start(bf16[8,288,768]{2,1,0:T(8,128)(2,1)S(1)} %get-tuple-element.944.source_ref) | copy-start | bytes 10616836 | tf_op jit(solution)/shard_map/cond
  40.2 14.4 %copy-start = (f32[9,288,768]{2,1,0:T(8,128)}, f32[9,288,768]{2,1,0:T(8,128)S(1)}, u32[]{:S(2)}) copy-start(f32[9,288,768]{2,1,0:T(8,128)S(1)} %stencil_weights.3.weight_ref) | copy-start | bytes 23887876 | tf_op jit(solution)/shard_map/cond
  52.7 17.4 %collective-permute-start = (f32[88,2,8,128]{3,2,1,0:T(8,128)S(1)}, f32[88,2,8,128]{3,2,1,0:T(8,128)S(1)}, u32[]{:S(2)}, u32[]{:S(2)}) collective-permute-start(f32[88,2,8,128]{3,2,1,0:T(8,128)S(1)} %get-tuple-element.677), channel_id=1, source_target_pairs={{0,4},{4,0},{8,12},{12,8},{1,5},{5,1},{9,13},{13,9},{2,6},{6,2},{1... | collective-permute-start | bytes 2162696 | tf_op jit(solution)/shard_map/cond/branch_0_fun/ppermute | solution.py:308
  65.6 10.2 %copy-start.7 = (f32[32,288,768]{2,1,0:T(8,128)}, f32[32,288,768]{2,1,0:T(8,128)S(1)}, u32[]{:S(2)}) copy-start(f32[32,288,768]{2,1,0:T(8,128)S(1)} %get-tuple-element.679.rest_0_) | copy-start | bytes 84934656 | tf_op jit(solution)/shard_map/cond
  75.8 18.5 %collective-permute-start.2 = (f32[88,2,8,128]{3,2,1,0:T(8,128)S(1)}, f32[88,2,8,128]{3,2,1,0:T(8,128)}, u32[]{:S(2)}, u32[]{:S(2)}) collective-permute-start(f32[88,2,8,128]{3,2,1,0:T(8,128)S(1)} %get-tuple-element.684), channel_id=1, source_target_pairs={{0,4},{4,0},{8,12},{12,8},{1,5},{5,1},{9,13},{13,9},{2,6},{6,2},{1... | collective-permute-start | bytes 2162696 | tf_op jit(solution)/shard_map/cond/branch_0_fun/ppermute | solution.py:308
  76.0 19.7 %collective-permute-start.1 = (f32[88,2,8,128]{3,2,1,0:T(8,128)}, f32[88,2,8,128]{3,2,1,0:T(8,128)}, u32[]{:S(2)}, u32[]{:S(2)}) collective-permute-start(f32[88,2,8,128]{3,2,1,0:T(8,128)} %add.199), channel_id=1, source_target_pairs={{4,8},{8,4},{5,9},{9,5},{6,10},{10,6},{7,11},{11,7},{20,24},{24,20... | collective-permute-start | bytes 2162696 | tf_op jit(solution)/shard_map/cond/branch_0_fun/ppermute | solution.py:309
  77.8 3.3 %copy-start.1 = (f32[9,288,768]{2,1,0:T(8,128)S(1)}, f32[9,288,768]{2,1,0:T(8,128)}, u32[]{:S(2)}) copy-start(f32[9,288,768]{2,1,0:T(8,128)} %copy-done) | copy-start | bytes 23887876 | tf_op jit(solution)/shard_map/cond
  94.3 7.8 %copy-start.12 = (bf16[8,288,768]{2,1,0:T(8,128)(2,1)S(1)}, bf16[8,288,768]{2,1,0:T(8,128)(2,1)}, u32[]{:S(2)}) copy-start(bf16[8,288,768]{2,1,0:T(8,128)(2,1)} %copy-done.11) | copy-start | bytes 10616836 | tf_op jit(solution)/shard_map/cond
  95.7 25.4 %slice-start = ((s8[28311552]{0:T(1024)(128)(4,1)}), s8[4194304]{0:T(1024)(128)(4,1)S(1)}, s32[]{:S(2)}) async-start(s8[28311552]{0:T(1024)(128)(4,1)} %bitcast.64), calls=%async_computation | async-start | bytes 8388608 | tf_op jit(solution)/shard_map/cond
  97.4 23.8 %slice-start.1 = ((s8[28311552]{0:T(1024)(128)(4,1)}), s8[4194304]{0:T(1024)(128)(4,1)S(1)}, s32[]{:S(2)}) async-start(s8[28311552]{0:T(1024)(128)(4,1)} %bitcast.64), calls=%async_computation.1 | async-start | bytes 8388608 | tf_op jit(solution)/shard_map/cond
  97.4 23.8 %slice-start.2 = ((s8[28311552]{0:T(1024)(128)(4,1)}), s8[4194304]{0:T(1024)(128)(4,1)S(1)}, s32[]{:S(2)}) async-start(s8[28311552]{0:T(1024)(128)(4,1)} %bitcast.64), calls=%async_computation.2 | async-start | bytes 8388608 | tf_op jit(solution)/shard_map/cond
  97.4 23.8 %slice-start.3 = ((s8[28311552]{0:T(1024)(128)(4,1)}), s8[4194304]{0:T(1024)(128)(4,1)S(1)}, s32[]{:S(2)}) async-start(s8[28311552]{0:T(1024)(128)(4,1)} %bitcast.64), calls=%async_computation.3 | async-start | bytes 8388608 | tf_op jit(solution)/shard_map/cond
  97.4 23.8 %slice-start.4 = ((s8[28311552]{0:T(1024)(128)(4,1)}), s8[4194304]{0:T(1024)(128)(4,1)S(1)}, s32[]{:S(2)}) async-start(s8[28311552]{0:T(1024)(128)(4,1)} %bitcast.64), calls=%async_computation.4 | async-start | bytes 8388608 | tf_op jit(solution)/shard_map/cond
  97.4 23.8 %slice-start.5 = ((s8[28311552]{0:T(1024)(128)(4,1)}), s8[4194304]{0:T(1024)(128)(4,1)S(1)}, s32[]{:S(2)}) async-start(s8[28311552]{0:T(1024)(128)(4,1)} %bitcast.64), calls=%async_computation.5 | async-start | bytes 8388608 | tf_op jit(solution)/shard_map/cond
  97.4 23.8 %slice-start.6 = ((s8[28311552]{0:T(1024)(128)(4,1)}), s8[3145728]{0:T(1024)(128)(4,1)S(1)}, s32[]{:S(2)}) async-start(s8[28311552]{0:T(1024)(128)(4,1)} %bitcast.64), calls=%async_computation.6 | async-start | bytes 6291456 | tf_op jit(solution)/shard_map/cond
  97.5 18.3 %collective-permute-start.4 = (f32[88,2,8,128]{3,2,1,0:T(8,128)S(1)}, f32[88,2,8,128]{3,2,1,0:T(8,128)S(1)}, u32[]{:S(2)}, u32[]{:S(2)}) collective-permute-start(f32[88,2,8,128]{3,2,1,0:T(8,128)S(1)} %add_select_fusion.5.rest_1_), channel_id=1, source_target_pairs={{0,4},{4,0},{8,12},{12,8},{1,5},{5,1},{9,13},{13,9},{2,6},{6,2},{1... | collective-permute-start | bytes 2162696 | tf_op jit(solution)/shard_map/cond/branch_0_fun/ppermute | solution.py:308
  101.3 14.5 %collective-permute-start.3 = (f32[88,2,8,128]{3,2,1,0:T(8,128)S(1)}, f32[88,2,8,128]{3,2,1,0:T(8,128)S(1)}, u32[]{:S(2)}, u32[]{:S(2)}) collective-permute-start(f32[88,2,8,128]{3,2,1,0:T(8,128)S(1)} %add.201), channel_id=1, source_target_pairs={{4,8},{8,4},{5,9},{9,5},{6,10},{10,6},{7,11},{11,7},{20,24},{24,20... | collective-permute-start | bytes 2162696 | tf_op jit(solution)/shard_map/cond/branch_0_fun/ppermute | solution.py:309
  116.0 17.6 %collective-permute-start.6 = (f32[88,2,8,128]{3,2,1,0:T(8,128)S(1)}, f32[88,2,8,128]{3,2,1,0:T(8,128)S(1)}, u32[]{:S(2)}, u32[]{:S(2)}) collective-permute-start(f32[88,2,8,128]{3,2,1,0:T(8,128)S(1)} %add_select_fusion.4.rest_3_), channel_id=1, source_target_pairs={{0,4},{4,0},{8,12},{12,8},{1,5},{5,1},{9,13},{13,9},{2,6},{6,2},{1... | collective-permute-start | bytes 2162696 | tf_op jit(solution)/shard_map/cond/branch_0_fun/ppermute | solution.py:308
  120.0 13.7 %collective-permute-start.5 = (f32[88,2,8,128]{3,2,1,0:T(8,128)S(1)}, f32[88,2,8,128]{3,2,1,0:T(8,128)S(1)}, u32[]{:S(2)}, u32[]{:S(2)}) collective-permute-start(f32[88,2,8,128]{3,2,1,0:T(8,128)S(1)} %add.203), channel_id=1, source_target_pairs={{4,8},{8,4},{5,9},{9,5},{6,10},{10,6},{7,11},{11,7},{20,24},{24,20... | collective-permute-start | bytes 2162696 | tf_op jit(solution)/shard_map/cond/branch_0_fun/ppermute | solution.py:309
  133.8 16.6 %collective-permute-start.8 = (f32[88,2,8,128]{3,2,1,0:T(8,128)S(1)}, f32[88,2,8,128]{3,2,1,0:T(8,128)S(1)}, u32[]{:S(2)}, u32[]{:S(2)}) collective-permute-start(f32[88,2,8,128]{3,2,1,0:T(8,128)S(1)} %add_select_fusion.3.rest_5_), channel_id=1, source_target_pairs={{0,4},{4,0},{8,12},{12,8},{1,5},{5,1},{9,13},{13,9},{2,6},{6,2},{1... | collective-permute-start | bytes 2162696 | tf_op jit(solution)/shard_map/cond/branch_0_fun/ppermute | solution.py:308
  137.3 13.1 %collective-permute-start.7 = (f32[88,2,8,128]{3,2,1,0:T(8,128)S(1)}, f32[88,2,8,128]{3,2,1,0:T(8,128)S(1)}, u32[]{:S(2)}, u32[]{:S(2)}) collective-permute-start(f32[88,2,8,128]{3,2,1,0:T(8,128)S(1)} %add.205), channel_id=1, source_target_pairs={{4,8},{8,4},{5,9},{9,5},{6,10},{10,6},{7,11},{11,7},{20,24},{24,20... | collective-permute-start | bytes 2162696 | tf_op jit(solution)/shard_map/cond/branch_0_fun/ppermute | solution.py:309
  150.4 4.3 %copy-start.13 = (bf16[8,288,768]{2,1,0:T(8,128)(2,1)S(1)}, bf16[8,288,768]{2,1,0:T(8,128)(2,1)}, u32[]{:S(2)}) copy-start(bf16[8,288,768]{2,1,0:T(8,128)(2,1)} %copy-done.11) | copy-start | bytes 10616836 | tf_op jit(solution)/shard_map/cond
  150.6 16.2 %collective-permute-start.10 = (f32[88,2,8,128]{3,2,1,0:T(8,128)S(1)}, f32[88,2,8,128]{3,2,1,0:T(8,128)S(1)}, u32[]{:S(2)}, u32[]{:S(2)}) collective-permute-start(f32[88,2,8,128]{3,2,1,0:T(8,128)S(1)} %add_select_fusion.2.rest_1_), channel_id=1, source_target_pairs={{0,4},{4,0},{8,12},{12,8},{1,5},{5,1},{9,13},{13,9},{2,6},{6,2},{1... | collective-permute-start | bytes 2162696 | tf_op jit(solution)/shard_map/cond/branch_0_fun/ppermute | solution.py:308
  153.8 13.2 %collective-permute-start.9 = (f32[88,2,8,128]{3,2,1,0:T(8,128)S(1)}, f32[88,2,8,128]{3,2,1,0:T(8,128)S(1)}, u32[]{:S(2)}, u32[]{:S(2)}) collective-permute-start(f32[88,2,8,128]{3,2,1,0:T(8,128)S(1)} %add.207), channel_id=1, source_target_pairs={{4,8},{8,4},{5,9},{9,5},{6,10},{10,6},{7,11},{11,7},{20,24},{24,20... | collective-permute-start | bytes 2162696 | tf_op jit(solution)/shard_map/cond/branch_0_fun/ppermute | solution.py:309
  167.1 15.4 %collective-permute-start.12 = (f32[88,2,8,128]{3,2,1,0:T(8,128)S(1)}, f32[88,2,8,128]{3,2,1,0:T(8,128)S(1)}, u32[]{:S(2)}, u32[]{:S(2)}) collective-permute-start(f32[88,2,8,128]{3,2,1,0:T(8,128)S(1)} %add_select_fusion.1.rest_3_), channel_id=1, source_target_pairs={{0,4},{4,0},{8,12},{12,8},{1,5},{5,1},{9,13},{13,9},{2,6},{6,2},{1... | collective-permute-start | bytes 2162696 | tf_op jit(solution)/shard_map/cond/branch_0_fun/ppermute | solution.py:308
  169.6 13.0 %collective-permute-start.11 = (f32[88,2,8,128]{3,2,1,0:T(8,128)S(1)}, f32[88,2,8,128]{3,2,1,0:T(8,128)S(1)}, u32[]{:S(2)}, u32[]{:S(2)}) collective-permute-start(f32[88,2,8,128]{3,2,1,0:T(8,128)S(1)} %add.209), channel_id=1, source_target_pairs={{4,8},{8,4},{5,9},{9,5},{6,10},{10,6},{7,11},{11,7},{20,24},{24,20... | collective-permute-start | bytes 2162696 | tf_op jit(solution)/shard_map/cond/branch_0_fun/ppermute | solution.py:309
  182.6 5.7 %copy-start.21 = (bf16[576,576]{1,0:T(8,128)(2,1)S(1)}, bf16[576,576]{1,0:T(8,128)(2,1)}, u32[]{:S(2)}) copy-start(bf16[576,576]{1,0:T(8,128)(2,1)} %get-tuple-element.718.rest_8_.rest_6_.rest_4_) | copy-start | bytes 1990660 | tf_op jit(solution)/shard_map/cond
  182.6 5.7 %copy-start.24 = (bf16[256,768]{1,0:T(8,128)(2,1)S(1)}, bf16[256,768]{1,0:T(8,128)(2,1)}, u32[]{:S(2)}) copy-start(bf16[256,768]{1,0:T(8,128)(2,1)} %get-tuple-element.720.rest_10_.rest_8_.rest_6_) | copy-start | bytes 1179652 | tf_op jit(solution)/shard_map/cond
  182.8 19.9 %collective-permute-start.13 = (f32[88,2,8,128]{3,2,1,0:T(8,128)S(1)}, f32[88,2,8,128]{3,2,1,0:T(8,128)S(1)}, u32[]{:S(2)}, u32[]{:S(2)}) collective-permute-start(f32[88,2,8,128]{3,2,1,0:T(8,128)S(1)} %add.211), channel_id=1, source_target_pairs={{4,8},{8,4},{5,9},{9,5},{6,10},{10,6},{7,11},{11,7},{20,24},{24,20... | collective-permute-start | bytes 2162696 | tf_op jit(solution)/shard_map/cond/branch_0_fun/ppermute | solution.py:309
  183.6 19.2 %collective-permute-start.14 = (f32[88,2,8,128]{3,2,1,0:T(8,128)S(1)}, f32[88,2,8,128]{3,2,1,0:T(8,128)S(1)}, u32[]{:S(2)}, u32[]{:S(2)}) collective-permute-start(f32[88,2,8,128]{3,2,1,0:T(8,128)S(1)} %add_select_fusion.rest_1_), channel_id=1, source_target_pairs={{0,4},{4,0},{8,12},{12,8},{1,5},{5,1},{9,13},{13,9},{2,6},{6,2},{1... | collective-permute-start | bytes 2162696 | tf_op jit(solution)/shard_map/cond/branch_0_fun/ppermute | solution.py:308
  202.9 13.7 %collective-permute-start.15 = (f32[88,2,8,128]{3,2,1,0:T(8,128)S(1)}, f32[88,2,8,128]{3,2,1,0:T(8,128)S(1)}, u32[]{:S(2)}, u32[]{:S(2)}) collective-permute-start(f32[88,2,8,128]{3,2,1,0:T(8,128)S(1)} %add.213), channel_id=1, source_target_pairs={{4,8},{8,4},{5,9},{9,5},{6,10},{10,6},{7,11},{11,7},{20,24},{24,20... | collective-permute-start | bytes 2162696 | tf_op jit(solution)/shard_map/cond/branch_0_fun/ppermute | solution.py:309
  203.8 16.4 %collective-permute-start.16 = (f32[88,2,8,128]{3,2,1,0:T(8,128)S(1)}, f32[88,2,8,128]{3,2,1,0:T(8,128)S(1)}, u32[]{:S(2)}, u32[]{:S(2)}) collective-permute-start(f32[88,2,8,128]{3,2,1,0:T(8,128)S(1)} %add.212.rest_3_), channel_id=1, source_target_pairs={{0,4},{4,0},{8,12},{12,8},{1,5},{5,1},{9,13},{13,9},{2,6},{6,2},{1... | collective-permute-start | bytes 2162696 | tf_op jit(solution)/shard_map/cond/branch_0_fun/ppermute | solution.py:308
  216.7 15.2 %collective-permute-start.17 = (f32[88,2,8,128]{3,2,1,0:T(8,128)S(1)}, f32[88,2,8,128]{3,2,1,0:T(8,128)S(1)}, u32[]{:S(2)}, u32[]{:S(2)}) collective-permute-start(f32[88,2,8,128]{3,2,1,0:T(8,128)S(1)} %add.214.rest_1_), channel_id=1, source_target_pairs={{0,4},{4,0},{8,12},{12,8},{1,5},{5,1},{9,13},{13,9},{2,6},{6,2},{1... | collective-permute-start | bytes 2162696 | tf_op jit(solution)/shard_map/cond/branch_0_fun/ppermute | solution.py:308

commit v3 on v2

--- a/solution.py
+++ b/solution.py
@@ -15,7 +15,7 @@
 LANES = 128
 CHUNK = 4
 CAPS = (0.605, 0.66, 1.0)
-VMEM = 18 * 1024 * 1024
+VMEM = 32 * 1024 * 1024
 
 
 def wave_table(length):

time: 250 us -> 244 us (0.976)
  local copies, waits for them, and re-layouts: 13.6 us -> 9.63 us
    cond x30 -> x12, local copies, waits for them, and re-layouts: 7.22 us -> 3.27 us
  transfers between devices with their start and end apart: 24 -> 24, of which waited for: 5 -> 5; matrix products, arithmetic and copies ran while one was open for 5% -> 5% of each run, Pallas kernels for 49% -> 51%
where the time goes in v3:
time: 244 us; the launch traced here: 241 us
  Pallas kernels  144 us (59%)
  starting transfers between devices  45.9 us (19%)
  waiting for transfers between devices  18.8 us (8%)
  other arithmetic  11.9 us (5%)
  local copies, waits for them, and re-layouts  9.63 us (4%)
  loops' own time  7.67 us (3%)
  between operations  2.89 us (1%)
    pallas_call x8, Pallas kernels, forward(): pl.pallas_call(functools.partial(forward_kernel, cap, first=base), grid_s...  100 us
    pallas_call x4, Pallas kernels, inverse(): pl.pallas_call(functools.partial(inverse_kernel, cap, pairs, many), grid_...  41.4 us
    ppermute x10, starting transfers between devices, stepped_pipeline(): swapped = None if sent is None else lax.ppermute(sent, 'lon', swap)  26 us
    ppermute x1, waiting for transfers between devices, body(): lax.ppermute(thickness, 'tag', cross)  10.6 us
    ppermute x10, waiting for transfers between devices, stepped_pipeline(): swapped = None if sent is None else lax.ppermute(sent, 'lon', swap)  8.15 us
    another operation x1, loops' own time, body(): out = lax.switch(index, [functools.partial(run, cap) for cap in caps])  7.67 us
    ppermute x8, starting transfers between devices, stepped_pipeline(): crossed = None if pair_sum is None else lax.ppermute(pair_sum, 'lon', cross)  7.59 us
    ppermute x1, starting transfers between devices, body(): lax.ppermute(ahead_zonal, ('lon', 'tag'), [((i + 1) % count * 2, i * 2 +...  5.46 us
  transfers between devices with their start and end apart: 24, of which 5 were waited for; matrix products, arithmetic and copies ran while one was open for 5% of the time, Pallas kernels for 51%

profile of v3, /device:TPU:0, one launch (start us, length us, event | category | flops | bytes accessed | tf_op | source)
XLA Modules:
  0.0 240.8 jit_solution(17336207185487264835)
XLA Ops:
  0.0 2.9 %collective-permute-start.56 = (f32[2,144,768]{2,1,0:T(8,128)}, f32[2,144,768]{2,1,0:T(8,128)}, u32[]{:S(2)}, u32[]{:S(2)}) collective-permute-start(f32[2,144,768]{2,1,0:T(8,128)} %bitcast.64), channel_id=1, source_target_pairs={{0,2},{2,0},{1,3},{3,1},{4,6},{6,4},{5,7},{7,5},{8,10},{10,8},{9,1... | collective-permute-start | bytes 2654216 | tf_op jit(solution)/shard_map/ppermute | solution.py:383
  2.9 0.8 slice_bitcast_fusion
  3.7 5.5 %collective-permute-start.55 = (f32[1,768]{1,0:T(1,128)S(1)}, f32[1,768]{1,0:T(1,128)S(1)}, u32[]{:S(2)}, u32[]{:S(2)}) collective-permute-start(f32[1,768]{1,0:T(1,128)S(1)} %slice_bitcast_fusion), channel_id=1, source_target_pairs={{4,2},{8,6},{12,10},{0,14},{5,3},{9,7},{13,11},{1,15},{20,18},{24,... | collective-permute-start | bytes 9224 | tf_op jit(solution)/shard_map/ppermute | solution.py:386
  9.2 1.5 fusion.26
  10.8 3.8 %collective-permute-start.59 = (f32[32,2,768]{2,1,0:T(2,128)S(1)}, f32[32,2,768]{2,1,0:T(2,128)S(1)}, u32[]{:S(2)}, u32[]{:S(2)}) collective-permute-start(f32[32,2,768]{2,1,0:T(2,128)S(1)} %get-tuple-element.981), channel_id=1, source_target_pairs={{4,0},{8,4},{12,8},{0,12},{5,1},{9,5},{13,9},{1,13},{6,2},{10,6},{... | collective-permute-start | bytes 589832 | tf_op jit(solution)/shard_map/ppermute | solution.py:324
  17.0 1.2 constant_dynamic-slice_fusion
  18.2 0.9 pad_maximum_fusion.2
  20.4 0.8 add_convert_fusion
  21.7 10.6 %collective-permute-done.57 = f32[144,768]{1,0:T(8,128)S(1)} collective-permute-done((f32[144,768]{1,0:T(8,128)}, f32[144,768]{1,0:T(8,128)S(1)}, u32[]{:S(2)}, u32[]{:S(2)}) %collective-permute-start.57) | collective-permute-done | bytes 442400 | tf_op jit(solution)/shard_map/ppermute | solution.py:383
  32.4 1.1 copy-done.21
  33.5 1.3 broadcast_select_fusion.4
  35.0 1.8 copy-done.6
  36.8 202.5 %conditional.1 = (f32[32,1,288,768]{3,2,1,0:T(8,128)}) conditional(s32[]{:T(128)} %clamp.3, (s32[9,9]{1,0:T(8,128)S(1)}, s32[9,9]{1,0:T(8,128)S(1)}, s32[9]{0:T(128)S(1)}, (), s32[]{:T(128)}, /*index=5*/s32[]{:T(128)}, s32[]{:T(128)}, pred[]{:T(512)}, f32[1,768]{1,0:T(1,128)S(1)}, f32[1,768]{1,0:T(1,128)S(1)}, ...), branch_computations={%region_4.7_spmd, %region_7.10_spmd, %region_10.13_spmd} | conditional | flops 15421826048 | bytes 469628160 | solution.py:419
  37.6 2.6 %stencil_weights.3.weight_ref = f32[9,288,768]{2,1,0:T(8,128)S(1)} custom-call(f32[2,288,768]{2,1,0:T(8,128)S(1)} %get-tuple-element.646.fields_ref, f32[288,768]{1,0:T(8,128)S(1)} %get-tuple-element.647.thick_ref, f32[1,768]{1,0:T(1,128)S(1)} %broadcast_select_fusion.end_ref), custom_call_target="tpu_custom_call" | custom-call | flops 13271040 | bytes 10616832 | tf_op jit(solution)/shard_map/cond/branch_0_fun/stencil_weights/pallas_call | solution.py:74
  40.3 13.5 %step_and_transform.24 = (f32[32,288,768]{2,1,0:T(8,128)}, f32[88,2,8,128]{3,2,1,0:T(8,128)S(1)}) custom-call(s32[9]{0:T(128)S(1)} %select_reduce_fusion.offset_ref, s32[32]{0:T(128)S(1)} %get-tuple-element.941.region_ref, f32[32,288,768]{2,1,0:T(8,128)} %get-tuple-element.645.q_ref, f32[32,4,768]{2,1,0:T(4,128)S(1)} %get-tuple-element.664.edge_ref, ...), custom_call_target="tpu_custom_call" | custom-call | flops 962592768 | bytes 17694720 | tf_op jit(solution)/shard_map/cond/branch_0_fun/step_and_transform/pallas_call | solution.py:216
  53.8 1.8 collective-permute-start
  55.7 12.2 %step_and_transform.25 = (f32[32,288,768]{2,1,0:T(8,128)}, f32[88,2,8,128]{3,2,1,0:T(8,128)S(1)}) custom-call(s32[9]{0:T(128)S(1)} %select_reduce_fusion.offset_ref, s32[32]{0:T(128)S(1)} %get-tuple-element.941.region_ref, f32[32,288,768]{2,1,0:T(8,128)} %get-tuple-element.645.q_ref, ...), custom_call_target="tpu_custom_call", output_to_operand_aliasing={{0}: (11, {})} | custom-call | flops 962592768 | bytes 17694720 | tf_op jit(solution)/shard_map/cond/branch_0_fun/step_and_transform/pallas_call | solution.py:216
  67.8 3.3 %collective-permute-done = f32[88,2,8,128]{3,2,1,0:T(8,128)S(1)} collective-permute-done((f32[88,2,8,128]{3,2,1,0:T(8,128)S(1)}, f32[88,2,8,128]{3,2,1,0:T(8,128)S(1)}, u32[]{:S(2)}, u32[]{:S(2)}) %collective-permute-start) | collective-permute-done | bytes 720928 | tf_op jit(solution)/shard_map/cond/branch_0_fun/ppermute | solution.py:308
  71.1 1.0 add.199
  72.2 1.5 collective-permute-start.2
  73.7 1.7 collective-permute-start.1
  75.4 3.3 %copy-done.1 = f32[9,288,768]{2,1,0:T(8,128)S(1)} copy-done((f32[9,288,768]{2,1,0:T(8,128)S(1)}, f32[9,288,768]{2,1,0:T(8,128)}, u32[]{:S(2)}) %copy-start.1) | copy-done | bytes 7962648 | tf_op jit(solution)/shard_map/cond
  78.7 13.3 %step_and_transform.26 = (f32[32,288,768]{2,1,0:T(8,128)}, f32[88,2,8,128]{3,2,1,0:T(8,128)S(1)}) custom-call(s32[9]{0:T(128)S(1)} %select_reduce_fusion.offset_ref, s32[32]{0:T(128)S(1)} %get-tuple-element.941.region_ref, f32[32,288,768]{2,1,0:T(8,128)} %get-tuple-element.645.q_ref, ...), custom_call_target="tpu_custom_call", output_to_operand_aliasing={{0}: (11, {})} | custom-call | flops 962592768 | bytes 17694720 | tf_op jit(solution)/shard_map/cond/branch_0_fun/step_and_transform/pallas_call | solution.py:216
  91.9 1.4 add.201
  93.3 1.5 add_select_fusion.5.rest_1_
  94.8 3.6 %collective-permute-start.4 = (f32[88,2,8,128]{3,2,1,0:T(8,128)S(1)}, f32[88,2,8,128]{3,2,1,0:T(8,128)S(1)}, u32[]{:S(2)}, u32[]{:S(2)}) collective-permute-start(f32[88,2,8,128]{3,2,1,0:T(8,128)S(1)} %add_select_fusion.5.rest_1_), channel_id=1, source_target_pairs={{0,4},{4,0},{8,12},{12,8},{1,5},{5,1},{9,13},{13,9},{2,6},{6,2},{1... | collective-permute-start | bytes 2162696 | tf_op jit(solution)/shard_map/cond/branch_0_fun/ppermute | solution.py:308
  99.2 12.2 %step_and_transform.27 = (f32[32,288,768]{2,1,0:T(8,128)}, f32[88,2,8,128]{3,2,1,0:T(8,128)S(1)}) custom-call(s32[9]{0:T(128)S(1)} %select_reduce_fusion.offset_ref, s32[32]{0:T(128)S(1)} %get-tuple-element.941.region_ref, f32[32,288,768]{2,1,0:T(8,128)} %get-tuple-element.645.q_ref, ...), custom_call_target="tpu_custom_call", output_to_operand_aliasing={{0}: (11, {})} | custom-call | flops 962592768 | bytes 17694720 | tf_op jit(solution)/shard_map/cond/branch_0_fun/step_and_transform/pallas_call | solution.py:216
  111.4 0.9 collective-permute-done.4.rest_0_
  112.5 3.6 %collective-permute-start.6 = (f32[88,2,8,128]{3,2,1,0:T(8,128)S(1)}, f32[88,2,8,128]{3,2,1,0:T(8,128)S(1)}, u32[]{:S(2)}, u32[]{:S(2)}) collective-permute-start(f32[88,2,8,128]{3,2,1,0:T(8,128)S(1)} %add_select_fusion.4.rest_3_), channel_id=1, source_target_pairs={{0,4},{4,0},{8,12},{12,8},{1,5},{5,1},{9,13},{13,9},{2,6},{6,2},{1... | collective-permute-start | bytes 2162696 | tf_op jit(solution)/shard_map/cond/branch_0_fun/ppermute | solution.py:308
  116.1 1.2 collective-permute-start.5
  117.3 12.2 %step_and_transform.28 = (f32[32,288,768]{2,1,0:T(8,128)}, f32[88,2,8,128]{3,2,1,0:T(8,128)S(1)}) custom-call(s32[9]{0:T(128)S(1)} %select_reduce_fusion.offset_ref, s32[32]{0:T(128)S(1)} %get-tuple-element.941.region_ref, f32[32,288,768]{2,1,0:T(8,128)} %get-tuple-element.645.q_ref, ...), custom_call_target="tpu_custom_call", output_to_operand_aliasing={{0}: (11, {})} | custom-call | flops 962592768 | bytes 17694720 | tf_op jit(solution)/shard_map/cond/branch_0_fun/step_and_transform/pallas_call | solution.py:216
  129.7 3.1 %collective-permute-start.8 = (f32[88,2,8,128]{3,2,1,0:T(8,128)S(1)}, f32[88,2,8,128]{3,2,1,0:T(8,128)S(1)}, u32[]{:S(2)}, u32[]{:S(2)}) collective-permute-start(f32[88,2,8,128]{3,2,1,0:T(8,128)S(1)} %add_select_fusion.3.rest_5_), channel_id=1, source_target_pairs={{0,4},{4,0},{8,12},{12,8},{1,5},{5,1},{9,13},{13,9},{2,6},{6,2},{1... | collective-permute-start | bytes 2162696 | tf_op jit(solution)/shard_map/cond/branch_0_fun/ppermute | solution.py:308
  133.5 12.2 %step_and_transform.29 = (f32[32,288,768]{2,1,0:T(8,128)}, f32[88,2,8,128]{3,2,1,0:T(8,128)S(1)}) custom-call(s32[9]{0:T(128)S(1)} %select_reduce_fusion.offset_ref, s32[32]{0:T(128)S(1)} %get-tuple-element.941.region_ref, f32[32,288,768]{2,1,0:T(8,128)} %get-tuple-element.645.q_ref, ...), custom_call_target="tpu_custom_call", output_to_operand_aliasing={{0}: (11, {})} | custom-call | flops 962592768 | bytes 17694720 | tf_op jit(solution)/shard_map/cond/branch_0_fun/step_and_transform/pallas_call | solution.py:216
  146.0 3.0 %collective-permute-start.10 = (f32[88,2,8,128]{3,2,1,0:T(8,128)S(1)}, f32[88,2,8,128]{3,2,1,0:T(8,128)S(1)}, u32[]{:S(2)}, u32[]{:S(2)}) collective-permute-start(f32[88,2,8,128]{3,2,1,0:T(8,128)S(1)} %add_select_fusion.2.rest_1_), channel_id=1, source_target_pairs={{0,4},{4,0},{8,12},{12,8},{1,5},{5,1},{9,13},{13,9},{2,6},{6,2},{1... | collective-permute-start | bytes 2162696 | tf_op jit(solution)/shard_map/cond/branch_0_fun/ppermute | solution.py:308
  149.0 0.9 collective-permute-start.9
  149.8 12.2 %step_and_transform.30 = (f32[32,288,768]{2,1,0:T(8,128)}, f32[88,2,8,128]{3,2,1,0:T(8,128)S(1)}) custom-call(s32[9]{0:T(128)S(1)} %select_reduce_fusion.offset_ref, s32[32]{0:T(128)S(1)} %get-tuple-element.941.region_ref, f32[32,288,768]{2,1,0:T(8,128)} %get-tuple-element.645.q_ref, ...), custom_call_target="tpu_custom_call", output_to_operand_aliasing={{0}: (11, {})} | custom-call | flops 962592768 | bytes 17694720 | tf_op jit(solution)/shard_map/cond/branch_0_fun/step_and_transform/pallas_call | solution.py:216
  162.3 2.1 collective-permute-start.12
  165.0 12.2 %step_and_transform.31 = (f32[32,288,768]{2,1,0:T(8,128)}, f32[88,2,8,128]{3,2,1,0:T(8,128)S(1)}) custom-call(s32[9]{0:T(128)S(1)} %select_reduce_fusion.offset_ref, s32[32]{0:T(128)S(1)} %get-tuple-element.941.region_ref, f32[32,288,768]{2,1,0:T(8,128)} %get-tuple-element.645.q_ref, ...), custom_call_target="tpu_custom_call", output_to_operand_aliasing={{0}: (11, {})} | custom-call | flops 962592768 | bytes 17694720 | tf_op jit(solution)/shard_map/cond/branch_0_fun/step_and_transform/pallas_call | solution.py:216
  177.5 0.8 collective-permute-start.13
  178.4 4.5 %collective-permute-start.14 = (f32[88,2,8,128]{3,2,1,0:T(8,128)S(1)}, f32[88,2,8,128]{3,2,1,0:T(8,128)S(1)}, u32[]{:S(2)}, u32[]{:S(2)}) collective-permute-start(f32[88,2,8,128]{3,2,1,0:T(8,128)S(1)} %add_select_fusion.rest_1_), channel_id=1, source_target_pairs={{0,4},{4,0},{8,12},{12,8},{1,5},{5,1},{9,13},{13,9},{2,6},{6,2},{1... | collective-permute-start | bytes 2162696 | tf_op jit(solution)/shard_map/cond/branch_0_fun/ppermute | solution.py:308
  182.9 14.4 %restore.12.moved_ref = f32[32,288,768]{2,1,0:T(8,128)} custom-call(s32[9]{0:T(128)S(1)} %select_reduce_fusion.offset_ref, s32[1]{0:T(128)} %bitcast.2.end_ref, f32[32,288,768]{2,1,0:T(8,128)} %get-tuple-element.716.moved_ref, f32[88,2,8,128]{3,2,1,0:T(8,128)S(1)} %collective-permute-done.4.rest_0_, ...), custom_call_target="tpu_custom_call", output_to_operand_aliasing={{}: (2, {})} | custom-call | flops 2887778304 | bytes 21233664 | tf_op jit(solution)/shard_map/cond/branch_0_fun/restore/pallas_call | solution.py:246
  197.5 0.9 collective-permute-start.15
  198.4 2.6 %collective-permute-start.16 = (f32[88,2,8,128]{3,2,1,0:T(8,128)S(1)}, f32[88,2,8,128]{3,2,1,0:T(8,128)S(1)}, u32[]{:S(2)}, u32[]{:S(2)}) collective-permute-start(f32[88,2,8,128]{3,2,1,0:T(8,128)S(1)} %add.212.rest_3_), channel_id=1, source_target_pairs={{0,4},{4,0},{8,12},{12,8},{1,5},{5,1},{9,13},{13,9},{2,6},{6,2},{1... | collective-permute-start | bytes 2162696 | tf_op jit(solution)/shard_map/cond/branch_0_fun/ppermute | solution.py:308
  201.0 10.5 %restore.13.moved_ref = f32[32,288,768]{2,1,0:T(8,128)} custom-call(s32[9]{0:T(128)S(1)} %select_reduce_fusion.offset_ref, s32[1]{0:T(128)} %bitcast.2.end_ref, f32[32,288,768]{2,1,0:T(8,128)} %restore.12.moved_ref, f32[88,2,8,128]{3,2,1,0:T(8,128)S(1)} %collective-permute-done.10.rest_0_, ...), custom_call_target="tpu_custom_call", output_to_operand_aliasing={{}: (2, {})} | custom-call | flops 1925185536 | bytes 14155776 | tf_op jit(solution)/shard_map/cond/branch_0_fun/restore/pallas_call | solution.py:246
  211.7 3.0 %collective-permute-done.16.rest_2_ = f32[88,2,8,128]{3,2,1,0:T(8,128)S(1)} collective-permute-done((f32[88,2,8,128]{3,2,1,0:T(8,128)S(1)}, f32[88,2,8,128]{3,2,1,0:T(8,128)S(1)}, u32[]{:S(2)}, u32[]{:S(2)}) %collective-permute-start.16) | collective-permute-done | bytes 720928 | tf_op jit(solution)/shard_map/cond/branch_0_fun/ppermute | solution.py:308
  214.7 10.5 %restore.14.moved_ref = f32[32,288,768]{2,1,0:T(8,128)} custom-call(s32[9]{0:T(128)S(1)} %select_reduce_fusion.offset_ref, s32[1]{0:T(128)} %bitcast.2.end_ref, f32[32,288,768]{2,1,0:T(8,128)} %restore.13.moved_ref, f32[88,2,8,128]{3,2,1,0:T(8,128)S(1)} %collective-permute-done.14.rest_0_, ...), custom_call_target="tpu_custom_call", output_to_operand_aliasing={{}: (2, {})} | custom-call | flops 1925185536 | bytes 14155776 | tf_op jit(solution)/shard_map/cond/branch_0_fun/restore/pallas_call | solution.py:246
  225.1 1.0 collective-permute-done.17.rest_0_
  226.1 6.1 %restore.15 = f32[32,288,768]{2,1,0:T(8,128)} custom-call(s32[9]{0:T(128)S(1)} %select_reduce_fusion.offset_ref, s32[1]{0:T(128)} %bitcast.2.end_ref, f32[32,288,768]{2,1,0:T(8,128)} %restore.14.moved_ref, f32[88,2,8,128]{3,2,1,0:T(8,128)S(1)} %collective-permute-done.17.rest_0_, ...), custom_call_target="tpu_custom_call", output_to_operand_aliasing={{}: (2, {})} | custom-call | flops 962592768 | bytes 7077888 | tf_op jit(solution)/shard_map/cond/branch_0_fun/restore/pallas_call | solution.py:246
  (85 shorter events, 7.5 us)
Async XLA Ops:
  0.0 32.4 %collective-permute-start.56 = (f32[2,144,768]{2,1,0:T(8,128)}, f32[2,144,768]{2,1,0:T(8,128)}, u32[]{:S(2)}, u32[]{:S(2)}) collective-permute-start(f32[2,144,768]{2,1,0:T(8,128)} %bitcast.64), channel_id=1, source_target_pairs={{0,2},{2,0},{1,3},{3,1},{4,6},{6,4},{5,7},{7,5},{8,10},{10,8},{9,1... | collective-permute-start | bytes 2654216 | tf_op jit(solution)/shard_map/ppermute | solution.py:383
  3.7 31.3 %collective-permute-start.55 = (f32[1,768]{1,0:T(1,128)S(1)}, f32[1,768]{1,0:T(1,128)S(1)}, u32[]{:S(2)}, u32[]{:S(2)}) collective-permute-start(f32[1,768]{1,0:T(1,128)S(1)} %slice_bitcast_fusion), channel_id=1, source_target_pairs={{4,2},{8,6},{12,10},{0,14},{5,3},{9,7},{13,11},{1,15},{20,18},{24,... | collective-permute-start | bytes 9224 | tf_op jit(solution)/shard_map/ppermute | solution.py:386
  10.7 10.7 %collective-permute-start.58 = (f32[32,2,768]{2,1,0:T(2,128)S(1)}, f32[32,2,768]{2,1,0:T(2,128)S(1)}, u32[]{:S(2)}, u32[]{:S(2)}) collective-permute-start(f32[32,2,768]{2,1,0:T(2,128)S(1)} %get-tuple-element.980), channel_id=1, source_target_pairs={{0,4},{4,8},{8,12},{12,0},{1,5},{5,9},{9,13},{13,1},{2,6},{6,10},{... | collective-permute-start | bytes 589832 | tf_op jit(solution)/shard_map/ppermute | solution.py:323
  10.8 10.7 %collective-permute-start.59 = (f32[32,2,768]{2,1,0:T(2,128)S(1)}, f32[32,2,768]{2,1,0:T(2,128)S(1)}, u32[]{:S(2)}, u32[]{:S(2)}) collective-permute-start(f32[32,2,768]{2,1,0:T(2,128)S(1)} %get-tuple-element.981), channel_id=1, source_target_pairs={{4,0},{8,4},{12,8},{0,12},{5,1},{9,5},{13,9},{1,13},{6,2},{10,6},{... | collective-permute-start | bytes 589832 | tf_op jit(solution)/shard_map/ppermute | solution.py:324
  14.6 17.7 %collective-permute-start.57 = (f32[144,768]{1,0:T(8,128)}, f32[144,768]{1,0:T(8,128)S(1)}, u32[]{:S(2)}, u32[]{:S(2)}) collective-permute-start(f32[144,768]{1,0:T(8,128)} %bitcast.66), channel_id=1, source_target_pairs={{0,2},{2,0},{1,3},{3,1},{4,6},{6,4},{5,7},{7,5},{8,10},{10,8},{9,1... | collective-permute-start | bytes 1327112 | tf_op jit(solution)/shard_map/ppermute | solution.py:383
  18.2 14.1 %copy-start.22 = (f32[1,144,768]{2,1,0:T(8,128)S(1)}, f32[1,144,768]{2,1,0:T(8,128)}, u32[]{:S(2)}) copy-start(f32[1,144,768]{2,1,0:T(8,128)} %param.14) | copy-start | bytes 1327108
  21.4 13.6 %collective-permute-start.54 = (f32[1,768]{1,0:T(1,128)S(1)}, f32[1,768]{1,0:T(1,128)S(1)}, u32[]{:S(2)}, u32[]{:S(2)}) collective-permute-start(f32[1,768]{1,0:T(1,128)S(1)} %slice_bitcast_fusion), channel_id=1, source_target_pairs={{4,0},{8,4},{12,8},{0,12},{5,1},{9,5},{13,9},{1,13},{6,2},{10,6},{... | collective-permute-start | bytes 9224 | tf_op jit(solution)/shard_map/ppermute | solution.py:385
  32.3 1.2 copy-start.21
  34.8 2.0 copy-start.6
  34.8 2.0 copy-start.23
  34.8 2.0 copy-start.24
  37.0 18.6 %copy-start.7 = (bf16[8,288,768]{2,1,0:T(8,128)(2,1)}, bf16[8,288,768]{2,1,0:T(8,128)(2,1)S(1)}, u32[]{:S(2)}) copy-start(bf16[8,288,768]{2,1,0:T(8,128)(2,1)S(1)} %get-tuple-element.944.source_ref) | copy-start | bytes 10616836 | tf_op jit(solution)/shard_map/cond
  40.2 15.5 %copy-start = (f32[9,288,768]{2,1,0:T(8,128)}, f32[9,288,768]{2,1,0:T(8,128)S(1)}, u32[]{:S(2)}) copy-start(f32[9,288,768]{2,1,0:T(8,128)S(1)} %stencil_weights.3.weight_ref) | copy-start | bytes 23887876 | tf_op jit(solution)/shard_map/cond
  53.8 17.3 %collective-permute-start = (f32[88,2,8,128]{3,2,1,0:T(8,128)S(1)}, f32[88,2,8,128]{3,2,1,0:T(8,128)S(1)}, u32[]{:S(2)}, u32[]{:S(2)}) collective-permute-start(f32[88,2,8,128]{3,2,1,0:T(8,128)S(1)} %get-tuple-element.677), channel_id=1, source_target_pairs={{0,4},{4,0},{8,12},{12,8},{1,5},{5,1},{9,13},{13,9},{2,6},{6,2},{1... | collective-permute-start | bytes 2162696 | tf_op jit(solution)/shard_map/cond/branch_0_fun/ppermute | solution.py:308
  72.2 19.8 %collective-permute-start.2 = (f32[88,2,8,128]{3,2,1,0:T(8,128)S(1)}, f32[88,2,8,128]{3,2,1,0:T(8,128)}, u32[]{:S(2)}, u32[]{:S(2)}) collective-permute-start(f32[88,2,8,128]{3,2,1,0:T(8,128)S(1)} %get-tuple-element.684), channel_id=1, source_target_pairs={{0,4},{4,0},{8,12},{12,8},{1,5},{5,1},{9,13},{13,9},{2,6},{6,2},{1... | collective-permute-start | bytes 2162696 | tf_op jit(solution)/shard_map/cond/branch_0_fun/ppermute | solution.py:308
  73.7 19.6 %collective-permute-start.1 = (f32[88,2,8,128]{3,2,1,0:T(8,128)}, f32[88,2,8,128]{3,2,1,0:T(8,128)}, u32[]{:S(2)}, u32[]{:S(2)}) collective-permute-start(f32[88,2,8,128]{3,2,1,0:T(8,128)} %add.199), channel_id=1, source_target_pairs={{4,8},{8,4},{5,9},{9,5},{6,10},{10,6},{7,11},{11,7},{20,24},{24,20... | collective-permute-start | bytes 2162696 | tf_op jit(solution)/shard_map/cond/branch_0_fun/ppermute | solution.py:309
  75.4 3.3 %copy-start.1 = (f32[9,288,768]{2,1,0:T(8,128)S(1)}, f32[9,288,768]{2,1,0:T(8,128)}, u32[]{:S(2)}) copy-start(f32[9,288,768]{2,1,0:T(8,128)} %copy-done) | copy-start | bytes 23887876 | tf_op jit(solution)/shard_map/cond
  91.9 7.2 %copy-start.8 = (bf16[8,288,768]{2,1,0:T(8,128)(2,1)S(1)}, bf16[8,288,768]{2,1,0:T(8,128)(2,1)}, u32[]{:S(2)}) copy-start(bf16[8,288,768]{2,1,0:T(8,128)(2,1)} %copy-done.7) | copy-start | bytes 10616836 | tf_op jit(solution)/shard_map/cond
  94.8 17.4 %collective-permute-start.4 = (f32[88,2,8,128]{3,2,1,0:T(8,128)S(1)}, f32[88,2,8,128]{3,2,1,0:T(8,128)S(1)}, u32[]{:S(2)}, u32[]{:S(2)}) collective-permute-start(f32[88,2,8,128]{3,2,1,0:T(8,128)S(1)} %add_select_fusion.5.rest_1_), channel_id=1, source_target_pairs={{0,4},{4,0},{8,12},{12,8},{1,5},{5,1},{9,13},{13,9},{2,6},{6,2},{1... | collective-permute-start | bytes 2162696 | tf_op jit(solution)/shard_map/cond/branch_0_fun/ppermute | solution.py:308
  98.5 13.9 %collective-permute-start.3 = (f32[88,2,8,128]{3,2,1,0:T(8,128)S(1)}, f32[88,2,8,128]{3,2,1,0:T(8,128)S(1)}, u32[]{:S(2)}, u32[]{:S(2)}) collective-permute-start(f32[88,2,8,128]{3,2,1,0:T(8,128)S(1)} %add.201), channel_id=1, source_target_pairs={{4,8},{8,4},{5,9},{9,5},{6,10},{10,6},{7,11},{11,7},{20,24},{24,20... | collective-permute-start | bytes 2162696 | tf_op jit(solution)/shard_map/cond/branch_0_fun/ppermute | solution.py:309
  112.5 17.0 %collective-permute-start.6 = (f32[88,2,8,128]{3,2,1,0:T(8,128)S(1)}, f32[88,2,8,128]{3,2,1,0:T(8,128)S(1)}, u32[]{:S(2)}, u32[]{:S(2)}) collective-permute-start(f32[88,2,8,128]{3,2,1,0:T(8,128)S(1)} %add_select_fusion.4.rest_3_), channel_id=1, source_target_pairs={{0,4},{4,0},{8,12},{12,8},{1,5},{5,1},{9,13},{13,9},{2,6},{6,2},{1... | collective-permute-start | bytes 2162696 | tf_op jit(solution)/shard_map/cond/branch_0_fun/ppermute | solution.py:308
  116.1 13.5 %collective-permute-start.5 = (f32[88,2,8,128]{3,2,1,0:T(8,128)S(1)}, f32[88,2,8,128]{3,2,1,0:T(8,128)S(1)}, u32[]{:S(2)}, u32[]{:S(2)}) collective-permute-start(f32[88,2,8,128]{3,2,1,0:T(8,128)S(1)} %add.203), channel_id=1, source_target_pairs={{4,8},{8,4},{5,9},{9,5},{6,10},{10,6},{7,11},{11,7},{20,24},{24,20... | collective-permute-start | bytes 2162696 | tf_op jit(solution)/shard_map/cond/branch_0_fun/ppermute | solution.py:309
  129.7 16.0 %collective-permute-start.8 = (f32[88,2,8,128]{3,2,1,0:T(8,128)S(1)}, f32[88,2,8,128]{3,2,1,0:T(8,128)S(1)}, u32[]{:S(2)}, u32[]{:S(2)}) collective-permute-start(f32[88,2,8,128]{3,2,1,0:T(8,128)S(1)} %add_select_fusion.3.rest_5_), channel_id=1, source_target_pairs={{0,4},{4,0},{8,12},{12,8},{1,5},{5,1},{9,13},{13,9},{2,6},{6,2},{1... | collective-permute-start | bytes 2162696 | tf_op jit(solution)/shard_map/cond/branch_0_fun/ppermute | solution.py:308
  132.8 13.0 %collective-permute-start.7 = (f32[88,2,8,128]{3,2,1,0:T(8,128)S(1)}, f32[88,2,8,128]{3,2,1,0:T(8,128)S(1)}, u32[]{:S(2)}, u32[]{:S(2)}) collective-permute-start(f32[88,2,8,128]{3,2,1,0:T(8,128)S(1)} %add.205), channel_id=1, source_target_pairs={{4,8},{8,4},{5,9},{9,5},{6,10},{10,6},{7,11},{11,7},{20,24},{24,20... | collective-permute-start | bytes 2162696 | tf_op jit(solution)/shard_map/cond/branch_0_fun/ppermute | solution.py:309
  146.0 16.1 %collective-permute-start.10 = (f32[88,2,8,128]{3,2,1,0:T(8,128)S(1)}, f32[88,2,8,128]{3,2,1,0:T(8,128)S(1)}, u32[]{:S(2)}, u32[]{:S(2)}) collective-permute-start(f32[88,2,8,128]{3,2,1,0:T(8,128)S(1)} %add_select_fusion.2.rest_1_), channel_id=1, source_target_pairs={{0,4},{4,0},{8,12},{12,8},{1,5},{5,1},{9,13},{13,9},{2,6},{6,2},{1... | collective-permute-start | bytes 2162696 | tf_op jit(solution)/shard_map/cond/branch_0_fun/ppermute | solution.py:308
  149.0 13.2 %collective-permute-start.9 = (f32[88,2,8,128]{3,2,1,0:T(8,128)S(1)}, f32[88,2,8,128]{3,2,1,0:T(8,128)S(1)}, u32[]{:S(2)}, u32[]{:S(2)}) collective-permute-start(f32[88,2,8,128]{3,2,1,0:T(8,128)S(1)} %add.207), channel_id=1, source_target_pairs={{4,8},{8,4},{5,9},{9,5},{6,10},{10,6},{7,11},{11,7},{20,24},{24,20... | collective-permute-start | bytes 2162696 | tf_op jit(solution)/shard_map/cond/branch_0_fun/ppermute | solution.py:309
  162.3 15.0 %collective-permute-start.12 = (f32[88,2,8,128]{3,2,1,0:T(8,128)S(1)}, f32[88,2,8,128]{3,2,1,0:T(8,128)S(1)}, u32[]{:S(2)}, u32[]{:S(2)}) collective-permute-start(f32[88,2,8,128]{3,2,1,0:T(8,128)S(1)} %add_select_fusion.1.rest_3_), channel_id=1, source_target_pairs={{0,4},{4,0},{8,12},{12,8},{1,5},{5,1},{9,13},{13,9},{2,6},{6,2},{1... | collective-permute-start | bytes 2162696 | tf_op jit(solution)/shard_map/cond/branch_0_fun/ppermute | solution.py:308
  164.3 13.0 %collective-permute-start.11 = (f32[88,2,8,128]{3,2,1,0:T(8,128)S(1)}, f32[88,2,8,128]{3,2,1,0:T(8,128)S(1)}, u32[]{:S(2)}, u32[]{:S(2)}) collective-permute-start(f32[88,2,8,128]{3,2,1,0:T(8,128)S(1)} %add.209), channel_id=1, source_target_pairs={{4,8},{8,4},{5,9},{9,5},{6,10},{10,6},{7,11},{11,7},{20,24},{24,20... | collective-permute-start | bytes 2162696 | tf_op jit(solution)/shard_map/cond/branch_0_fun/ppermute | solution.py:309
  177.4 5.5 %copy-start.15 = (bf16[576,576]{1,0:T(8,128)(2,1)S(1)}, bf16[576,576]{1,0:T(8,128)(2,1)}, u32[]{:S(2)}) copy-start(bf16[576,576]{1,0:T(8,128)(2,1)} %get-tuple-element.718.rest_8_.rest_6_.rest_4_) | copy-start | bytes 1990660 | tf_op jit(solution)/shard_map/cond
  177.4 5.5 %copy-start.18 = (bf16[256,768]{1,0:T(8,128)(2,1)S(1)}, bf16[256,768]{1,0:T(8,128)(2,1)}, u32[]{:S(2)}) copy-start(bf16[256,768]{1,0:T(8,128)(2,1)} %get-tuple-element.720.rest_10_.rest_8_.rest_6_) | copy-start | bytes 1179652 | tf_op jit(solution)/shard_map/cond
  177.5 19.7 %collective-permute-start.13 = (f32[88,2,8,128]{3,2,1,0:T(8,128)S(1)}, f32[88,2,8,128]{3,2,1,0:T(8,128)S(1)}, u32[]{:S(2)}, u32[]{:S(2)}) collective-permute-start(f32[88,2,8,128]{3,2,1,0:T(8,128)S(1)} %add.211), channel_id=1, source_target_pairs={{4,8},{8,4},{5,9},{9,5},{6,10},{10,6},{7,11},{11,7},{20,24},{24,20... | collective-permute-start | bytes 2162696 | tf_op jit(solution)/shard_map/cond/branch_0_fun/ppermute | solution.py:309
  178.4 19.0 %collective-permute-start.14 = (f32[88,2,8,128]{3,2,1,0:T(8,128)S(1)}, f32[88,2,8,128]{3,2,1,0:T(8,128)S(1)}, u32[]{:S(2)}, u32[]{:S(2)}) collective-permute-start(f32[88,2,8,128]{3,2,1,0:T(8,128)S(1)} %add_select_fusion.rest_1_), channel_id=1, source_target_pairs={{0,4},{4,0},{8,12},{12,8},{1,5},{5,1},{9,13},{13,9},{2,6},{6,2},{1... | collective-permute-start | bytes 2162696 | tf_op jit(solution)/shard_map/cond/branch_0_fun/ppermute | solution.py:308
  197.5 14.0 %collective-permute-start.15 = (f32[88,2,8,128]{3,2,1,0:T(8,128)S(1)}, f32[88,2,8,128]{3,2,1,0:T(8,128)S(1)}, u32[]{:S(2)}, u32[]{:S(2)}) collective-permute-start(f32[88,2,8,128]{3,2,1,0:T(8,128)S(1)} %add.213), channel_id=1, source_target_pairs={{4,8},{8,4},{5,9},{9,5},{6,10},{10,6},{7,11},{11,7},{20,24},{24,20... | collective-permute-start | bytes 2162696 | tf_op jit(solution)/shard_map/cond/branch_0_fun/ppermute | solution.py:309
  198.4 16.3 %collective-permute-start.16 = (f32[88,2,8,128]{3,2,1,0:T(8,128)S(1)}, f32[88,2,8,128]{3,2,1,0:T(8,128)S(1)}, u32[]{:S(2)}, u32[]{:S(2)}) collective-permute-start(f32[88,2,8,128]{3,2,1,0:T(8,128)S(1)} %add.212.rest_3_), channel_id=1, source_target_pairs={{0,4},{4,0},{8,12},{12,8},{1,5},{5,1},{9,13},{13,9},{2,6},{6,2},{1... | collective-permute-start | bytes 2162696 | tf_op jit(solution)/shard_map/cond/branch_0_fun/ppermute | solution.py:308
  211.6 14.5 %collective-permute-start.17 = (f32[88,2,8,128]{3,2,1,0:T(8,128)S(1)}, f32[88,2,8,128]{3,2,1,0:T(8,128)S(1)}, u32[]{:S(2)}, u32[]{:S(2)}) collective-permute-start(f32[88,2,8,128]{3,2,1,0:T(8,128)S(1)} %add.214.rest_1_), channel_id=1, source_target_pairs={{0,4},{4,0},{8,12},{12,8},{1,5},{5,1},{9,13},{13,9},{2,6},{6,2},{1... | collective-permute-start | bytes 2162696 | tf_op jit(solution)/shard_map/cond/branch_0_fun/ppermute | solution.py:308
